TPU v7x, 512 devices: a whole 4x4x16 slice. The times are simulated.
512 devices in a mesh: outer: 16 (over y, z_lo), inner: 32 (over z_hi, x, core).
Axes of the slice: x: 4, y: 4, z: 16 (z_hi: 4, z_lo: 4; z = z_hi * 4 + z_lo), core: 2. Of those that a mesh axis runs over, the one named last changes fastest.
Arguments:
- queries: bfloat16 [4096, 2048], P('inner', 'outer'), may hold values from -7.5 to 7.5
- keys: bfloat16 [4096, 2048], P('inner', 'outer'), may hold values from -4 to 4
- values: bfloat16 [4096, 2048], P('inner', 'outer'), may hold values from -6 to 6
- w_out: bfloat16 [2048, 4096], P('outer'), may hold values from -0.5 to 0.5
- grad_out: bfloat16 [4096, 4096], P('inner', 'outer'), may hold values from -1.5 to 1.5
Outputs:
- output: bfloat16 [4096, 4096], P('inner', 'outer')
- grad_queries: bfloat16 [4096, 2048], P('inner', 'outer')
- grad_keys: bfloat16 [4096, 2048], P('inner', 'outer')
- grad_values: bfloat16 [4096, 2048], P('inner', 'outer')
- grad_w_out: float32 [2048, 4096], P('outer', 'inner')
All inputs are finite; a program needn't handle non-finite values.
Results may differ from a plain program's by a relative error of at most 0.04.
Values may be sent and summed in bfloat16 or wider, within the bound.
No kernel may reach another device: no remote copies, remote signals or barrier semaphores. Data moves between devices by JAX's collectives and lax.ppermute only.
A program may use at most 64 MiB of HBM per device.

v0:
```python
import math

import jax
import jax.numpy as jnp
from jax import lax
from jax.sharding import PartitionSpec as P

HDIM = 128


def block_size(amount):
    return math.gcd(amount, 1024)


def to_heads(array, head_count):
    row_count = array.shape[0]
    return array.reshape(row_count, head_count, HDIM).transpose(1, 0, 2)


def forward_fold(query_heads, score_scale):
    head_count = query_heads.shape[0]

    def attend(running_state, pieces, anchor):
        key_piece, value_piece = pieces
        piece_rows = key_piece.shape[0]
        block_rows = block_size(piece_rows)

        def attend_advance(block_index, state_in):
            running, totals, accumulated = state_in
            key_block = lax.dynamic_slice_in_dim(
                key_piece, block_index * block_rows, block_rows, 0
            ).reshape(block_rows, head_count, HDIM)
            value_block = lax.dynamic_slice_in_dim(
                value_piece, block_index * block_rows, block_rows, 0
            ).reshape(block_rows, head_count, HDIM)
            scores = (
                jnp.einsum(
                    "hrd,phd->hrp", query_heads, key_block, preferred_element_type=jnp.float32
                )
                * score_scale
            )
            newest = jnp.maximum(running, jnp.max(scores, axis=2))
            shrink = jnp.exp(running - newest)
            weights = jnp.exp(scores - newest[:, :, None])
            totals = totals * shrink + jnp.sum(weights, axis=2)
            accumulated = accumulated * shrink[:, :, None] + jnp.einsum(
                "hrp,phd->hrd",
                weights.astype(jnp.bfloat16),
                value_block,
                preferred_element_type=jnp.float32,
            )
            return (newest, totals, accumulated)

        return lax.fori_loop(0, piece_rows // block_rows, attend_advance, running_state)

    return attend


def query_grad_fold(query_heads, grad_heads, log_totals, row_dots, score_scale):
    head_count = query_heads.shape[0]

    def query_collect(accumulated, pieces, anchor):
        key_piece, value_piece = pieces
        piece_rows = key_piece.shape[0]
        block_rows = block_size(piece_rows)

        def query_advance(block_index, state_in):
            key_block = lax.dynamic_slice_in_dim(
                key_piece, block_index * block_rows, block_rows, 0
            ).reshape(block_rows, head_count, HDIM)
            value_block = lax.dynamic_slice_in_dim(
                value_piece, block_index * block_rows, block_rows, 0
            ).reshape(block_rows, head_count, HDIM)
            scores = (
                jnp.einsum(
                    "hrd,phd->hrp", query_heads, key_block, preferred_element_type=jnp.float32
                )
                * score_scale
            )
            probs = jnp.exp(scores - log_totals[:, :, None])
            dprobs = jnp.einsum(
                "hrd,phd->hrp", grad_heads, value_block, preferred_element_type=jnp.float32
            )
            dscores = probs * (dprobs - row_dots[:, :, None])
            return state_in + jnp.einsum(
                "hrp,phd->hrd",
                dscores.astype(jnp.bfloat16),
                key_block,
                preferred_element_type=jnp.float32,
            )

        return lax.fori_loop(0, piece_rows // block_rows, query_advance, accumulated)

    return query_collect


def key_grad_fold(key_local, value_local, stats_whole, score_scale):
    head_count = key_local.shape[1]
    log_whole, dots_whole = stats_whole

    def key_collect(running_state, pieces, anchor):
        query_piece, grad_piece = pieces
        piece_rows = query_piece.shape[0]
        block_rows = block_size(piece_rows)

        def key_advance(block_index, state_in):
            key_grad, value_grad = state_in
            offset = block_index * block_rows
            query_block = lax.dynamic_slice_in_dim(query_piece, offset, block_rows, 0).reshape(
                block_rows, head_count, HDIM
            )
            grad_block = lax.dynamic_slice_in_dim(grad_piece, offset, block_rows, 0).reshape(
                block_rows, head_count, HDIM
            )
            log_block = lax.dynamic_slice_in_dim(log_whole, offset, block_rows, 0).T
            dots_block = lax.dynamic_slice_in_dim(dots_whole, offset, block_rows, 0).T
            scores = (
                jnp.einsum(
                    "phd,khd->hpk", query_block, key_local, preferred_element_type=jnp.float32
                )
                * score_scale
            )
            probs = jnp.exp(scores - log_block[:, :, None])
            dprobs = jnp.einsum(
                "phd,khd->hpk", grad_block, value_local, preferred_element_type=jnp.float32
            )
            dscores = probs * (dprobs - dots_block[:, :, None])
            key_grad = key_grad + jnp.einsum(
                "hpk,phd->khd",
                dscores.astype(jnp.bfloat16),
                query_block,
                preferred_element_type=jnp.float32,
            )
            value_grad = value_grad + jnp.einsum(
                "hpk,phd->khd",
                probs.astype(jnp.bfloat16),
                grad_block,
                preferred_element_type=jnp.float32,
            )
            return (key_grad, value_grad)

        return lax.fori_loop(0, piece_rows // block_rows, key_advance, running_state)

    return key_collect


def body(queries, keys, values, w_out, grad_out):
    score_scale = HDIM ** (-0.5)
    row_count = queries.shape[0]
    head_count = queries.shape[1] // HDIM
    query_heads = to_heads(queries, head_count)
    attend = forward_fold(query_heads, score_scale)
    start_state = (
        jnp.full((head_count, row_count), -jnp.inf, jnp.float32),
        jnp.zeros((head_count, row_count), jnp.float32),
        jnp.zeros((head_count, row_count, HDIM), jnp.float32),
    )
    running, totals, accumulated = attend(
        start_state,
        (
            lax.all_gather(keys, "inner", axis=0, tiled=True),
            lax.all_gather(values, "inner", axis=0, tiled=True),
        ),
        jnp.int32(0),
    )
    attn_heads = (accumulated / totals[:, :, None]).astype(jnp.bfloat16)
    attn_local = attn_heads.transpose(1, 0, 2).reshape(row_count, head_count * HDIM)
    log_totals = running + jnp.log(totals)
    partial_out = jnp.dot(attn_local, w_out, preferred_element_type=jnp.float32)
    output = lax.psum_scatter(
        partial_out.astype(jnp.bfloat16), "outer", scatter_dimension=1, tiled=True
    )
    cotangent = lax.all_gather(grad_out, "outer", axis=1, tiled=True)
    grad_attn = lax.dot_general(
        cotangent, w_out, (((1,), (1,)), ((), ())), preferred_element_type=jnp.float32
    ).astype(jnp.bfloat16)
    weight_term = lax.dot_general(
        attn_local, cotangent, (((0,), (0,)), ((), ())), preferred_element_type=jnp.float32
    )
    grad_w_out = lax.psum_scatter(
        weight_term.astype(jnp.bfloat16), "inner", scatter_dimension=1, tiled=True
    ).astype(jnp.float32)
    grad_heads = to_heads(grad_attn, head_count)
    row_dots = jnp.sum(grad_heads.astype(jnp.float32) * attn_heads.astype(jnp.float32), axis=2)
    collect_query = query_grad_fold(query_heads, grad_heads, log_totals, row_dots, score_scale)
    empty_query = jnp.zeros((head_count, row_count, HDIM), jnp.float32)
    query_acc = collect_query(
        empty_query,
        (
            lax.all_gather(keys, "inner", axis=0, tiled=True),
            lax.all_gather(values, "inner", axis=0, tiled=True),
        ),
        jnp.int32(0),
    )
    grad_queries = (
        (query_acc * score_scale)
        .astype(jnp.bfloat16)
        .transpose(1, 0, 2)
        .reshape(row_count, head_count * HDIM)
    )
    stats_whole = (
        lax.all_gather(log_totals.T, "inner", axis=0, tiled=True),
        lax.all_gather(row_dots.T, "inner", axis=0, tiled=True),
    )
    key_split = keys.reshape(row_count, head_count, HDIM)
    value_split = values.reshape(row_count, head_count, HDIM)
    collect_keys = key_grad_fold(key_split, value_split, stats_whole, score_scale)
    empty_keys = jnp.zeros((row_count, head_count, HDIM), jnp.float32)
    key_acc, value_acc = collect_keys(
        (empty_keys, empty_keys),
        (
            lax.all_gather(queries, "inner", axis=0, tiled=True),
            lax.all_gather(grad_attn, "inner", axis=0, tiled=True),
        ),
        jnp.int32(0),
    )
    grad_keys = (key_acc * score_scale).astype(jnp.bfloat16).reshape(row_count, head_count * HDIM)
    grad_values = value_acc.astype(jnp.bfloat16).reshape(row_count, head_count * HDIM)
    return (output, grad_queries, grad_keys, grad_values, grad_w_out)


def solution(mesh):
    return jax.shard_map(
        body,
        mesh=mesh,
        in_specs=(
            P("inner", "outer"),
            P("inner", "outer"),
            P("inner", "outer"),
            P("outer", None),
            P("inner", "outer"),
        ),
        out_specs=(
            P("inner", "outer"),
            P("inner", "outer"),
            P("inner", "outer"),
            P("inner", "outer"),
            P("outer", "inner"),
        ),
        check_vma=False,
    )
```

profile of v0, /device:TPU:4, one launch (start us, length us, event | category | flops | bytes accessed | tf_op | source)
XLA Modules:
  0.0 582.6 jit_solution(9947396430785812761)
XLA Ops:
  7.2 0.7 all-gather.11.cloned.1.call-update
  8.0 0.7 all-gather.9.cloned.1.call-update
  8.7 0.7 all-gather.13.cloned.1.call-update
  9.4 0.0 reduce-scatter.7.cloned.1.call-start
  9.5 76.3 %all-gather.11.cloned.1.call-done = bf16[4096,128]{1,0:T(8,128)(2,1)} async-done(((bf16[128,128]{1,0:T(8,128)(2,1)}), bf16[4096,128]{1,0:T(8,128)(2,1)}) %all-gather.11.cloned.1.call-update) | async-done | bytes 1048592 | tf_op jit(solution)/shard_map/all_gather | solution.py:162
  85.8 68.6 %all-gather.9.cloned.1.call-done = bf16[4096,128]{1,0:T(8,128)(2,1)} async-done(((bf16[128,128]{1,0:T(8,128)(2,1)}), bf16[4096,128]{1,0:T(8,128)(2,1)}) %all-gather.9.cloned.1.call-update) | async-done | bytes 1048592 | tf_op jit(solution)/shard_map/all_gather | solution.py:161
  154.4 10.9 %while.48 = (s32[]{:T(128)}, f32[1,128]{1,0:T(1,128)S(1)}, f32[1,128]{1,0:T(1,128)S(1)}, f32[1,128,128]{2,1,0:T(8,128)S(1)}, bf16[4096,128]{1,0:T(8,128)(2,1)}, ...) while((s32[]{:T(128)}, f32[1,128]{1,0:T(1,128)S(1)}, ...), condition=%wide.region_3.0_spmd.clone, body=%wide.region_0.0_spmd.clone.sunk | while | flops 67945224 | bytes 2269359 | solution.py:54
  154.4 1.3 fusion.88
  155.7 1.2 fusion.92
  156.9 0.2 fusion.90
  157.1 1.3 fusion.88
  158.4 1.2 fusion.92
  159.6 0.2 fusion.90
  159.8 1.3 fusion.88
  161.1 1.2 fusion.92
  162.3 0.2 fusion.90
  162.5 1.3 fusion.88
  163.8 1.2 fusion.92
  165.1 0.2 fusion.90
  165.3 0.1 copy.20
  165.3 62.8 %all-gather.13.cloned.1.call-done = bf16[128,4096]{1,0:T(8,128)(2,1)} async-done(((bf16[128,256]{1,0:T(8,128)(2,1)}), bf16[128,4096]{1,0:T(8,128)(2,1)}) %all-gather.13.cloned.1.call-update) | async-done | bytes 1048592 | tf_op jit(solution)/shard_map/all_gather | solution.py:173
  228.2 1.8 multiply_reduce_fusion
  229.9 0.4 convolution_convert_fusion
  230.4 1.3 copy.25
  231.7 0.0 all-gather.15.cloned.1.call-start
  231.8 0.5 all-gather.15.cloned.1.call-update
  232.3 0.0 all-gather.17.cloned.1.call-start
  232.4 0.1 copy.21
  232.5 45.0 %all-gather.2 = f32[32,1,128]{2,1,0:T(1,128)S(1)} all-gather(f32[1,1,128]{2,1,0:T(1,128)S(1)} %bitcast.125), channel_id=3, replica_groups=mesh['outer'=16,'inner'=32] {'inner'}, dimensions={0}, use_global_device_ids=true | all-gather | bytes 16896 | tf_op jit(solution)/shard_map/all_gather | solution.py:203
  277.5 0.0 reduce-scatter.5.cloned.1.call-start
  277.6 47.2 %all-gather = f32[1,4096]{1,0:T(1,128)S(1)} all-gather(f32[1,128]{1,0:T(1,128)S(1)} %log_add_fusion), channel_id=2, replica_groups=mesh['outer'=16,'inner'=32] {'inner'}, dimensions={1}, use_global_device_ids=true | all-gather | bytes 16896 | tf_op jit(solution)/shard_map/all_gather | solution.py:202
  324.8 6.8 %while.49 = (s32[]{:T(128)}, f32[1,128,128]{2,1,0:T(8,128)S(1)}, bf16[4096,128]{1,0:T(8,128)(2,1)S(1)}, bf16[1,128,128]{2,1,0:T(8,128)(2,1)S(1)}, f32[1,128]{1,0...) while((s32[]{:T(128)}, f32[1,128,128]{2,1,0:T(8,128)S(1)}, ...), condition=%wide.region_7.0_spmd.clone, body=%wide.region_6.0_spmd.clone.sunk | while | flops 101351424 | bytes 2034352 | solution.py:92
  324.8 1.2 convolution_subtract_fusion.3
  326.0 0.5 fusion.98
  326.5 1.2 convolution_subtract_fusion.3
  327.7 0.5 fusion.98
  328.2 1.2 convolution_subtract_fusion.3
  329.4 0.5 fusion.98
  329.9 1.2 convolution_subtract_fusion.3
  331.1 0.5 fusion.98
  331.6 0.6 fusion.54
  332.2 1.4 convolution_convert_fusion.1
  333.7 9.1 %reduce-scatter.7.cloned.1.call-done = bf16[128,128]{1,0:T(8,128)(2,1)} async-done(((bf16[4096,128]{1,0:T(8,128)(2,1)}), bf16[128,128]{1,0:T(8,128)(2,1)}) %reduce-scatter.7.cloned.1.call-update) | async-done | bytes 32784
  342.8 0.9 copy.26
  343.7 0.6 convert_element_type.71
  344.3 67.9 %all-gather.15.cloned.1.call-done = bf16[4096,128]{1,0:T(8,128)(2,1)} async-done(((bf16[128,128]{1,0:T(8,128)(2,1)}), bf16[4096,128]{1,0:T(8,128)(2,1)}) %all-gather.15.cloned.1.call-update) | async-done | bytes 1048592 | tf_op jit(solution)/shard_map/all_gather | solution.py:212
  412.3 70.7 %all-gather.17.cloned.1.call-done = bf16[4096,128]{0,1:T(8,128)(2,1)} async-done(((bf16[128,128]{0,1:T(8,128)(2,1)}), bf16[4096,128]{0,1:T(8,128)(2,1)}) %all-gather.17.cloned.1.call-update) | async-done | bytes 1048592 | tf_op jit(solution)/shard_map/all_gather | solution.py:213
  483.0 16.0 %while.50 = (s32[]{:T(128)}, f32[128,1,128]{0,2,1:T(8,128)S(1)}, f32[128,1,128]{0,2,1:T(8,128)S(1)}, bf16[4096,128]{1,0:T(8,128)(2,1)}, bf16[128,1,128]{2,0,1:T(...) while((s32[]{:T(128)}, f32[128,1,128]{0,2,1:T(8,128)S(1)}, ...), condition=%wide.region_9.0_spmd.clone, body=%wide.region_8.0_spmd.clone.sunk | while | flops 135069696 | bytes 2975425 | solution.py:142
  483.0 1.2 fusion.106
  484.2 1.2 fusion.108
  485.4 1.5 fusion.107
  487.0 1.2 fusion.106
  488.2 1.2 fusion.108
  489.4 1.5 fusion.107
  491.0 1.2 fusion.106
  492.2 1.2 fusion.108
  493.4 1.5 fusion.107
  495.0 1.2 fusion.106
  496.2 1.2 fusion.108
  497.4 1.5 fusion.107
  498.9 0.1 copy.23
  499.0 0.7 copy.24
  499.8 0.6 fusion.55
  500.4 75.4 %reduce-scatter.5.cloned.1.call-done = bf16[128,256]{1,0:T(8,128)(2,1)} async-done(((bf16[128,4096]{1,0:T(8,128)(2,1)}), bf16[128,256]{1,0:T(8,128)(2,1)}) %reduce-scatter.5.cloned.1.call-update) | async-done | bytes 65552 | tf_op jit(solution)/shard_map/reduce_scatter | solution.py:170
  (43 shorter events, 0.4 us)
Async XLA Ops:
  7.2 221.0 %copy-start = (bf16[128,4096]{1,0:T(8,128)(2,1)S(1)}, bf16[128,4096]{1,0:T(8,128)(2,1)}, u32[]{:S(2)}) copy-start(bf16[128,4096]{1,0:T(8,128)(2,1)} %param.14) | copy-start | bytes 3145732
  7.2 78.6 %all-gather.11.cloned.1.call-start = ((), (), s32[]{:S(2)}) async-start(), calls=%async_computation.3 | async-start | bytes 1081344 | tf_op jit(solution)/shard_map/all_gather | solution.py:162
  7.9 146.5 %all-gather.9.cloned.1.call-start = ((), (), s32[]{:S(2)}) async-start(), calls=%async_computation.2 | async-start | bytes 1081344 | tf_op jit(solution)/shard_map/all_gather | solution.py:161
  8.7 219.5 %all-gather.13.cloned.1.call-start = ((), (), s32[]{:S(2)}) async-start(), calls=%async_computation.5 | async-start | bytes 1114112 | tf_op jit(solution)/shard_map/all_gather | solution.py:173
  9.4 333.4 %reduce-scatter.7.cloned.1.call-start = ((), (), s32[]{:S(2)}) async-start(), calls=%async_computation.8 | async-start | bytes 1081344
  228.2 1.8 copy-start.2
  229.9 2.5 copy-start.6
  231.7 93.1 %copy-start.1 = (bf16[4096,128]{1,0:T(8,128)(2,1)S(1)}, bf16[4096,128]{1,0:T(8,128)(2,1)}, u32[]{:S(2)}) copy-start(bf16[4096,128]{1,0:T(8,128)(2,1)} %get-tuple-element.895) | copy-start | bytes 3145732
  231.7 93.1 %copy-start.3 = (bf16[1,128,128]{2,1,0:T(8,128)(2,1)S(1)}, bf16[1,128,128]{2,1,0:T(8,128)(2,1)}, u32[]{:S(2)}) copy-start(bf16[1,128,128]{2,1,0:T(8,128)(2,1)} %get-tuple-element.905) | copy-start | bytes 98308
  231.7 180.5 %all-gather.15.cloned.1.call-start = ((), (), s32[]{:S(2)}) async-start(), calls=%async_computation.6 | async-start | bytes 1081344 | tf_op jit(solution)/shard_map/all_gather | solution.py:212
  232.3 250.7 %all-gather.17.cloned.1.call-start = ((), (), s32[]{:S(2)}) async-start(), calls=%async_computation.7 | async-start | bytes 1081344 | tf_op jit(solution)/shard_map/all_gather | solution.py:213
  277.5 298.2 %reduce-scatter.5.cloned.1.call-start = ((), (), s32[]{:S(2)}) async-start(), calls=%async_computation.4 | async-start | bytes 1114112 | tf_op jit(solution)/shard_map/reduce_scatter | solution.py:170
  333.7 149.3 %copy-start.4 = (bf16[128,128]{1,0:T(8,128)(2,1)S(1)}, bf16[128,128]{1,0:T(8,128)(2,1)}, u32[]{:S(2)}) copy-start(bf16[128,128]{1,0:T(8,128)(2,1)} %param.13) | copy-start | bytes 98308
  333.7 149.3 %copy-start.5 = (bf16[128,128]{1,0:T(8,128)(2,1)S(1)}, bf16[128,128]{1,0:T(8,128)(2,1)}, u32[]{:S(2)}) copy-start(bf16[128,128]{1,0:T(8,128)(2,1)} %param.12) | copy-start | bytes 98308
Sparse Core Ops, SparseCore 0:
  11.1 74.5 all-gather.10
  88.9 65.4 all-gather.8
  156.4 71.7 all-gather.12
  232.4 110.3 reduce-scatter.6
  346.3 65.9 all-gather.14
  416.2 66.7 all-gather.16
  486.6 89.1 reduce-scatter.4
where the time goes:
time: 583 us
  waiting for transfers between devices  433 us (74%)
  blocking collectives  92.2 us (16%)
  matrix products  36.1 us (6%)
  between operations  14.3 us (2%)
    all_gather x1, waiting for transfers between devices, body(): lax.all_gather(values, 'inner', axis=0, tiled=True)  76.3 us
    reduce_scatter x1, waiting for transfers between devices, body(): lax.psum_scatter(partial_out.astype(jnp.bfloat16), 'outer', scatter_dimen...  75.4 us
    all_gather x1, waiting for transfers between devices, body(): lax.all_gather(grad_attn, 'inner', axis=0, tiled=True)  70.7 us
    all_gather x1, waiting for transfers between devices, body(): lax.all_gather(keys, 'inner', axis=0, tiled=True)  68.6 us
    all_gather x1, waiting for transfers between devices, body(): lax.all_gather(queries, 'inner', axis=0, tiled=True)  67.9 us
    all_gather x1, waiting for transfers between devices, body(): cotangent = lax.all_gather(grad_out, 'outer', axis=1, tiled=True)  62.8 us
    all_gather x1, blocking collectives, body(): lax.all_gather(log_totals.T, 'inner', axis=0, tiled=True)  47.2 us
    all_gather x1, blocking collectives, body(): lax.all_gather(row_dots.T, 'inner', axis=0, tiled=True)  45 us
  transfers between devices with their start and end apart: 7, of which 7 were waited for; matrix products, arithmetic and copies ran while one was open for 7% of the time, Pallas kernels for 0%

commit v1 on v0

v1 whole, which is shorter than its diff:
```python
import functools

import jax
import jax.numpy as jnp
from jax import lax
from jax.experimental import pallas as pl
from jax.experimental.pallas import tpu as pltpu
from jax.sharding import Mesh, PartitionSpec as P

HDIM = 128
BLK = 128
SCALE = HDIM ** (-0.5)
F32 = jnp.float32
BF16 = jnp.bfloat16


def dot(a, b, dims=((1,), (0,))):
    return lax.dot_general(a, b, (dims, ((), ())), preferred_element_type=F32)


def forward_kernel(q_ref, *refs):
    pieces, (w_ref, attn_ref, lse_ref, out_ref, s_ref) = refs[:8], refs[8:]
    q = q_ref[...]
    width = 4 * BLK
    top = jnp.full((BLK, BLK), -jnp.inf, F32)
    for j, piece in enumerate(pieces):
        k = piece[:, 0].reshape(width, HDIM)
        s = dot(q, k, ((1,), (1,))) * SCALE
        s_ref[:, j * width : (j + 1) * width] = s
        for t in range(4):
            top = jnp.maximum(top, s[:, t * BLK : (t + 1) * BLK])
    row_max = jnp.max(top, axis=1, keepdims=True)
    sums = jnp.zeros((BLK, BLK), F32)
    acc = jnp.zeros((BLK, HDIM), F32)
    for j, piece in enumerate(pieces):
        p = jnp.exp(s_ref[:, j * width : (j + 1) * width] - row_max)
        for t in range(4):
            sums = sums + p[:, t * BLK : (t + 1) * BLK]
        v = piece[:, 1].reshape(width, HDIM)
        acc = acc + dot(p.astype(BF16), v)
    totals = jnp.sum(sums, axis=1, keepdims=True)
    attn = (acc / totals).astype(BF16)
    attn_ref[...] = attn
    lse_ref[...] = jnp.broadcast_to(row_max + jnp.log(totals), (BLK, BLK))
    for o in range(16):
        out_ref[o] = dot(attn, w_ref[:, o * 256 : (o + 1) * 256]).astype(BF16)


def backward_kernel(core_ref, q_ref, *refs):
    pieces = refs[:8]
    w_ref, cot_ref, attn_ref, lse_ref, dq_ref, own_ref, oth_ref = refs[8:]
    core = core_ref[0]
    x_pos = core_ref[1]
    width = 4 * BLK
    q = q_ref[...]
    attn = attn_ref[...]
    grad = jnp.zeros((BLK, HDIM), F32)
    for o in range(16):
        grad = grad + dot(cot_ref[o], w_ref[:, o * 256 : (o + 1) * 256], ((1,), (1,)))
    dattn = grad.astype(BF16)
    dots = jnp.sum(dattn.astype(F32) * attn.astype(F32), axis=1, keepdims=True)
    lse = lse_ref[...][:, :1]
    q_t = q.T
    dattn_t = dattn.T
    attn_t = attn.T
    dq = jnp.zeros((BLK, HDIM), F32)
    for j, piece in enumerate(pieces):
        k = piece[:, 0].reshape(width, HDIM)
        v = piece[:, 1].reshape(width, HDIM)
        s = dot(q, k, ((1,), (1,))) * SCALE
        p = jnp.exp(s - lse)
        dp = dot(dattn, v, ((1,), (1,)))
        ds = (p * (dp - dots)).astype(BF16)
        dq = dq + dot(ds, k)
        dk_t = dot(q_t, ds).astype(BF16)
        dv_t = dot(dattn_t, p.astype(BF16)).astype(BF16)
        ref = own_ref if j < 4 else oth_ref
        for z in range(4):
            ref[j % 4, z, 0] = dk_t[:, z * BLK : (z + 1) * BLK]
            ref[j % 4, z, 1] = dv_t[:, z * BLK : (z + 1) * BLK]
    dq_ref[...] = (dq * SCALE).astype(BF16)
    first = core == 0
    for r in range(4):
        x_dst = lax.rem(x_pos + (4 - r), 4)
        for z in range(4):
            g = dot(attn_t, cot_ref[z * 4 + x_dst])
            left, right = g[:, :BLK], g[:, BLK:]
            own_ref[r, z, 2] = jnp.where(first, left, right).astype(BF16)
            oth_ref[r, z, 2] = jnp.where(first, right, left).astype(BF16)


def rot(shift):
    return [(i, (i + shift) % 4) for i in range(4)]


SWAP = [(0, 1), (1, 0)]
VMEM = pl.BlockSpec(memory_space=pltpu.VMEM)
SMEM = pl.BlockSpec(memory_space=pltpu.SMEM)


def body(queries, keys, values, w_out, grad_out):
    kv = jnp.stack([keys, values])
    cot = lax.all_gather(grad_out, "zl", axis=0)
    kv, cot = lax.optimization_barrier((kv, cot))
    cot = lax.all_gather(cot, "y", axis=0, tiled=True)
    kv0 = lax.all_gather(kv, "zh", axis=0)
    own = [kv0] + [lax.ppermute(kv0, "x", rot(k)) for k in (1, 2, 3)]
    other = [lax.ppermute(piece, "c", SWAP) for piece in own]
    pieces = own + other
    shape = jax.ShapeDtypeStruct
    attn, lse, partial_out = pl.pallas_call(
        forward_kernel,
        out_shape=(
            shape((BLK, HDIM), BF16),
            shape((BLK, BLK), F32),
            shape((16, BLK, 256), BF16),
        ),
        in_specs=[VMEM] * 10,
        out_specs=(VMEM,) * 3,
        scratch_shapes=[pltpu.VMEM((BLK, 32 * BLK), F32)],
        compiler_params=pltpu.CompilerParams(vmem_limit_bytes=40 << 20),
        cost_estimate=pl.CostEstimate(
            flops=6 * BLK * BLK * 4096, bytes_accessed=5 << 20, transcendentals=BLK * 4096
        ),
        name="forward",
    )(queries, *pieces, w_out)
    out = lax.psum_scatter(partial_out, "y", scatter_dimension=0, tiled=True)
    place = jnp.stack([lax.axis_index("c"), lax.axis_index("x")]).astype(jnp.int32)
    dq, pay_own, pay_oth = pl.pallas_call(
        backward_kernel,
        out_shape=(
            shape((BLK, HDIM), BF16),
            shape((4, 4, 3, BLK, BLK), BF16),
            shape((4, 4, 3, BLK, BLK), BF16),
        ),
        in_specs=[SMEM] + [VMEM] * 13,
        out_specs=(VMEM,) * 3,
        compiler_params=pltpu.CompilerParams(vmem_limit_bytes=40 << 20),
        cost_estimate=pl.CostEstimate(
            flops=14 * BLK * BLK * 4096, bytes_accessed=9 << 20, transcendentals=BLK * 4096
        ),
        name="backward",
    )(place, queries, *pieces, w_out, cot, attn, lse)
    got = lax.ppermute(pay_oth, "c", SWAP)
    parts = [(pay_own[r].astype(F32) + got[r].astype(F32)).astype(BF16) for r in range(4)]
    total = parts[0].astype(F32)
    for r in (1, 2, 3):
        total = total + lax.ppermute(parts[r], "x", rot(4 - r)).astype(F32)
    total = total.astype(BF16)
    total = jnp.sum(
        lax.all_to_all(total, "zh", 0, 0, tiled=True).astype(F32), axis=0
    )
    dk = (total[0].T * SCALE).astype(BF16)
    dv = total[1].T.astype(BF16)
    dw = total[2]
    out = lax.all_to_all(out, "zl", 0, 0, tiled=True)
    out = jnp.sum(out.astype(F32), axis=0).astype(BF16)
    return out, dq, dk, dv, dw


def solution(mesh):
    fine = Mesh(mesh.devices.reshape(4, 4, 4, 4, 2), ("y", "zl", "zh", "x", "c"))
    outer, inner = ("y", "zl"), ("zh", "x", "c")
    spread = P(inner, outer)
    return jax.shard_map(
        body,
        mesh=fine,
        in_specs=(spread, spread, spread, P(outer, None), spread),
        out_specs=(spread, spread, spread, spread, P(outer, inner)),
        check_vma=False,
    )
```

time: 583 us -> 179 us (0.31)
  the two profiles are of different devices: /device:TPU:4 before, /device:TPU:32 now
where the time goes in v1:
time: 179 us; the launch traced here: 178 us
  waiting for transfers between devices  54.8 us (31%)
  starting transfers between devices  47.3 us (26%)
  blocking collectives  39.5 us (22%)
  between operations  14.2 us (8%)
  local copies, waits for them, and re-layouts  8.21 us (5%)
  Pallas kernels  7.56 us (4%)
  other arithmetic  5.9 us (3%)
    all_to_all x1, waiting for transfers between devices, body(): lax.all_to_all(total, 'zh', 0, 0, tiled=True).astype(F32)  21.5 us
    all_gather x1, blocking collectives, body(): kv0 = lax.all_gather(kv, 'zh', axis=0)  21.3 us
    all_gather x1, blocking collectives, body(): cot = lax.all_gather(grad_out, 'zl', axis=0)  18.3 us
    reduce_scatter x1, waiting for transfers between devices, body(): out = lax.psum_scatter(partial_out, 'y', scatter_dimension=0, tiled=True)  16.7 us
    ppermute x3, waiting for transfers between devices, body(): total = total + lax.ppermute(parts[r], 'x', rot(4 - r)).astype(F32)  14 us
    all_to_all x1, starting transfers between devices, body(): lax.all_to_all(total, 'zh', 0, 0, tiled=True).astype(F32)  11 us
    ppermute x3, starting transfers between devices, body(): total = total + lax.ppermute(parts[r], 'x', rot(4 - r)).astype(F32)  10.7 us
    ppermute x3, starting transfers between devices, body(): own = [kv0] + [lax.ppermute(kv0, 'x', rot(k)) for k in (1, 2, 3)]  10.2 us
  transfers between devices with their start and end apart: 15, of which 8 were waited for; matrix products, arithmetic and copies ran while one was open for 2% of the time, Pallas kernels for 4%

profile of v1, /device:TPU:32, one launch (start us, length us, event | category | flops | bytes accessed | tf_op | source)
XLA Modules:
  0.0 177.5 jit_solution(7217601605480065839)
XLA Ops:
  7.2 0.0 copy-start
  7.2 0.0 all-gather.4.cloned.1.call-start
  7.2 18.3 %all-gather = bf16[512,256]{1,0:T(8,128)(2,1)} all-gather(bf16[128,256]{1,0:T(8,128)(2,1)} %param.9), channel_id=2, replica_groups=mesh['y'=4,'zl'=4,'zh'=4,'x'=4,'c'=2] {'zl'}, dimensions={0}, use_global_device_ids=true | all-gather | bytes 327680 | tf_op jit(solution)/shard_map/all_gather | solution.py:103
  25.5 0.8 pad_maximum_fusion
  26.3 0.0 all-gather.4.cloned.1.call-update
  26.3 0.0 reduce-scatter.2.cloned.1.call-start
  26.3 21.3 %all-gather.1 = bf16[8,128,128]{2,1,0:T(8,128)(2,1)S(1)} all-gather(bf16[2,128,128]{2,1,0:T(8,128)(2,1)S(1)} %pad_maximum_fusion), channel_id=3, replica_groups=mesh['y'=4,'zl'=4,'zh'=4,'x'=4,'c'=2] {'zh'}, dimensions={0}, use_global_device_ids=true | all-gather | bytes 327680 | tf_op jit(solution)/shard_map/all_gather | solution.py:106
  47.6 4.7 %collective-permute-start.2 = (bf16[4,2,128,128]{3,2,1,0:T(8,128)(2,1)S(1)}, bf16[4,2,128,128]{3,2,1,0:T(8,128)(2,1)S(1)}, u32[]{:S(2)}, u32[]{:S(2)}) collective-permute-start(bf16[4,2,128,128]{3,2,1,0:T(8,128)(2,1)S(1)} %bitcast.27), channel_id=1, source_target_pairs={{0,6},{2,0},{4,2},{6,4},{1,7},{3,1},{5,3},{7,5},{8,14},{10,8},{12,... | collective-permute-start | bytes 786440 | tf_op jit(solution)/shard_map/ppermute | solution.py:107
  52.3 2.7 %collective-permute-start.1 = (bf16[4,2,128,128]{3,2,1,0:T(8,128)(2,1)S(1)}, bf16[4,2,128,128]{3,2,1,0:T(8,128)(2,1)S(1)}, u32[]{:S(2)}, u32[]{:S(2)}) collective-permute-start(bf16[4,2,128,128]{3,2,1,0:T(8,128)(2,1)S(1)} %bitcast.28), channel_id=1, source_target_pairs={{0,4},{2,6},{4,0},{6,2},{1,5},{3,7},{5,1},{7,3},{8,12},{10,14},{12... | collective-permute-start | bytes 786440 | tf_op jit(solution)/shard_map/ppermute | solution.py:107
  55.0 2.8 %collective-permute-start = (bf16[4,2,128,128]{3,2,1,0:T(8,128)(2,1)S(1)}, bf16[4,2,128,128]{3,2,1,0:T(8,128)(2,1)S(1)}, u32[]{:S(2)}, u32[]{:S(2)}) collective-permute-start(bf16[4,2,128,128]{3,2,1,0:T(8,128)(2,1)S(1)} %bitcast.29), channel_id=1, source_target_pairs={{0,2},{2,4},{4,6},{6,0},{1,3},{3,5},{5,7},{7,1},{8,10},{10,12},{12... | collective-permute-start | bytes 786440 | tf_op jit(solution)/shard_map/ppermute | solution.py:107
  57.8 1.9 %collective-permute-start.3 = (bf16[4,2,128,128]{3,2,1,0:T(8,128)(2,1)S(1)}, bf16[4,2,128,128]{3,2,1,0:T(8,128)(2,1)S(1)}, u32[]{:S(2)}, u32[]{:S(2)}) collective-permute-start(bf16[4,2,128,128]{3,2,1,0:T(8,128)(2,1)S(1)} %bitcast.30), channel_id=1, source_target_pairs={{0,1},{1,0},{2,3},{3,2},{4,5},{5,4},{6,7},{7,6},{8,9},{9,8},{10,11... | collective-permute-start | bytes 786440 | tf_op jit(solution)/shard_map/ppermute | solution.py:108
  59.7 0.3 collective-permute-done.2.refs_3_
  60.0 2.1 %collective-permute-start.6 = (bf16[4,2,128,128]{3,2,1,0:T(8,128)(2,1)S(1)}, bf16[4,2,128,128]{3,2,1,0:T(8,128)(2,1)S(1)}, u32[]{:S(2)}, u32[]{:S(2)}) collective-permute-start(bf16[4,2,128,128]{3,2,1,0:T(8,128)(2,1)S(1)} %collective-permute-done.2.refs_3_), channel_id=1, source_target_pairs={{0,1},{1,0},{2,3},{3,2},{4,5},{5,4},{6,7},{7,6},{8,9},{9,8},{10,11... | collective-permute-start | bytes 786440 | tf_op jit(solution)/shard_map/ppermute | solution.py:108
  62.2 0.1 collective-permute-done.1.refs_2_
  62.3 2.1 %collective-permute-start.5 = (bf16[4,2,128,128]{3,2,1,0:T(8,128)(2,1)S(1)}, bf16[4,2,128,128]{3,2,1,0:T(8,128)(2,1)S(1)}, u32[]{:S(2)}, u32[]{:S(2)}) collective-permute-start(bf16[4,2,128,128]{3,2,1,0:T(8,128)(2,1)S(1)} %collective-permute-done.1.refs_2_), channel_id=1, source_target_pairs={{0,1},{1,0},{2,3},{3,2},{4,5},{5,4},{6,7},{7,6},{8,9},{9,8},{10,11... | collective-permute-start | bytes 786440 | tf_op jit(solution)/shard_map/ppermute | solution.py:108
  64.4 0.7 collective-permute-done.refs_1_
  65.0 0.0 copy-start.2
  65.0 1.9 %collective-permute-start.4 = (bf16[4,2,128,128]{3,2,1,0:T(8,128)(2,1)S(1)}, bf16[4,2,128,128]{3,2,1,0:T(8,128)(2,1)S(1)}, u32[]{:S(2)}, u32[]{:S(2)}) collective-permute-start(bf16[4,2,128,128]{3,2,1,0:T(8,128)(2,1)S(1)} %collective-permute-done.refs_1_), channel_id=1, source_target_pairs={{0,1},{1,0},{2,3},{3,2},{4,5},{5,4},{6,7},{7,6},{8,9},{9,8},{10,11... | collective-permute-start | bytes 786440 | tf_op jit(solution)/shard_map/ppermute | solution.py:108
  66.9 0.0 collective-permute-done.3.refs_4_
  67.0 0.0 copy-start.4
  67.0 0.0 collective-permute-done.6.refs_7_
  67.0 0.0 copy-start.6
  67.0 0.0 collective-permute-done.5.refs_6_
  67.0 0.0 copy-start.8
  67.0 1.4 collective-permute-done.4.refs_5_
  68.4 0.0 copy-done
  68.4 0.0 copy-start.12
  68.4 0.8 copy-done.12
  69.2 0.0 copy-start.10
  69.2 2.6 %forward.1 = (bf16[128,128]{1,0:T(8,128)(2,1)S(1)}, f32[128,128]{1,0:T(8,128)S(1)}, bf16[16,128,256]{2,1,0:T(8,128)(2,1)}) custom-call(bf16[128,128]{1,0:T(8,128)(2,1)S(1)} %copy-done.12, bf16[4,2,128,128]{3,2,1,0:T(8,128)(2,1)S(1)} %bitcast.31, bf16[4,2,128,128]{3,2,1,0:T(8,128)(2,1)S(1)} %collective-permute-done.refs_1_, ...), custom_call_target="tpu_custom_call" | custom-call | flops 402653184 | bytes 5242880 | tf_op jit(solution)/shard_map/forward/pallas_call | solution.py:111
  71.8 0.0 copy-done.2
  71.8 0.0 copy-done.4
  71.8 0.0 copy-done.6
  71.8 0.0 copy-done.8
  71.8 0.0 copy-done.10
  71.8 0.0 reduce-scatter.2.cloned.1.call-update
  71.8 0.1 pad_add_fusion.core_ref
  71.9 0.0 copy-done.13
  71.9 1.2 copy-done.1
  73.1 0.9 copy-done.3
  74.1 0.9 copy-done.5
  75.0 0.9 copy-done.7
  76.0 0.9 copy-done.9
  76.9 0.9 copy-done.11
  77.9 5.0 %backward.1 = (bf16[128,128]{1,0:T(8,128)(2,1)}, bf16[4,4,3,128,128]{4,3,2,1,0:T(8,128)(2,1)S(1)}, bf16[4,4,3,128,128]{4,3,2,1,0:T(8,128)(2,1)}) custom-call(s32[2]{0:T(128)S(1)} %pad_add_fusion.core_ref, bf16[128,128]{1,0:T(8,128)(2,1)S(1)} %copy-done.13, bf16[4,2,128,128]{3,2,1,0:T(8,128)(2,1)S(1)} %bitcast.32, bf16[4,2,128,128]{3,2,1,0:T(8,128)(2,1)S(1)} %copy-done.3, ...), custom_call_target="tpu_custom_call" | custom-call | flops 939524096 | bytes 9437184 | tf_op jit(solution)/shard_map/backward/pallas_call | solution.py:129
  82.9 2.0 %collective-permute-start.7 = (bf16[4,4,3,128,128]{4,3,2,1,0:T(8,128)(2,1)}, bf16[4,4,3,128,128]{4,3,2,1,0:T(8,128)(2,1)}, u32[]{:S(2)}, u32[]{:S(2)}) collective-permute-start(bf16[4,4,3,128,128]{4,3,2,1,0:T(8,128)(2,1)} %get-tuple-element.20), channel_id=1, source_target_pairs={{0,1},{1,0},{2,3},{3,2},{4,5},{5,4},{6,7},{7,6},{8,9},{9,8},{10,11... | collective-permute-start | bytes 4718600 | tf_op jit(solution)/shard_map/ppermute | solution.py:144
  84.9 16.7 %reduce-scatter.2.cloned.1.call-done = bf16[4,128,256]{2,1,0:T(8,128)(2,1)} async-done(((bf16[16,128,256]{2,1,0:T(8,128)(2,1)}), bf16[4,128,256]{2,1,0:T(8,128)(2,1)}) %reduce-scatter.2.cloned.1.call-update) | async-done | bytes 262160 | tf_op jit(solution)/shard_map/reduce_scatter | solution.py:127
  101.7 5.2 %all-to-all-start = ((bf16[4,128,256]{2,1,0:T(8,128)(2,1)}), bf16[4,128,256]{2,1,0:T(8,128)(2,1)S(1)}, u32[]{:S(2)}, u32[]{:S(2)}) async-start(bf16[4,128,256]{2,1,0:T(8,128)(2,1)} %reduce-scatter.2.cloned.1.call-done), calls=%async_computation.1 | async-start | bytes 524288 | tf_op jit(solution)/shard_map/all_to_all | solution.py:156
  106.9 0.0 collective-permute-done.7
  106.9 1.6 fusion.4
  108.5 4.6 %collective-permute-start.8 = (bf16[4,3,128,128]{3,2,1,0:T(8,128)(2,1)S(1)}, bf16[4,3,128,128]{3,2,1,0:T(8,128)(2,1)S(1)}, u32[]{:S(2)}, u32[]{:S(2)}) collective-permute-start(bf16[4,3,128,128]{3,2,1,0:T(8,128)(2,1)S(1)} %get-tuple-element.31), channel_id=1, source_target_pairs={{0,6},{2,0},{4,2},{6,4},{1,7},{3,1},{5,3},{7,5},{8,14},{10,8},{12,... | collective-permute-start | bytes 1179656 | tf_op jit(solution)/shard_map/ppermute | solution.py:148
  113.1 1.9 %collective-permute-start.10 = (bf16[4,3,128,128]{3,2,1,0:T(8,128)(2,1)S(1)}, bf16[4,3,128,128]{3,2,1,0:T(8,128)(2,1)S(1)}, u32[]{:S(2)}, u32[]{:S(2)}) collective-permute-start(bf16[4,3,128,128]{3,2,1,0:T(8,128)(2,1)S(1)} %get-tuple-element.32), channel_id=1, source_target_pairs={{0,2},{2,4},{4,6},{6,0},{1,3},{3,5},{5,7},{7,1},{8,10},{10,12},{12... | collective-permute-start | bytes 1179656 | tf_op jit(solution)/shard_map/ppermute | solution.py:148
  115.0 4.2 %collective-permute-start.9 = (bf16[4,3,128,128]{3,2,1,0:T(8,128)(2,1)S(1)}, bf16[4,3,128,128]{3,2,1,0:T(8,128)(2,1)S(1)}, u32[]{:S(2)}, u32[]{:S(2)}) collective-permute-start(bf16[4,3,128,128]{3,2,1,0:T(8,128)(2,1)S(1)} %get-tuple-element.33), channel_id=1, source_target_pairs={{0,4},{2,6},{4,0},{6,2},{1,5},{3,7},{5,1},{7,3},{8,12},{10,14},{12... | collective-permute-start | bytes 1179656 | tf_op jit(solution)/shard_map/ppermute | solution.py:148
  119.3 8.6 %collective-permute-done.8 = bf16[4,3,128,128]{3,2,1,0:T(8,128)(2,1)S(1)} collective-permute-done((bf16[4,3,128,128]{3,2,1,0:T(8,128)(2,1)S(1)}, bf16[4,3,128,128]{3,2,1,0:T(8,128)(2,1)S(1)}, u32[]{:S(2)}, u32[]{:S(2)}) %collective-permute-start.8) | collective-permute-done | bytes 393248 | tf_op jit(solution)/shard_map/ppermute | solution.py:148
  127.9 5.3 %collective-permute-done.10 = bf16[4,3,128,128]{3,2,1,0:T(8,128)(2,1)S(1)} collective-permute-done((bf16[4,3,128,128]{3,2,1,0:T(8,128)(2,1)S(1)}, bf16[4,3,128,128]{3,2,1,0:T(8,128)(2,1)S(1)}, u32[]{:S(2)}, u32[]{:S(2)}) %collective-permute-start.10) | collective-permute-done | bytes 393248 | tf_op jit(solution)/shard_map/ppermute | solution.py:148
  133.3 0.0 collective-permute-done.9
  133.3 2.1 %fusion.2 = bf16[4,3,128,128]{3,2,1,0:T(8,128)(2,1)} fusion(bf16[4,3,128,128]{3,2,1,0:T(8,128)(2,1)S(1)} %collective-permute-done.10, bf16[4,3,128,128]{3,2,1,0:T(8,128)(2,1)S(1)} %collective-permute-done.9, bf16[4,3,128,128]{3,2,1,0:T(8,128)(2,1)S(1)} %collective-permute-done.8, bf16[4,4,3,128,128]{4,3,2,1,0:T(8,128)(2,1)} %collective-permute-done.7, ...), kind=kLoop, calls=%fused_computation.3 | loop fusion | flops 2359296 | bytes 2359296 | tf_op jit(solution)/shard_map/convert_element_type | solution.py:149
  135.3 0.0 all-to-all-done
  135.3 11.0 %all-to-all-start.1 = ((bf16[4,3,128,128]{3,2,1,0:T(8,128)(2,1)}), bf16[4,3,128,128]{3,2,1,0:T(8,128)(2,1)S(1)}, u32[]{:S(2)}, u32[]{:S(2)}) async-start(bf16[4,3,128,128]{3,2,1,0:T(8,128)(2,1)} %fusion.2), calls=%async_computation.2 | async-start | bytes 786432 | tf_op jit(solution)/shard_map/all_to_all | solution.py:151
  146.4 0.7 reduce_sum.21
  147.0 21.5 %all-to-all-done.1 = bf16[4,3,128,128]{3,2,1,0:T(8,128)(2,1)S(1)} async-done(((bf16[4,3,128,128]{3,2,1,0:T(8,128)(2,1)}), bf16[4,3,128,128]{3,2,1,0:T(8,128)(2,1)S(1)}, u32[]{:S(2)}, u32[]{:S(2)}) %all-to-all-start.1) | async-done | bytes 393248 | tf_op jit(solution)/shard_map/all_to_all | solution.py:151
  168.6 0.6 slice_bitcast_fusion
  169.3 0.7 copy.13
  170.0 0.7 copy.12
  (10 shorter events, 0.1 us)
Async XLA Ops:
  7.2 61.3 %copy-start = (bf16[128,4096]{1,0:T(8,128)(2,1)S(1)}, bf16[128,4096]{1,0:T(8,128)(2,1)}, u32[]{:S(2)}) copy-start(bf16[128,4096]{1,0:T(8,128)(2,1)} %refs_8_.3) | copy-start | bytes 3145732
  7.2 64.7 %all-gather.4.cloned.1.call-start = ((), (), s32[]{:S(2)}) async-start(), calls=%async_computation.4 | async-start | bytes 1310720 | tf_op jit(solution)/shard_map/all_gather | solution.py:105
  26.3 75.4 %reduce-scatter.2.cloned.1.call-start = ((), (), s32[]{:S(2)}) async-start(), calls=%async_computation.3 | async-start | bytes 1310720 | tf_op jit(solution)/shard_map/reduce_scatter | solution.py:127
  47.6 12.4 %collective-permute-start.2 = (bf16[4,2,128,128]{3,2,1,0:T(8,128)(2,1)S(1)}, bf16[4,2,128,128]{3,2,1,0:T(8,128)(2,1)S(1)}, u32[]{:S(2)}, u32[]{:S(2)}) collective-permute-start(bf16[4,2,128,128]{3,2,1,0:T(8,128)(2,1)S(1)} %bitcast.27), channel_id=1, source_target_pairs={{0,6},{2,0},{4,2},{6,4},{1,7},{3,1},{5,3},{7,5},{8,14},{10,8},{12,... | collective-permute-start | bytes 786440 | tf_op jit(solution)/shard_map/ppermute | solution.py:107
  52.3 10.0 %collective-permute-start.1 = (bf16[4,2,128,128]{3,2,1,0:T(8,128)(2,1)S(1)}, bf16[4,2,128,128]{3,2,1,0:T(8,128)(2,1)S(1)}, u32[]{:S(2)}, u32[]{:S(2)}) collective-permute-start(bf16[4,2,128,128]{3,2,1,0:T(8,128)(2,1)S(1)} %bitcast.28), channel_id=1, source_target_pairs={{0,4},{2,6},{4,0},{6,2},{1,5},{3,7},{5,1},{7,3},{8,12},{10,14},{12... | collective-permute-start | bytes 786440 | tf_op jit(solution)/shard_map/ppermute | solution.py:107
  55.0 10.0 %collective-permute-start = (bf16[4,2,128,128]{3,2,1,0:T(8,128)(2,1)S(1)}, bf16[4,2,128,128]{3,2,1,0:T(8,128)(2,1)S(1)}, u32[]{:S(2)}, u32[]{:S(2)}) collective-permute-start(bf16[4,2,128,128]{3,2,1,0:T(8,128)(2,1)S(1)} %bitcast.29), channel_id=1, source_target_pairs={{0,2},{2,4},{4,6},{6,0},{1,3},{3,5},{5,7},{7,1},{8,10},{10,12},{12... | collective-permute-start | bytes 786440 | tf_op jit(solution)/shard_map/ppermute | solution.py:107
  57.8 9.1 %collective-permute-start.3 = (bf16[4,2,128,128]{3,2,1,0:T(8,128)(2,1)S(1)}, bf16[4,2,128,128]{3,2,1,0:T(8,128)(2,1)S(1)}, u32[]{:S(2)}, u32[]{:S(2)}) collective-permute-start(bf16[4,2,128,128]{3,2,1,0:T(8,128)(2,1)S(1)} %bitcast.30), channel_id=1, source_target_pairs={{0,1},{1,0},{2,3},{3,2},{4,5},{5,4},{6,7},{7,6},{8,9},{9,8},{10,11... | collective-permute-start | bytes 786440 | tf_op jit(solution)/shard_map/ppermute | solution.py:108
  60.0 6.9 %collective-permute-start.6 = (bf16[4,2,128,128]{3,2,1,0:T(8,128)(2,1)S(1)}, bf16[4,2,128,128]{3,2,1,0:T(8,128)(2,1)S(1)}, u32[]{:S(2)}, u32[]{:S(2)}) collective-permute-start(bf16[4,2,128,128]{3,2,1,0:T(8,128)(2,1)S(1)} %collective-permute-done.2.refs_3_), channel_id=1, source_target_pairs={{0,1},{1,0},{2,3},{3,2},{4,5},{5,4},{6,7},{7,6},{8,9},{9,8},{10,11... | collective-permute-start | bytes 786440 | tf_op jit(solution)/shard_map/ppermute | solution.py:108
  62.3 4.7 %collective-permute-start.5 = (bf16[4,2,128,128]{3,2,1,0:T(8,128)(2,1)S(1)}, bf16[4,2,128,128]{3,2,1,0:T(8,128)(2,1)S(1)}, u32[]{:S(2)}, u32[]{:S(2)}) collective-permute-start(bf16[4,2,128,128]{3,2,1,0:T(8,128)(2,1)S(1)} %collective-permute-done.1.refs_2_), channel_id=1, source_target_pairs={{0,1},{1,0},{2,3},{3,2},{4,5},{5,4},{6,7},{7,6},{8,9},{9,8},{10,11... | collective-permute-start | bytes 786440 | tf_op jit(solution)/shard_map/ppermute | solution.py:108
  65.0 6.8 %copy-start.2 = (bf16[4,2,128,128]{3,2,1,0:T(8,128)(2,1)}, bf16[4,2,128,128]{3,2,1,0:T(8,128)(2,1)S(1)}, u32[]{:S(2)}) copy-start(bf16[4,2,128,128]{3,2,1,0:T(8,128)(2,1)S(1)} %collective-permute-done.refs_1_) | copy-start | bytes 786436
  65.0 3.4 %collective-permute-start.4 = (bf16[4,2,128,128]{3,2,1,0:T(8,128)(2,1)S(1)}, bf16[4,2,128,128]{3,2,1,0:T(8,128)(2,1)S(1)}, u32[]{:S(2)}, u32[]{:S(2)}) collective-permute-start(bf16[4,2,128,128]{3,2,1,0:T(8,128)(2,1)S(1)} %collective-permute-done.refs_1_), channel_id=1, source_target_pairs={{0,1},{1,0},{2,3},{3,2},{4,5},{5,4},{6,7},{7,6},{8,9},{9,8},{10,11... | collective-permute-start | bytes 786440 | tf_op jit(solution)/shard_map/ppermute | solution.py:108
  67.0 4.8 %copy-start.4 = (bf16[4,2,128,128]{3,2,1,0:T(8,128)(2,1)}, bf16[4,2,128,128]{3,2,1,0:T(8,128)(2,1)S(1)}, u32[]{:S(2)}) copy-start(bf16[4,2,128,128]{3,2,1,0:T(8,128)(2,1)S(1)} %collective-permute-done.3.refs_4_) | copy-start | bytes 786436
  67.0 4.8 %copy-start.6 = (bf16[4,2,128,128]{3,2,1,0:T(8,128)(2,1)}, bf16[4,2,128,128]{3,2,1,0:T(8,128)(2,1)S(1)}, u32[]{:S(2)}) copy-start(bf16[4,2,128,128]{3,2,1,0:T(8,128)(2,1)S(1)} %collective-permute-done.6.refs_7_) | copy-start | bytes 786436
  67.0 4.8 %copy-start.8 = (bf16[4,2,128,128]{3,2,1,0:T(8,128)(2,1)}, bf16[4,2,128,128]{3,2,1,0:T(8,128)(2,1)S(1)}, u32[]{:S(2)}) copy-start(bf16[4,2,128,128]{3,2,1,0:T(8,128)(2,1)S(1)} %collective-permute-done.5.refs_6_) | copy-start | bytes 786436
  68.4 0.8 copy-start.12
  69.2 2.6 %copy-start.10 = (bf16[4,2,128,128]{3,2,1,0:T(8,128)(2,1)}, bf16[4,2,128,128]{3,2,1,0:T(8,128)(2,1)S(1)}, u32[]{:S(2)}) copy-start(bf16[4,2,128,128]{3,2,1,0:T(8,128)(2,1)S(1)} %collective-permute-done.4.refs_5_) | copy-start | bytes 786436
  69.2 2.7 %copy-start.13 = (bf16[128,128]{1,0:T(8,128)(2,1)S(1)}, bf16[128,128]{1,0:T(8,128)(2,1)}, u32[]{:S(2)}) copy-start(bf16[128,128]{1,0:T(8,128)(2,1)} %q_ref.3) | copy-start | bytes 98308
  71.9 1.2 copy-start.1
  73.1 0.9 copy-start.3
  74.1 0.9 copy-start.5
  75.0 0.9 copy-start.7
  76.0 0.9 copy-start.9
  76.9 0.9 copy-start.11
  82.9 24.0 %collective-permute-start.7 = (bf16[4,4,3,128,128]{4,3,2,1,0:T(8,128)(2,1)}, bf16[4,4,3,128,128]{4,3,2,1,0:T(8,128)(2,1)}, u32[]{:S(2)}, u32[]{:S(2)}) collective-permute-start(bf16[4,4,3,128,128]{4,3,2,1,0:T(8,128)(2,1)} %get-tuple-element.20), channel_id=1, source_target_pairs={{0,1},{1,0},{2,3},{3,2},{4,5},{5,4},{6,7},{7,6},{8,9},{9,8},{10,11... | collective-permute-start | bytes 4718600 | tf_op jit(solution)/shard_map/ppermute | solution.py:144
  101.7 33.7 %all-to-all-start = ((bf16[4,128,256]{2,1,0:T(8,128)(2,1)}), bf16[4,128,256]{2,1,0:T(8,128)(2,1)S(1)}, u32[]{:S(2)}, u32[]{:S(2)}) async-start(bf16[4,128,256]{2,1,0:T(8,128)(2,1)} %reduce-scatter.2.cloned.1.call-done), calls=%async_computation.1 | async-start | bytes 524288 | tf_op jit(solution)/shard_map/all_to_all | solution.py:156
  108.5 19.4 %collective-permute-start.8 = (bf16[4,3,128,128]{3,2,1,0:T(8,128)(2,1)S(1)}, bf16[4,3,128,128]{3,2,1,0:T(8,128)(2,1)S(1)}, u32[]{:S(2)}, u32[]{:S(2)}) collective-permute-start(bf16[4,3,128,128]{3,2,1,0:T(8,128)(2,1)S(1)} %get-tuple-element.31), channel_id=1, source_target_pairs={{0,6},{2,0},{4,2},{6,4},{1,7},{3,1},{5,3},{7,5},{8,14},{10,8},{12,... | collective-permute-start | bytes 1179656 | tf_op jit(solution)/shard_map/ppermute | solution.py:148
  113.1 20.1 %collective-permute-start.10 = (bf16[4,3,128,128]{3,2,1,0:T(8,128)(2,1)S(1)}, bf16[4,3,128,128]{3,2,1,0:T(8,128)(2,1)S(1)}, u32[]{:S(2)}, u32[]{:S(2)}) collective-permute-start(bf16[4,3,128,128]{3,2,1,0:T(8,128)(2,1)S(1)} %get-tuple-element.32), channel_id=1, source_target_pairs={{0,2},{2,4},{4,6},{6,0},{1,3},{3,5},{5,7},{7,1},{8,10},{10,12},{12... | collective-permute-start | bytes 1179656 | tf_op jit(solution)/shard_map/ppermute | solution.py:148
  115.0 18.2 %collective-permute-start.9 = (bf16[4,3,128,128]{3,2,1,0:T(8,128)(2,1)S(1)}, bf16[4,3,128,128]{3,2,1,0:T(8,128)(2,1)S(1)}, u32[]{:S(2)}, u32[]{:S(2)}) collective-permute-start(bf16[4,3,128,128]{3,2,1,0:T(8,128)(2,1)S(1)} %get-tuple-element.33), channel_id=1, source_target_pairs={{0,4},{2,6},{4,0},{6,2},{1,5},{3,7},{5,1},{7,3},{8,12},{10,14},{12... | collective-permute-start | bytes 1179656 | tf_op jit(solution)/shard_map/ppermute | solution.py:148
  135.3 33.2 %all-to-all-start.1 = ((bf16[4,3,128,128]{3,2,1,0:T(8,128)(2,1)}), bf16[4,3,128,128]{3,2,1,0:T(8,128)(2,1)S(1)}, u32[]{:S(2)}, u32[]{:S(2)}) async-start(bf16[4,3,128,128]{3,2,1,0:T(8,128)(2,1)} %fusion.2), calls=%async_computation.2 | async-start | bytes 786432 | tf_op jit(solution)/shard_map/all_to_all | solution.py:151
Sparse Core Ops, SparseCore 0:
  26.4 32.4 all-gather.3
  71.9 29.6 reduce-scatter.1

commit v2 on v1

v2 whole, which is shorter than its diff:
```python
import functools

import jax
import jax.numpy as jnp
from jax import lax
from jax.experimental import pallas as pl
from jax.experimental.pallas import tpu as pltpu
from jax.sharding import Mesh, PartitionSpec as P

HDIM = 128
BLK = 128
SCALE = HDIM ** (-0.5)
F32 = jnp.float32
BF16 = jnp.bfloat16


def dot(a, b, dims=((1,), (0,))):
    return lax.dot_general(a, b, (dims, ((), ())), preferred_element_type=F32)


def block_of(place_ref, y_step, zl_step):
    y = lax.rem(place_ref[1] + (4 + y_step), 4)
    zl = lax.rem(place_ref[2] + (4 + zl_step), 4)
    return y, zl


def pack_kernel(place_ref, q_ref, k_ref, v_ref, grad_ref, kv_ref, gift_ref, mine_ref):
    for z in range(4):
        kv_ref[z, 0] = k_ref[...]
        kv_ref[z, 1] = v_ref[...]
    first = place_ref[0] == 0
    left, right = grad_ref[:, :BLK], grad_ref[:, BLK:]
    mine_ref[...] = jnp.where(first, left, right)
    gift_ref[:, :HDIM] = q_ref[...]
    gift_ref[:, HDIM:] = jnp.where(first, right, left)


def forward_kernel(place_ref, q_ref, other_ref, kv_ref, w_ref, cot0, cot1, cot2, cot3, part_ref, s_ref):
    grad = jnp.zeros((2 * BLK, HDIM), F32)
    for r, cot_ref in enumerate((cot0, cot1, cot2, cot3)):
        for t in range(4):
            y, zl = block_of(place_ref, -r, -t)
            start = pl.multiple_of((y * 4 + zl) * 256 + place_ref[0] * BLK, BLK)
            grad = grad + dot(cot_ref[t], w_ref[:, pl.ds(start, BLK)], ((1,), (1,)))
    part_ref[:, :HDIM] = grad
    q = jnp.concatenate([q_ref[...], other_ref[:, :HDIM]], axis=0)
    width = 4 * BLK
    top = jnp.full((2 * BLK, BLK), -jnp.inf, F32)
    for j in range(4):
        k = kv_ref[j, :, 0].reshape(width, HDIM)
        s = dot(q, k, ((1,), (1,))) * SCALE
        s_ref[:, j * width : (j + 1) * width] = s
        for t in range(4):
            top = jnp.maximum(top, s[:, t * BLK : (t + 1) * BLK])
    row_max = jnp.max(top, axis=1, keepdims=True)
    sums = jnp.zeros((2 * BLK, BLK), F32)
    acc = jnp.zeros((2 * BLK, HDIM), F32)
    for j in range(4):
        p = jnp.exp(s_ref[:, j * width : (j + 1) * width] - row_max)
        for t in range(4):
            sums = sums + p[:, t * BLK : (t + 1) * BLK]
        v = kv_ref[j, :, 1].reshape(width, HDIM)
        acc = acc + dot(p.astype(BF16), v)
    totals = jnp.sum(sums, axis=1, keepdims=True)
    part_ref[:, HDIM : 2 * HDIM] = acc / totals
    part_ref[:, 2 * HDIM :] = jnp.broadcast_to(row_max + jnp.log(totals), (2 * BLK, BLK))


def merge_kernel(place_ref, mine_ref, theirs_ref, w_ref, grad_ref, attn_ref, lse_ref, dots_ref, *out_refs):
    for half in range(2):
        rows = slice(half * BLK, (half + 1) * BLK)
        swapped = slice((1 - half) * BLK, (2 - half) * BLK)
        grad = (mine_ref[rows, :HDIM] + theirs_ref[swapped, :HDIM]).astype(BF16)
        a, b = mine_ref[rows, 2 * HDIM :], theirs_ref[swapped, 2 * HDIM :]
        top = jnp.maximum(a, b)
        lse = top + jnp.log(jnp.exp(a - top) + jnp.exp(b - top))
        attn = mine_ref[rows, HDIM : 2 * HDIM] * jnp.exp(a - lse)
        attn = attn + theirs_ref[swapped, HDIM : 2 * HDIM] * jnp.exp(b - lse)
        attn = attn.astype(BF16)
        dots = jnp.sum(grad.astype(F32) * attn.astype(F32), axis=1, keepdims=True)
        grad_ref[rows, :] = grad
        attn_ref[rows, :] = attn
        lse_ref[rows, :] = lse
        dots_ref[rows, :] = jnp.broadcast_to(dots, (BLK, BLK))
    attn = attn_ref[:BLK, :]
    for r, out_ref in enumerate(out_refs):
        for t in range(4):
            y, zl = block_of(place_ref, r, t)
            cols = pl.ds(pl.multiple_of((y * 4 + zl) * 256, 256), 256)
            out_ref[t] = dot(attn, w_ref[:, cols]).astype(BF16)


def backward_kernel(
    place_ref,
    q_ref,
    other_ref,
    kv_ref,
    cot0,
    cot1,
    cot2,
    cot3,
    grad_ref,
    attn_ref,
    lse_ref,
    dots_ref,
    dq_own_ref,
    dq_oth_ref,
    pay_ref,
):
    width = 4 * BLK
    q = jnp.concatenate([q_ref[...], other_ref[:, :HDIM]], axis=0)
    grad = grad_ref[...]
    lse = lse_ref[:, :1]
    dots = dots_ref[:, :1]
    q_t = q.T
    grad_t = grad.T
    attn_t = attn_ref[...].T
    dq = jnp.zeros((2 * BLK, HDIM), F32)
    for j in range(4):
        k = kv_ref[j, :, 0].reshape(width, HDIM)
        v = kv_ref[j, :, 1].reshape(width, HDIM)
        s = dot(q, k, ((1,), (1,))) * SCALE
        p = jnp.exp(s - lse)
        dp = dot(grad, v, ((1,), (1,)))
        ds = (p * (dp - dots)).astype(BF16)
        dq = dq + dot(ds, k)
        dk_t = dot(q_t, ds).astype(BF16)
        dv_t = dot(grad_t, p.astype(BF16)).astype(BF16)
        for z in range(4):
            pay_ref[j, z, 0] = dk_t[:, z * BLK : (z + 1) * BLK]
            pay_ref[j, z, 1] = dv_t[:, z * BLK : (z + 1) * BLK]
    dq_own_ref[...] = dq[:BLK]
    dq_oth_ref[...] = dq[BLK:]
    for r, cot_ref in enumerate((cot0, cot1, cot2, cot3)):
        for t in range(4):
            z, x = block_of(place_ref, -r, -t)
            pay_ref[x, z, 2] = dot(attn_t, cot_ref[t]).astype(BF16)


def finish_kernel(parts_ref, dk_ref, dv_ref, dw_ref):
    total = jnp.sum(parts_ref[...].astype(F32), axis=0)
    dk_ref[...] = (total[0] * SCALE).T.astype(BF16)
    dv_ref[...] = total[1].T.astype(BF16)
    dw_ref[...] = total[2]


FIRST, SECOND = "zl", "y"
VMEM = pl.BlockSpec(memory_space=pltpu.VMEM)
SMEM = pl.BlockSpec(memory_space=pltpu.SMEM)
shape = jax.ShapeDtypeStruct


def exchange(blocks, axis):
    return lax.all_to_all(blocks, axis, 0, 0, tiled=True)


def spread_over(block, axis):
    return exchange(jnp.broadcast_to(block[None], (4,) + block.shape), axis)


def shift(block, axis, by):
    return lax.ppermute(block, axis, [(i, (i + by) % 4) for i in range(4)])


def swap(block):
    return lax.ppermute(block, "c", [(0, 1), (1, 0)])


def add_all(blocks):
    total = blocks[0].astype(F32)
    for block in blocks[1:]:
        total = total + block.astype(F32)
    return total.astype(BF16)


def call(kernel, name, out_shape, in_specs, limit, flops, nbytes, exps=0, scratch=()):
    return pl.pallas_call(
        kernel,
        out_shape=out_shape,
        in_specs=in_specs,
        out_specs=jax.tree.map(lambda _: VMEM, out_shape),
        scratch_shapes=scratch,
        compiler_params=pltpu.CompilerParams(vmem_limit_bytes=limit << 20),
        cost_estimate=pl.CostEstimate(flops=flops, bytes_accessed=nbytes, transcendentals=exps),
        name=name,
    )


def body(queries, keys, values, w_out, grad_out):
    unit = BLK * BLK * 4096
    tile = shape((BLK, BLK), BF16)
    pair = shape((2 * BLK, HDIM), BF16)
    wide = shape((2 * BLK, BLK), F32)
    place = jnp.stack([lax.axis_index(a) for a in ("c", "y", "zl")]).astype(jnp.int32)
    kv, gift, mine = call(
        pack_kernel,
        "pack",
        (shape((4, 2, BLK, BLK), BF16), shape((BLK, 2 * BLK), BF16), tile),
        [SMEM] + [VMEM] * 4,
        4,
        0,
        1 << 19,
    )(place, queries, keys, values, grad_out)
    place, kv, mine, gift = lax.optimization_barrier((place, kv, mine, gift))
    other = swap(gift)
    kv = exchange(kv, "zh")
    cot = jnp.concatenate([mine, other[:, BLK:]], axis=0)
    cot = jnp.stack([cot] + [shift(cot, FIRST, k) for k in (1, 2, 3)])
    kv, cot = lax.optimization_barrier((kv, cot))
    kv = spread_over(kv, "x")
    cots = [cot] + [shift(cot, SECOND, k) for k in (2, 1, 3)]
    kv, cots = lax.optimization_barrier((kv, cots))
    cots = [cots[0], cots[2], cots[1], cots[3]]
    part = call(
        forward_kernel,
        "forward",
        shape((2 * BLK, 3 * BLK), F32),
        [SMEM] + [VMEM] * 8,
        8,
        6 * unit,
        5 << 20,
        unit // BLK,
        [pltpu.VMEM((2 * BLK, 16 * BLK), F32)],
    )(place, queries, other, kv, w_out, *cots)
    theirs = swap(part)
    quarter = shape((4, BLK, 256), BF16)
    grad, attn, lse, dots, *outs = call(
        merge_kernel,
        "merge",
        (pair, pair, wide, wide) + (quarter,) * 4,
        [SMEM] + [VMEM] * 3,
        8,
        2 * unit,
        2 << 20,
    )(place, part, theirs, w_out)
    dq, dq_other, pay = call(
        backward_kernel,
        "backward",
        (shape((BLK, HDIM), F32), shape((BLK, HDIM), F32), shape((4, 4, 3, BLK, BLK), BF16)),
        [SMEM] + [VMEM] * 11,
        8,
        12 * unit,
        6 << 20,
        unit // BLK,
    )(place, queries, other, kv, *cots, grad, attn, lse, dots)
    pay, outs = lax.optimization_barrier((pay, outs))
    pay = exchange(pay, "x")
    outs = [outs[0]] + [shift(outs[k], SECOND, k) for k in (2, 1, 3)]
    pay, outs = lax.optimization_barrier((pay, outs))
    pay = add_all([pay[r] for r in range(4)])
    out = add_all(outs)
    pay, out = lax.optimization_barrier((pay, out))
    pay = exchange(pay, "zh")
    out = add_all([out[0]] + [shift(out[k], FIRST, k) for k in (1, 2, 3)])
    dq = ((dq + swap(dq_other)) * SCALE).astype(BF16)
    dk, dv, dw = call(
        finish_kernel, "finish", (tile, tile, shape((BLK, BLK), F32)), [VMEM], 4, 0, 1 << 20
    )(pay)
    return out, dq, dk, dv, dw


def solution(mesh):
    fine = Mesh(mesh.devices.reshape(4, 4, 4, 4, 2), ("y", "zl", "zh", "x", "c"))
    outer, inner = ("y", "zl"), ("zh", "x", "c")
    spread = P(inner, outer)
    return jax.shard_map(
        body,
        mesh=fine,
        in_specs=(spread, spread, spread, P(outer, None), spread),
        out_specs=(spread, spread, spread, spread, P(outer, inner)),
        check_vma=False,
    )
```

time: 179 us -> 146 us (0.82)
  blocking collectives: 39.5 us -> 0 us
  starting transfers between devices: 47.3 us -> 78.7 us
  between operations: 14.2 us -> 0.88 us
  waiting for transfers between devices: 54.8 us -> 46.6 us
  local copies, waits for them, and re-layouts: 8.21 us -> 5.76 us
  other arithmetic: 5.9 us -> 3.87 us
    all_gather x2 -> x0, blocking collectives: 39.5 us -> none  [the longest x1 21.3 us: body(): kv0 = lax.all_gather(kv, 'zh', axis=0)]
    ppermute x11 -> x15, waiting for transfers between devices: 16.5 us -> 35.2 us  [the longest x12 32.3 us: shift(): return lax.ppermute(block, axis, [(i, (i + by) % 4) for i in range(4)])]
    all_to_all x2 -> x4, starting transfers between devices: 16.3 us -> 33.4 us  [exchange(): return lax.all_to_all(blocks, axis, 0, 0, tiled=True)]
    reduce_scatter x1 -> x0, waiting for transfers between devices: 16.7 us -> none  [body(): out = lax.psum_scatter(partial_out, 'y', scatter_dimension=0, tiled=True)]
    ppermute x11 -> x15, starting transfers between devices: 31 us -> 45.3 us  [the longest x12 39.5 us: shift(): return lax.ppermute(block, axis, [(i, (i + by) % 4) for i in range(4)])]
    all_to_all x2 -> x4, waiting for transfers between devices: 21.5 us -> 11.4 us  [exchange(): return lax.all_to_all(blocks, axis, 0, 0, tiled=True)]
    unnamed x30 -> x24, local copies, waits for them, and re-layouts: 8.2 us -> 4.52 us
    add x0 -> x1, other arithmetic: none -> 2.33 us  [add_all(): total = total + block.astype(F32)]
  transfers between devices with their start and end apart: 15 -> 19, of which waited for: 8 -> 13; matrix products, arithmetic and copies ran while one was open for 2% -> 1% of each run, Pallas kernels for 4% -> 0%
where the time goes in v2:
time: 146 us; the launch traced here: 144 us
  starting transfers between devices  78.7 us (54%)
  waiting for transfers between devices  46.6 us (32%)
  Pallas kernels  8.68 us (6%)
  local copies, waits for them, and re-layouts  5.76 us (4%)
  other arithmetic  3.87 us (3%)
    ppermute x12, starting transfers between devices, shift(): return lax.ppermute(block, axis, [(i, (i + by) % 4) for i in range(4)])  39.5 us
    all_to_all x4, starting transfers between devices, exchange(): return lax.all_to_all(blocks, axis, 0, 0, tiled=True)  33.4 us
    ppermute x12, waiting for transfers between devices, shift(): return lax.ppermute(block, axis, [(i, (i + by) % 4) for i in range(4)])  32.3 us
    all_to_all x4, waiting for transfers between devices, exchange(): return lax.all_to_all(blocks, axis, 0, 0, tiled=True)  11.4 us
    ppermute x3, starting transfers between devices, swap(): return lax.ppermute(block, 'c', [(0, 1), (1, 0)])  5.74 us
    unnamed x24, local copies, waits for them, and re-layouts  4.52 us
    pallas_call x1, Pallas kernels, body(): call(backward_kernel, 'backward', (shape((BLK, HDIM), F32), shape((BLK, H...  3.62 us
  transfers between devices with their start and end apart: 19, of which 13 were waited for; matrix products, arithmetic and copies ran while one was open for 1% of the time, Pallas kernels for 0%

profile of v2, /device:TPU:32, one launch (start us, length us, event | category | flops | bytes accessed | tf_op | source)
XLA Modules:
  0.0 144.4 jit_solution(9410507150692296988)
XLA Ops:
  0.6 0.1 pad_add_fusion.place_ref
  0.7 0.8 copy-done.1
  1.5 0.8 copy-done.3
  2.3 0.8 copy-done.4
  3.1 0.8 copy-done.5
  3.8 1.3 pack.1
  5.1 14.2 %all-to-all-start = ((bf16[4,2,128,128]{3,2,1,0:T(8,128)(2,1)}), bf16[4,2,128,128]{3,2,1,0:T(8,128)(2,1)S(1)}, u32[]{:S(2)}, u32[]{:S(2)}) async-start(bf16[4,2,128,128]{3,2,1,0:T(8,128)(2,1)} %get-tuple-element.50), calls=%async_computation | async-start | bytes 524288 | tf_op jit(solution)/shard_map/all_to_all | solution.py:154
  19.3 1.9 %collective-permute-start = (bf16[128,256]{1,0:T(8,128)(2,1)S(1)}, bf16[128,256]{1,0:T(8,128)(2,1)S(1)}, u32[]{:S(2)}, u32[]{:S(2)}) collective-permute-start(bf16[128,256]{1,0:T(8,128)(2,1)S(1)} %get-tuple-element.49), channel_id=1, source_target_pairs={{0,1},{1,0},{2,3},{3,2},{4,5},{5,4},{6,7},{7,6},{8,9},{9,8},{10,11... | collective-permute-start | bytes 196616 | tf_op jit(solution)/shard_map/ppermute | solution.py:166
  21.2 1.2 collective-permute-done.other_ref
  22.5 3.4 %collective-permute-start.2 = (bf16[256,128]{1,0:T(8,128)(2,1)S(1)}, bf16[256,128]{1,0:T(8,128)(2,1)S(1)}, u32[]{:S(2)}, u32[]{:S(2)}) collective-permute-start(bf16[256,128]{1,0:T(8,128)(2,1)S(1)} %get-tuple-element.89), channel_id=1, source_target_pairs={{0,64},{32,96},{64,0},{96,32},{1,65},{33,97},{65,1},{97,33},{2,66}... | collective-permute-start | bytes 196616 | tf_op jit(solution)/shard_map/ppermute | solution.py:162
  25.9 2.9 %collective-permute-start.1 = (bf16[256,128]{1,0:T(8,128)(2,1)S(1)}, bf16[256,128]{1,0:T(8,128)(2,1)S(1)}, u32[]{:S(2)}, u32[]{:S(2)}) collective-permute-start(bf16[256,128]{1,0:T(8,128)(2,1)S(1)} %get-tuple-element.89), channel_id=1, source_target_pairs={{0,32},{32,64},{64,96},{96,0},{1,33},{33,65},{65,97},{97,1},{2,34}... | collective-permute-start | bytes 196616 | tf_op jit(solution)/shard_map/ppermute | solution.py:162
  28.8 2.9 %collective-permute-start.3 = (bf16[256,128]{1,0:T(8,128)(2,1)S(1)}, bf16[256,128]{1,0:T(8,128)(2,1)S(1)}, u32[]{:S(2)}, u32[]{:S(2)}) collective-permute-start(bf16[256,128]{1,0:T(8,128)(2,1)S(1)} %get-tuple-element.89), channel_id=1, source_target_pairs={{0,96},{32,0},{64,32},{96,64},{1,97},{33,1},{65,33},{97,65},{2,98}... | collective-permute-start | bytes 196616 | tf_op jit(solution)/shard_map/ppermute | solution.py:162
  31.7 3.2 %collective-permute-done.2 = bf16[256,128]{1,0:T(8,128)(2,1)S(1)} collective-permute-done((bf16[256,128]{1,0:T(8,128)(2,1)S(1)}, bf16[256,128]{1,0:T(8,128)(2,1)S(1)}, u32[]{:S(2)}, u32[]{:S(2)}) %collective-permute-start.2) | collective-permute-done | bytes 65568 | tf_op jit(solution)/shard_map/ppermute | solution.py:162
  34.9 1.8 %collective-permute-done.1 = bf16[256,128]{1,0:T(8,128)(2,1)S(1)} collective-permute-done((bf16[256,128]{1,0:T(8,128)(2,1)S(1)}, bf16[256,128]{1,0:T(8,128)(2,1)S(1)}, u32[]{:S(2)}, u32[]{:S(2)}) %collective-permute-start.1) | collective-permute-done | bytes 65568 | tf_op jit(solution)/shard_map/ppermute | solution.py:162
  36.7 1.4 collective-permute-done.3
  38.2 0.0 copy-start
  38.2 0.0 copy-start.2
  38.3 2.0 %all-to-all-done = bf16[4,2,128,128]{3,2,1,0:T(8,128)(2,1)S(1)} async-done(((bf16[4,2,128,128]{3,2,1,0:T(8,128)(2,1)}), bf16[4,2,128,128]{3,2,1,0:T(8,128)(2,1)S(1)}, u32[]{:S(2)}, u32[]{:S(2)}) %all-to-all-start) | async-done | bytes 262176 | tf_op jit(solution)/shard_map/all_to_all | solution.py:154
  40.3 1.2 broadcast_in_dim.2
  41.5 4.3 %all-to-all-start.1 = ((bf16[4,4,2,128,128]{4,3,2,1,0:T(8,128)(2,1)}), bf16[4,4,2,128,128]{4,3,2,1,0:T(8,128)(2,1)S(1)}, u32[]{:S(2)}, u32[]{:S(2)}) async-start(bf16[4,4,2,128,128]{4,3,2,1,0:T(8,128)(2,1)} %broadcast_in_dim.2), calls=%async_computation.1 | async-start | bytes 2097152 | tf_op jit(solution)/shard_map/all_to_all | solution.py:154
  45.8 4.9 %collective-permute-start.6 = (bf16[4,256,128]{2,1,0:T(8,128)(2,1)S(1)}, bf16[4,256,128]{2,1,0:T(8,128)(2,1)S(1)}, u32[]{:S(2)}, u32[]{:S(2)}) collective-permute-start(bf16[4,256,128]{2,1,0:T(8,128)(2,1)S(1)} %pad_maximum_fusion.cot0), channel_id=1, source_target_pairs={{0,384},{128,0},{256,128},{384,256},{1,385},{129,1},{257,129},{385... | collective-permute-start | bytes 786440 | tf_op jit(solution)/shard_map/ppermute | solution.py:162
  50.7 1.9 %collective-permute-start.5 = (bf16[4,256,128]{2,1,0:T(8,128)(2,1)S(1)}, bf16[4,256,128]{2,1,0:T(8,128)(2,1)S(1)}, u32[]{:S(2)}, u32[]{:S(2)}) collective-permute-start(bf16[4,256,128]{2,1,0:T(8,128)(2,1)S(1)} %pad_maximum_fusion.cot0), channel_id=1, source_target_pairs={{0,128},{128,256},{256,384},{384,0},{1,129},{129,257},{257,385},{3... | collective-permute-start | bytes 786440 | tf_op jit(solution)/shard_map/ppermute | solution.py:162
  52.6 4.1 %collective-permute-start.4 = (bf16[4,256,128]{2,1,0:T(8,128)(2,1)S(1)}, bf16[4,256,128]{2,1,0:T(8,128)(2,1)S(1)}, u32[]{:S(2)}, u32[]{:S(2)}) collective-permute-start(bf16[4,256,128]{2,1,0:T(8,128)(2,1)S(1)} %pad_maximum_fusion.cot0), channel_id=1, source_target_pairs={{0,256},{128,384},{256,0},{384,128},{1,257},{129,385},{257,1},{385... | collective-permute-start | bytes 786440 | tf_op jit(solution)/shard_map/ppermute | solution.py:162
  56.7 0.0 collective-permute-done.6.cot3
  56.7 8.6 %collective-permute-done.5.cot1 = bf16[4,256,128]{2,1,0:T(8,128)(2,1)S(1)} collective-permute-done((bf16[4,256,128]{2,1,0:T(8,128)(2,1)S(1)}, bf16[4,256,128]{2,1,0:T(8,128)(2,1)S(1)}, u32[]{:S(2)}, u32[]{:S(2)}) %collective-permute-start.5) | collective-permute-done | bytes 262176 | tf_op jit(solution)/shard_map/ppermute | solution.py:162
  65.3 0.0 collective-permute-done.4.cot2
  65.3 0.0 all-to-all-done.1.kv_ref
  65.3 0.0 copy-done
  65.3 0.0 copy-done.2
  65.3 2.0 %forward.1.mine_ref = f32[256,384]{1,0:T(8,128)S(1)} custom-call(s32[3]{0:T(128)S(1)} %pad_add_fusion.place_ref, bf16[128,128]{1,0:T(8,128)(2,1)S(1)} %copy-done.2, bf16[128,256]{1,0:T(8,128)(2,1)S(1)} %collective-permute-done.other_ref, bf16[4,4,2,128,128]{4,3,2,1,0:T(8,128)(2,1)S(1)} %all-to-all-done.1.kv_ref, bf16[128,4096]{1,0:T(8,128)(2,1)S(1)} %copy-done, ...), custom_call_target="tpu_custom_call" | custom-call | flops 402653184 | bytes 5242880 | tf_op jit(solution)/shard_map/forward/pallas_call | solution.py:214
  67.3 1.9 %collective-permute-start.7 = (f32[256,384]{1,0:T(8,128)S(1)}, f32[256,384]{1,0:T(8,128)S(1)}, u32[]{:S(2)}, u32[]{:S(2)}) collective-permute-start(f32[256,384]{1,0:T(8,128)S(1)} %forward.1.mine_ref), channel_id=1, source_target_pairs={{0,1},{1,0},{2,3},{3,2},{4,5},{5,4},{6,7},{7,6},{8,9},{9,8},{10,11... | collective-permute-start | bytes 1179656 | tf_op jit(solution)/shard_map/ppermute | solution.py:166
  69.2 1.7 %collective-permute-done.7.theirs_ref = f32[256,384]{1,0:T(8,128)S(1)} collective-permute-done((f32[256,384]{1,0:T(8,128)S(1)}, f32[256,384]{1,0:T(8,128)S(1)}, u32[]{:S(2)}, u32[]{:S(2)}) %collective-permute-start.7) | collective-permute-done | bytes 393248 | tf_op jit(solution)/shard_map/ppermute | solution.py:166
  70.9 1.0 merge.1
  72.0 0.0 copy-start.8
  72.0 0.7 copy-done.8
  72.7 0.7 copy-done.10
  73.4 3.6 %backward.1 = (f32[128,128]{1,0:T(8,128)S(1)}, f32[128,128]{1,0:T(8,128)S(1)}, bf16[4,4,3,128,128]{4,3,2,1,0:T(8,128)(2,1)}) custom-call(s32[3]{0:T(128)S(1)} %pad_add_fusion.place_ref, bf16[128,128]{1,0:T(8,128)(2,1)S(1)} %copy-done.2, bf16[128,256]{1,0:T(8,128)(2,1)S(1)} %collective-permute-done.other_ref, ...), custom_call_target="tpu_custom_call" | custom-call | flops 805306368 | bytes 6291456 | tf_op jit(solution)/shard_map/backward/pallas_call | solution.py:236
  77.0 0.0 copy-done.6
  77.0 4.7 %all-to-all-start.2 = ((bf16[4,4,3,128,128]{4,3,2,1,0:T(8,128)(2,1)}), bf16[4,4,3,128,128]{4,3,2,1,0:T(8,128)(2,1)}, u32[]{:S(2)}, u32[]{:S(2)}) async-start(bf16[4,4,3,128,128]{4,3,2,1,0:T(8,128)(2,1)} %get-tuple-element.68), calls=%async_computation.2 | async-start | bytes 3145728 | tf_op jit(solution)/shard_map/all_to_all | solution.py:154
  81.7 0.0 copy-done.11
  81.7 3.0 %collective-permute-start.8 = (bf16[4,128,256]{2,1,0:T(8,128)(2,1)S(1)}, bf16[4,128,256]{2,1,0:T(8,128)(2,1)S(1)}, u32[]{:S(2)}, u32[]{:S(2)}) collective-permute-start(bf16[4,128,256]{2,1,0:T(8,128)(2,1)S(1)} %copy-done.11), channel_id=1, source_target_pairs={{0,256},{128,384},{256,0},{384,128},{1,257},{129,385},{257,1},{385... | collective-permute-start | bytes 786440 | tf_op jit(solution)/shard_map/ppermute | solution.py:162
  84.6 0.0 copy-done.9
  84.6 2.3 %collective-permute-start.9 = (bf16[4,128,256]{2,1,0:T(8,128)(2,1)S(1)}, bf16[4,128,256]{2,1,0:T(8,128)(2,1)S(1)}, u32[]{:S(2)}, u32[]{:S(2)}) collective-permute-start(bf16[4,128,256]{2,1,0:T(8,128)(2,1)S(1)} %copy-done.9), channel_id=1, source_target_pairs={{0,128},{128,256},{256,384},{384,0},{1,129},{129,257},{257,385},{3... | collective-permute-start | bytes 786440 | tf_op jit(solution)/shard_map/ppermute | solution.py:162
  86.9 0.0 copy-done.7
  86.9 4.8 %collective-permute-start.10 = (bf16[4,128,256]{2,1,0:T(8,128)(2,1)S(1)}, bf16[4,128,256]{2,1,0:T(8,128)(2,1)S(1)}, u32[]{:S(2)}, u32[]{:S(2)}) collective-permute-start(bf16[4,128,256]{2,1,0:T(8,128)(2,1)S(1)} %copy-done.7), channel_id=1, source_target_pairs={{0,384},{128,0},{256,128},{384,256},{1,385},{129,1},{257,129},{385... | collective-permute-start | bytes 786440 | tf_op jit(solution)/shard_map/ppermute | solution.py:162
  91.7 2.5 %collective-permute-done.8 = bf16[4,128,256]{2,1,0:T(8,128)(2,1)S(1)} collective-permute-done((bf16[4,128,256]{2,1,0:T(8,128)(2,1)S(1)}, bf16[4,128,256]{2,1,0:T(8,128)(2,1)S(1)}, u32[]{:S(2)}, u32[]{:S(2)}) %collective-permute-start.8) | collective-permute-done | bytes 262176 | tf_op jit(solution)/shard_map/ppermute | solution.py:162
  94.3 4.6 %collective-permute-done.9 = bf16[4,128,256]{2,1,0:T(8,128)(2,1)S(1)} collective-permute-done((bf16[4,128,256]{2,1,0:T(8,128)(2,1)S(1)}, bf16[4,128,256]{2,1,0:T(8,128)(2,1)S(1)}, u32[]{:S(2)}, u32[]{:S(2)}) %collective-permute-start.9) | collective-permute-done | bytes 262176 | tf_op jit(solution)/shard_map/ppermute | solution.py:162
  98.9 0.0 collective-permute-done.10
  98.9 4.0 %all-to-all-done.2 = bf16[4,4,3,128,128]{4,3,2,1,0:T(8,128)(2,1)} async-done(((bf16[4,4,3,128,128]{4,3,2,1,0:T(8,128)(2,1)}), bf16[4,4,3,128,128]{4,3,2,1,0:T(8,128)(2,1)}, u32[]{:S(2)}, u32[]{:S(2)}) %all-to-all-start.2) | async-done | bytes 1572896 | tf_op jit(solution)/shard_map/all_to_all | solution.py:154
  102.9 2.3 %fusion = bf16[4,3,128,128]{3,2,1,0:T(8,128)(2,1)} fusion(bf16[4,4,3,128,128]{4,3,2,1,0:T(8,128)(2,1)} %all-to-all-done.2), kind=kLoop, calls=%fused_computation.2 | loop fusion | flops 1572864 | bytes 1966080 | tf_op jit(solution)/shard_map/add | solution.py:172
  105.2 0.1 add_convert_fusion.1
  105.3 10.3 %all-to-all-start.3 = ((bf16[4,3,128,128]{3,2,1,0:T(8,128)(2,1)}), bf16[4,3,128,128]{3,2,1,0:T(8,128)(2,1)S(1)}, u32[]{:S(2)}, u32[]{:S(2)}) async-start(bf16[4,3,128,128]{3,2,1,0:T(8,128)(2,1)} %fusion), calls=%async_computation.3 | async-start | bytes 786432 | tf_op jit(solution)/shard_map/all_to_all | solution.py:154
  115.6 1.9 %collective-permute-start.14 = (f32[128,128]{1,0:T(8,128)S(1)}, f32[128,128]{1,0:T(8,128)S(1)}, u32[]{:S(2)}, u32[]{:S(2)}) collective-permute-start(f32[128,128]{1,0:T(8,128)S(1)} %get-tuple-element.80), channel_id=1, source_target_pairs={{0,1},{1,0},{2,3},{3,2},{4,5},{5,4},{6,7},{7,6},{8,9},{9,8},{10,11... | collective-permute-start | bytes 196616 | tf_op jit(solution)/shard_map/ppermute | solution.py:166
  117.5 1.9 %collective-permute-start.11 = (bf16[128,256]{1,0:T(8,128)(2,1)S(1)}, bf16[128,256]{1,0:T(8,128)(2,1)S(1)}, u32[]{:S(2)}, u32[]{:S(2)}) collective-permute-start(bf16[128,256]{1,0:T(8,128)(2,1)S(1)} %get-tuple-element.85), channel_id=1, source_target_pairs={{0,32},{32,64},{64,96},{96,0},{1,33},{33,65},{65,97},{97,1},{2,34}... | collective-permute-start | bytes 196616 | tf_op jit(solution)/shard_map/ppermute | solution.py:162
  119.5 3.9 %collective-permute-start.13 = (bf16[128,256]{1,0:T(8,128)(2,1)S(1)}, bf16[128,256]{1,0:T(8,128)(2,1)S(1)}, u32[]{:S(2)}, u32[]{:S(2)}) collective-permute-start(bf16[128,256]{1,0:T(8,128)(2,1)S(1)} %get-tuple-element.86), channel_id=1, source_target_pairs={{0,96},{32,0},{64,32},{96,64},{1,97},{33,1},{65,33},{97,65},{2,98}... | collective-permute-start | bytes 196616 | tf_op jit(solution)/shard_map/ppermute | solution.py:162
  123.4 3.5 %collective-permute-start.12 = (bf16[128,256]{1,0:T(8,128)(2,1)S(1)}, bf16[128,256]{1,0:T(8,128)(2,1)S(1)}, u32[]{:S(2)}, u32[]{:S(2)}) collective-permute-start(bf16[128,256]{1,0:T(8,128)(2,1)S(1)} %get-tuple-element.87), channel_id=1, source_target_pairs={{0,64},{32,96},{64,0},{96,32},{1,65},{33,97},{65,1},{97,33},{2,66}... | collective-permute-start | bytes 196616 | tf_op jit(solution)/shard_map/ppermute | solution.py:162
  126.9 0.0 collective-permute-done.14
  126.9 0.6 multiply_convert_fusion
  127.5 8.1 %collective-permute-done.11 = bf16[128,256]{1,0:T(8,128)(2,1)S(1)} collective-permute-done((bf16[128,256]{1,0:T(8,128)(2,1)S(1)}, bf16[128,256]{1,0:T(8,128)(2,1)S(1)}, u32[]{:S(2)}, u32[]{:S(2)}) %collective-permute-start.11) | collective-permute-done | bytes 65568 | tf_op jit(solution)/shard_map/ppermute | solution.py:162
  135.7 0.0 collective-permute-done.13
  135.7 1.9 %collective-permute-done.12 = bf16[128,256]{1,0:T(8,128)(2,1)S(1)} collective-permute-done((bf16[128,256]{1,0:T(8,128)(2,1)S(1)}, bf16[128,256]{1,0:T(8,128)(2,1)S(1)}, u32[]{:S(2)}, u32[]{:S(2)}) %collective-permute-start.12) | collective-permute-done | bytes 65568 | tf_op jit(solution)/shard_map/ppermute | solution.py:162
  137.6 0.7 fusion.3
  138.3 5.4 %all-to-all-done.3.parts_ref = bf16[4,3,128,128]{3,2,1,0:T(8,128)(2,1)S(1)} async-done(((bf16[4,3,128,128]{3,2,1,0:T(8,128)(2,1)}), bf16[4,3,128,128]{3,2,1,0:T(8,128)(2,1)S(1)}, u32[]{:S(2)}, u32[]{:S(2)}) %all-to-all-start.3) | async-done | bytes 393248 | tf_op jit(solution)/shard_map/all_to_all | solution.py:154
  143.7 0.8 finish.1
  (13 shorter events, 0.1 us)
Async XLA Ops:
  0.7 0.8 copy-start.1
  1.5 0.8 copy-start.3
  2.3 0.8 copy-start.4
  3.1 0.8 copy-start.5
  5.1 35.1 %all-to-all-start = ((bf16[4,2,128,128]{3,2,1,0:T(8,128)(2,1)}), bf16[4,2,128,128]{3,2,1,0:T(8,128)(2,1)S(1)}, u32[]{:S(2)}, u32[]{:S(2)}) async-start(bf16[4,2,128,128]{3,2,1,0:T(8,128)(2,1)} %get-tuple-element.50), calls=%async_computation | async-start | bytes 524288 | tf_op jit(solution)/shard_map/all_to_all | solution.py:154
  19.3 3.1 %collective-permute-start = (bf16[128,256]{1,0:T(8,128)(2,1)S(1)}, bf16[128,256]{1,0:T(8,128)(2,1)S(1)}, u32[]{:S(2)}, u32[]{:S(2)}) collective-permute-start(bf16[128,256]{1,0:T(8,128)(2,1)S(1)} %get-tuple-element.49), channel_id=1, source_target_pairs={{0,1},{1,0},{2,3},{3,2},{4,5},{5,4},{6,7},{7,6},{8,9},{9,8},{10,11... | collective-permute-start | bytes 196616 | tf_op jit(solution)/shard_map/ppermute | solution.py:166
  22.5 12.4 %collective-permute-start.2 = (bf16[256,128]{1,0:T(8,128)(2,1)S(1)}, bf16[256,128]{1,0:T(8,128)(2,1)S(1)}, u32[]{:S(2)}, u32[]{:S(2)}) collective-permute-start(bf16[256,128]{1,0:T(8,128)(2,1)S(1)} %get-tuple-element.89), channel_id=1, source_target_pairs={{0,64},{32,96},{64,0},{96,32},{1,65},{33,97},{65,1},{97,33},{2,66}... | collective-permute-start | bytes 196616 | tf_op jit(solution)/shard_map/ppermute | solution.py:162
  25.9 10.9 %collective-permute-start.1 = (bf16[256,128]{1,0:T(8,128)(2,1)S(1)}, bf16[256,128]{1,0:T(8,128)(2,1)S(1)}, u32[]{:S(2)}, u32[]{:S(2)}) collective-permute-start(bf16[256,128]{1,0:T(8,128)(2,1)S(1)} %get-tuple-element.89), channel_id=1, source_target_pairs={{0,32},{32,64},{64,96},{96,0},{1,33},{33,65},{65,97},{97,1},{2,34}... | collective-permute-start | bytes 196616 | tf_op jit(solution)/shard_map/ppermute | solution.py:162
  28.8 9.4 %collective-permute-start.3 = (bf16[256,128]{1,0:T(8,128)(2,1)S(1)}, bf16[256,128]{1,0:T(8,128)(2,1)S(1)}, u32[]{:S(2)}, u32[]{:S(2)}) collective-permute-start(bf16[256,128]{1,0:T(8,128)(2,1)S(1)} %get-tuple-element.89), channel_id=1, source_target_pairs={{0,96},{32,0},{64,32},{96,64},{1,97},{33,1},{65,33},{97,65},{2,98}... | collective-permute-start | bytes 196616 | tf_op jit(solution)/shard_map/ppermute | solution.py:162
  38.2 27.1 %copy-start = (bf16[128,4096]{1,0:T(8,128)(2,1)S(1)}, bf16[128,4096]{1,0:T(8,128)(2,1)}, u32[]{:S(2)}) copy-start(bf16[128,4096]{1,0:T(8,128)(2,1)} %w_ref.3) | copy-start | bytes 3145732
  38.2 27.1 %copy-start.2 = (bf16[128,128]{1,0:T(8,128)(2,1)S(1)}, bf16[128,128]{1,0:T(8,128)(2,1)}, u32[]{:S(2)}) copy-start(bf16[128,128]{1,0:T(8,128)(2,1)} %q_ref.5) | copy-start | bytes 98308
  41.5 23.8 %all-to-all-start.1 = ((bf16[4,4,2,128,128]{4,3,2,1,0:T(8,128)(2,1)}), bf16[4,4,2,128,128]{4,3,2,1,0:T(8,128)(2,1)S(1)}, u32[]{:S(2)}, u32[]{:S(2)}) async-start(bf16[4,4,2,128,128]{4,3,2,1,0:T(8,128)(2,1)} %broadcast_in_dim.2), calls=%async_computation.1 | async-start | bytes 2097152 | tf_op jit(solution)/shard_map/all_to_all | solution.py:154
  45.8 11.0 %collective-permute-start.6 = (bf16[4,256,128]{2,1,0:T(8,128)(2,1)S(1)}, bf16[4,256,128]{2,1,0:T(8,128)(2,1)S(1)}, u32[]{:S(2)}, u32[]{:S(2)}) collective-permute-start(bf16[4,256,128]{2,1,0:T(8,128)(2,1)S(1)} %pad_maximum_fusion.cot0), channel_id=1, source_target_pairs={{0,384},{128,0},{256,128},{384,256},{1,385},{129,1},{257,129},{385... | collective-permute-start | bytes 786440 | tf_op jit(solution)/shard_map/ppermute | solution.py:162
  50.7 14.6 %collective-permute-start.5 = (bf16[4,256,128]{2,1,0:T(8,128)(2,1)S(1)}, bf16[4,256,128]{2,1,0:T(8,128)(2,1)S(1)}, u32[]{:S(2)}, u32[]{:S(2)}) collective-permute-start(bf16[4,256,128]{2,1,0:T(8,128)(2,1)S(1)} %pad_maximum_fusion.cot0), channel_id=1, source_target_pairs={{0,128},{128,256},{256,384},{384,0},{1,129},{129,257},{257,385},{3... | collective-permute-start | bytes 786440 | tf_op jit(solution)/shard_map/ppermute | solution.py:162
  52.6 12.7 %collective-permute-start.4 = (bf16[4,256,128]{2,1,0:T(8,128)(2,1)S(1)}, bf16[4,256,128]{2,1,0:T(8,128)(2,1)S(1)}, u32[]{:S(2)}, u32[]{:S(2)}) collective-permute-start(bf16[4,256,128]{2,1,0:T(8,128)(2,1)S(1)} %pad_maximum_fusion.cot0), channel_id=1, source_target_pairs={{0,256},{128,384},{256,0},{384,128},{1,257},{129,385},{257,1},{385... | collective-permute-start | bytes 786440 | tf_op jit(solution)/shard_map/ppermute | solution.py:162
  67.3 3.6 %collective-permute-start.7 = (f32[256,384]{1,0:T(8,128)S(1)}, f32[256,384]{1,0:T(8,128)S(1)}, u32[]{:S(2)}, u32[]{:S(2)}) collective-permute-start(f32[256,384]{1,0:T(8,128)S(1)} %forward.1.mine_ref), channel_id=1, source_target_pairs={{0,1},{1,0},{2,3},{3,2},{4,5},{5,4},{6,7},{7,6},{8,9},{9,8},{10,11... | collective-permute-start | bytes 1179656 | tf_op jit(solution)/shard_map/ppermute | solution.py:166
  72.0 0.7 copy-start.8
  72.7 0.7 copy-start.10
  73.4 3.6 %copy-start.6 = (bf16[4,128,256]{2,1,0:T(8,128)(2,1)}, bf16[4,128,256]{2,1,0:T(8,128)(2,1)S(1)}, u32[]{:S(2)}) copy-start(bf16[4,128,256]{2,1,0:T(8,128)(2,1)S(1)} %get-tuple-element.72) | copy-start | bytes 786436
  77.0 4.7 %copy-start.11 = (bf16[4,128,256]{2,1,0:T(8,128)(2,1)S(1)}, bf16[4,128,256]{2,1,0:T(8,128)(2,1)}, u32[]{:S(2)}) copy-start(bf16[4,128,256]{2,1,0:T(8,128)(2,1)} %copy-done.10) | copy-start | bytes 786436
  77.0 7.6 %copy-start.9 = (bf16[4,128,256]{2,1,0:T(8,128)(2,1)S(1)}, bf16[4,128,256]{2,1,0:T(8,128)(2,1)}, u32[]{:S(2)}) copy-start(bf16[4,128,256]{2,1,0:T(8,128)(2,1)} %copy-done.8) | copy-start | bytes 786436
  77.0 9.9 %copy-start.7 = (bf16[4,128,256]{2,1,0:T(8,128)(2,1)S(1)}, bf16[4,128,256]{2,1,0:T(8,128)(2,1)}, u32[]{:S(2)}) copy-start(bf16[4,128,256]{2,1,0:T(8,128)(2,1)} %copy-done.6) | copy-start | bytes 786436
  77.0 25.9 %all-to-all-start.2 = ((bf16[4,4,3,128,128]{4,3,2,1,0:T(8,128)(2,1)}), bf16[4,4,3,128,128]{4,3,2,1,0:T(8,128)(2,1)}, u32[]{:S(2)}, u32[]{:S(2)}) async-start(bf16[4,4,3,128,128]{4,3,2,1,0:T(8,128)(2,1)} %get-tuple-element.68), calls=%async_computation.2 | async-start | bytes 3145728 | tf_op jit(solution)/shard_map/all_to_all | solution.py:154
  81.7 12.6 %collective-permute-start.8 = (bf16[4,128,256]{2,1,0:T(8,128)(2,1)S(1)}, bf16[4,128,256]{2,1,0:T(8,128)(2,1)S(1)}, u32[]{:S(2)}, u32[]{:S(2)}) collective-permute-start(bf16[4,128,256]{2,1,0:T(8,128)(2,1)S(1)} %copy-done.11), channel_id=1, source_target_pairs={{0,256},{128,384},{256,0},{384,128},{1,257},{129,385},{257,1},{385... | collective-permute-start | bytes 786440 | tf_op jit(solution)/shard_map/ppermute | solution.py:162
  84.6 14.2 %collective-permute-start.9 = (bf16[4,128,256]{2,1,0:T(8,128)(2,1)S(1)}, bf16[4,128,256]{2,1,0:T(8,128)(2,1)S(1)}, u32[]{:S(2)}, u32[]{:S(2)}) collective-permute-start(bf16[4,128,256]{2,1,0:T(8,128)(2,1)S(1)} %copy-done.9), channel_id=1, source_target_pairs={{0,128},{128,256},{256,384},{384,0},{1,129},{129,257},{257,385},{3... | collective-permute-start | bytes 786440 | tf_op jit(solution)/shard_map/ppermute | solution.py:162
  86.9 11.9 %collective-permute-start.10 = (bf16[4,128,256]{2,1,0:T(8,128)(2,1)S(1)}, bf16[4,128,256]{2,1,0:T(8,128)(2,1)S(1)}, u32[]{:S(2)}, u32[]{:S(2)}) collective-permute-start(bf16[4,128,256]{2,1,0:T(8,128)(2,1)S(1)} %copy-done.7), channel_id=1, source_target_pairs={{0,384},{128,0},{256,128},{384,256},{1,385},{129,1},{257,129},{385... | collective-permute-start | bytes 786440 | tf_op jit(solution)/shard_map/ppermute | solution.py:162
  105.3 38.4 %all-to-all-start.3 = ((bf16[4,3,128,128]{3,2,1,0:T(8,128)(2,1)}), bf16[4,3,128,128]{3,2,1,0:T(8,128)(2,1)S(1)}, u32[]{:S(2)}, u32[]{:S(2)}) async-start(bf16[4,3,128,128]{3,2,1,0:T(8,128)(2,1)} %fusion), calls=%async_computation.3 | async-start | bytes 786432 | tf_op jit(solution)/shard_map/all_to_all | solution.py:154
  115.6 11.3 %collective-permute-start.14 = (f32[128,128]{1,0:T(8,128)S(1)}, f32[128,128]{1,0:T(8,128)S(1)}, u32[]{:S(2)}, u32[]{:S(2)}) collective-permute-start(f32[128,128]{1,0:T(8,128)S(1)} %get-tuple-element.80), channel_id=1, source_target_pairs={{0,1},{1,0},{2,3},{3,2},{4,5},{5,4},{6,7},{7,6},{8,9},{9,8},{10,11... | collective-permute-start | bytes 196616 | tf_op jit(solution)/shard_map/ppermute | solution.py:166
  117.5 18.2 %collective-permute-start.11 = (bf16[128,256]{1,0:T(8,128)(2,1)S(1)}, bf16[128,256]{1,0:T(8,128)(2,1)S(1)}, u32[]{:S(2)}, u32[]{:S(2)}) collective-permute-start(bf16[128,256]{1,0:T(8,128)(2,1)S(1)} %get-tuple-element.85), channel_id=1, source_target_pairs={{0,32},{32,64},{64,96},{96,0},{1,33},{33,65},{65,97},{97,1},{2,34}... | collective-permute-start | bytes 196616 | tf_op jit(solution)/shard_map/ppermute | solution.py:162
  119.5 16.2 %collective-permute-start.13 = (bf16[128,256]{1,0:T(8,128)(2,1)S(1)}, bf16[128,256]{1,0:T(8,128)(2,1)S(1)}, u32[]{:S(2)}, u32[]{:S(2)}) collective-permute-start(bf16[128,256]{1,0:T(8,128)(2,1)S(1)} %get-tuple-element.86), channel_id=1, source_target_pairs={{0,96},{32,0},{64,32},{96,64},{1,97},{33,1},{65,33},{97,65},{2,98}... | collective-permute-start | bytes 196616 | tf_op jit(solution)/shard_map/ppermute | solution.py:162
  123.4 14.2 %collective-permute-start.12 = (bf16[128,256]{1,0:T(8,128)(2,1)S(1)}, bf16[128,256]{1,0:T(8,128)(2,1)S(1)}, u32[]{:S(2)}, u32[]{:S(2)}) collective-permute-start(bf16[128,256]{1,0:T(8,128)(2,1)S(1)} %get-tuple-element.87), channel_id=1, source_target_pairs={{0,64},{32,96},{64,0},{96,32},{1,65},{33,97},{65,1},{97,33},{2,66}... | collective-permute-start | bytes 196616 | tf_op jit(solution)/shard_map/ppermute | solution.py:162

commit v3 on v2

v3 whole, which is shorter than its diff:
```python
import jax
import jax.numpy as jnp
from jax import lax
from jax.experimental import pallas as pl
from jax.experimental.pallas import tpu as pltpu
from jax.sharding import Mesh, PartitionSpec as P

HDIM = 128
BLK = 128
WIDTH = 4 * BLK
SCALE = HDIM ** (-0.5)
F32 = jnp.float32
BF16 = jnp.bfloat16
VMEM = pl.BlockSpec(memory_space=pltpu.VMEM)
SMEM = pl.BlockSpec(memory_space=pltpu.SMEM)
shape = jax.ShapeDtypeStruct


def dot(a, b, dims=((1,), (0,))):
    return lax.dot_general(a, b, (dims, ((), ())), preferred_element_type=F32)


def project_kernel(place_ref, attn_ref, w_ref, *out_refs):
    for r, out_ref in enumerate(out_refs):
        for t in range(4):
            o = lax.bitwise_xor(place_ref[2], r) * 4 + lax.bitwise_xor(place_ref[3], t)
            cols = pl.ds(pl.multiple_of(o * 256, 256), 256)
            out_ref[t] = dot(attn_ref[...], w_ref[:, cols]).astype(BF16)


def forward_kernel(place_ref, q_ref, other_ref, kv0, kv1, kv2, kv3, w_ref, cot_ref, part_ref, s_ref):
    pieces = (kv0, kv1, kv2, kv3)
    grad = jnp.zeros((2 * BLK, HDIM), F32)
    for o in range(16):
        start = pl.multiple_of(o * 256 + place_ref[0] * BLK, BLK)
        grad = grad + dot(cot_ref[o], w_ref[:, pl.ds(start, BLK)], ((1,), (1,)))
    part_ref[:, :HDIM] = grad
    q = jnp.concatenate([q_ref[...], other_ref[0]], axis=0)
    top = jnp.full((2 * BLK, BLK), -jnp.inf, F32)
    for j in range(4):
        k = pieces[j][:, 0].reshape(WIDTH, HDIM)
        s = dot(q, k, ((1,), (1,))) * SCALE
        s_ref[:, j * WIDTH : (j + 1) * WIDTH] = s
        for t in range(4):
            top = jnp.maximum(top, s[:, t * BLK : (t + 1) * BLK])
    row_max = jnp.max(top, axis=1, keepdims=True)
    sums = jnp.zeros((2 * BLK, BLK), F32)
    acc = jnp.zeros((2 * BLK, HDIM), F32)
    for j in range(4):
        p = jnp.exp(s_ref[:, j * WIDTH : (j + 1) * WIDTH] - row_max)
        for t in range(4):
            sums = sums + p[:, t * BLK : (t + 1) * BLK]
        v = pieces[j][:, 1].reshape(WIDTH, HDIM)
        acc = acc + dot(p.astype(BF16), v)
    totals = jnp.sum(sums, axis=1, keepdims=True)
    part_ref[:, HDIM : 2 * HDIM] = acc / totals
    part_ref[:, 2 * HDIM :] = jnp.broadcast_to(row_max + jnp.log(totals), (2 * BLK, BLK))


def merged(mine_ref, theirs_ref, half):
    rows = slice(half * BLK, (half + 1) * BLK)
    swapped = slice((1 - half) * BLK, (2 - half) * BLK)
    grad = (mine_ref[rows, :HDIM] + theirs_ref[swapped, :HDIM]).astype(BF16)
    a, b = mine_ref[rows, 2 * HDIM :], theirs_ref[swapped, 2 * HDIM :]
    top = jnp.maximum(a, b)
    lse = top + jnp.log(jnp.exp(a - top) + jnp.exp(b - top))
    attn = mine_ref[rows, HDIM : 2 * HDIM] * jnp.exp(a - lse)
    attn = (attn + theirs_ref[swapped, HDIM : 2 * HDIM] * jnp.exp(b - lse)).astype(BF16)
    dots = jnp.sum(grad.astype(F32) * attn.astype(F32), axis=1, keepdims=True)
    return grad, attn, lse[:, :1], dots


def backward_kernel(place_ref, q_ref, other_ref, kv0, kv1, kv2, kv3, cot_ref, mine_ref, theirs_ref, *refs):
    pieces = (kv0, kv1, kv2, kv3)
    dq_ref, pay_ref, attn_ref = refs
    halves = [merged(mine_ref, theirs_ref, half) for half in range(2)]
    grad, attn, lse, dots = (jnp.concatenate(pair, axis=0) for pair in zip(*halves))
    attn_ref[...] = halves[0][1]
    q = jnp.concatenate([q_ref[...], other_ref[0]], axis=0)
    q_t = q.T
    grad_t = grad.T
    attn_t = attn.T
    dq = jnp.zeros((2 * BLK, HDIM), F32)
    for j in range(4):
        k = pieces[j][:, 0].reshape(WIDTH, HDIM)
        v = pieces[j][:, 1].reshape(WIDTH, HDIM)
        s = dot(q, k, ((1,), (1,))) * SCALE
        p = jnp.exp(s - lse)
        dp = dot(grad, v, ((1,), (1,)))
        ds = (p * (dp - dots)).astype(BF16)
        dq = dq + dot(ds, k)
        dk_t = dot(q_t, ds).astype(BF16)
        dv_t = dot(grad_t, p.astype(BF16)).astype(BF16)
        x = lax.bitwise_xor(place_ref[1], j)
        for z in range(4):
            pay_ref[x, z, 0] = dk_t[:, z * BLK : (z + 1) * BLK]
            pay_ref[x, z, 1] = dv_t[:, z * BLK : (z + 1) * BLK]
    dq_ref[0] = dq[:BLK]
    dq_ref[1] = dq[BLK:]
    for x in range(4):
        for z in range(4):
            pay_ref[x, z, 2] = dot(attn_t, cot_ref[z * 4 + x]).astype(BF16)


def finish_kernel(parts_ref, dk_ref, dv_ref, dw_ref):
    total = jnp.sum(parts_ref[...].astype(F32), axis=0)
    dk_ref[...] = (total[0] * SCALE).T.astype(BF16)
    dv_ref[...] = total[1].T.astype(BF16)
    dw_ref[...] = total[2]


def exchange(blocks, axis):
    return lax.all_to_all(blocks, axis, 0, 0, tiled=True)


def trade(block, axis, step):
    return lax.ppermute(block, axis, [(i, i ^ step) for i in range(2 if axis == "c" else 4)])


def add_all(blocks):
    total = blocks[0].astype(F32)
    for block in blocks[1:]:
        total = total + block.astype(F32)
    return total


def call(kernel, name, out_shape, in_specs, limit, flops, nbytes, exps=0, scratch=()):
    return pl.pallas_call(
        kernel,
        out_shape=out_shape,
        in_specs=in_specs,
        out_specs=jax.tree.map(lambda _: VMEM, out_shape),
        scratch_shapes=scratch,
        compiler_params=pltpu.CompilerParams(vmem_limit_bytes=limit << 20),
        cost_estimate=pl.CostEstimate(flops=flops, bytes_accessed=nbytes, transcendentals=exps),
        name=name,
    )


def body(queries, keys, values, w_out, grad_out):
    unit = BLK * BLK * 4096
    tile = shape((BLK, BLK), BF16)
    place = jnp.stack([lax.axis_index(a) for a in ("c", "x", "y", "zl")]).astype(jnp.int32)
    place, keys = lax.optimization_barrier((place, keys))
    first = place[0] == 0
    left, right = grad_out[:, :BLK], grad_out[:, BLK:]
    other = trade(jnp.stack([queries, jnp.where(first, right, left)]), "c", 1)
    cot = jnp.concatenate([jnp.where(first, left, right), other[1]], axis=0)
    kv = lax.all_gather(jnp.concatenate([keys, values]), "zh", axis=0, tiled=True)
    kv = kv.reshape(4, 2, BLK, HDIM)
    kv, cot = lax.optimization_barrier((kv, cot))
    cot = exchange(jnp.broadcast_to(cot[None], (16, 2 * BLK, BLK)), ("y", "zl"))
    pieces = [kv] + [trade(kv, "x", r) for r in (1, 2, 3)]
    cot, pieces = lax.optimization_barrier((cot, pieces))
    part = call(
        forward_kernel,
        "forward",
        shape((2 * BLK, 3 * BLK), F32),
        [SMEM] + [VMEM] * 8,
        8,
        6 * unit,
        5 << 20,
        unit // BLK,
        [pltpu.VMEM((2 * BLK, 16 * BLK), F32)],
    )(place, queries, other, *pieces, w_out, cot)
    theirs = trade(part, "c", 1)
    dq, pay, attn = call(
        backward_kernel,
        "backward",
        (shape((2, BLK, HDIM), F32), shape((4, 4, 3, BLK, BLK), BF16), tile),
        [SMEM] + [VMEM] * 9,
        8,
        12 * unit,
        7 << 20,
        unit // BLK,
    )(place, queries, other, *pieces, cot, part, theirs)
    dq, pay, attn = lax.optimization_barrier((dq, pay, attn))
    pay = exchange(pay, "x")
    dq_got = trade(dq[1], "c", 1)
    attn, dq_got = lax.optimization_barrier((attn, dq_got))
    quarter = shape((4, BLK, 256), BF16)
    outs = call(
        project_kernel, "project", (quarter,) * 4, [SMEM] + [VMEM] * 2, 8, 2 * unit, 2 << 20
    )(place, attn, w_out)
    outs = [outs[0]] + [trade(outs[r], "y", r) for r in (1, 2, 3)]
    pay = add_all([pay[r] for r in range(4)]).astype(BF16)
    out = add_all(outs).astype(BF16)
    pay = exchange(pay, "zh")
    out = add_all([out[0]] + [trade(out[t], "zl", t) for t in (1, 2, 3)]).astype(BF16)
    dq = ((dq[0] + dq_got) * SCALE).astype(BF16)
    dk, dv, dw = call(
        finish_kernel, "finish", (tile, tile, shape((BLK, BLK), F32)), [VMEM], 4, 0, 1 << 20
    )(pay)
    return out, dq, dk, dv, dw


def solution(mesh):
    fine = Mesh(mesh.devices.reshape(4, 4, 4, 4, 2), ("y", "zl", "zh", "x", "c"))
    outer, inner = ("y", "zl"), ("zh", "x", "c")
    spread = P(inner, outer)
    return jax.shard_map(
        body,
        mesh=fine,
        in_specs=(spread, spread, spread, P(outer, None), spread),
        out_specs=(spread, spread, spread, spread, P(outer, inner)),
        check_vma=False,
    )
```

time: 146 us -> 136 us (0.932)
  the two profiles are of different devices: /device:TPU:32 before, /device:TPU:8 now
where the time goes in v3:
time: 136 us; the launch traced here: 135 us
  starting transfers between devices  52.4 us (39%)
  waiting for transfers between devices  39.6 us (29%)
  blocking collectives  27.6 us (20%)
  Pallas kernels  6.39 us (5%)
  other arithmetic  6.2 us (5%)
  local copies, waits for them, and re-layouts  2.38 us (2%)
    ppermute x12, starting transfers between devices, trade(): lax.ppermute(block, axis, [(i, i ^ step) for i in range(2 if axis == 'c'...  34.8 us
    all_gather x1, blocking collectives, body(): lax.all_gather(jnp.concatenate([keys, values]), 'zh', axis=0, tiled=True)  27.6 us
    ppermute x12, waiting for transfers between devices, trade(): lax.ppermute(block, axis, [(i, i ^ step) for i in range(2 if axis == 'c'...  22.2 us
    all_to_all x3, starting transfers between devices, exchange(): return lax.all_to_all(blocks, axis, 0, 0, tiled=True)  17.6 us
    all_to_all x3, waiting for transfers between devices, exchange(): return lax.all_to_all(blocks, axis, 0, 0, tiled=True)  17.4 us
  transfers between devices with their start and end apart: 15, of which 11 were waited for; matrix products, arithmetic and copies ran while one was open for 3% of the time, Pallas kernels for 1%

profile of v3, /device:TPU:8, one launch (start us, length us, event | category | flops | bytes accessed | tf_op | source)
XLA Modules:
  0.0 135.5 jit_solution(6494950919414709326)
XLA Ops:
  0.6 0.1 pad_add_fusion.place_ref
  0.8 0.8 broadcast_select_fusion
  1.5 0.8 pad_maximum_fusion
  2.3 1.9 %collective-permute-start = (bf16[2,128,128]{2,1,0:T(8,128)(2,1)S(1)}, bf16[2,128,128]{2,1,0:T(8,128)(2,1)S(1)}, u32[]{:S(2)}, u32[]{:S(2)}) collective-permute-start(bf16[2,128,128]{2,1,0:T(8,128)(2,1)S(1)} %pad_maximum_fusion), channel_id=1, source_target_pairs={{0,1},{1,0},{2,3},{3,2},{4,5},{5,4},{6,7},{7,6},{8,9},{9,8},{10,11... | collective-permute-start | bytes 196616 | tf_op jit(solution)/shard_map/ppermute | solution.py:117
  4.2 0.8 pad_maximum_fusion.1
  5.0 27.6 %all_gather.3 = bf16[1024,128]{1,0:T(8,128)(2,1)S(1)} all-gather(bf16[256,128]{1,0:T(8,128)(2,1)S(1)} %pad_maximum_fusion.1), channel_id=1, replica_groups=mesh['y'=4,'zl'=4,'zh'=4,'x'=4,'c'=2] {'zh'}, dimensions={0}, use_global_device_ids=true | all-gather | bytes 327680 | tf_op jit(solution)/shard_map/all_gather | solution.py:149
  32.6 0.0 collective-permute-done.other_ref
  32.7 0.0 copy-start
  32.7 0.0 copy-start.2
  32.7 1.2 broadcast_in_dim.2
  33.9 6.6 %all-to-all-start = ((bf16[16,256,128]{2,1,0:T(8,128)(2,1)}), bf16[16,256,128]{2,1,0:T(8,128)(2,1)S(1)}, u32[]{:S(2)}, u32[]{:S(2)}) async-start(bf16[16,256,128]{2,1,0:T(8,128)(2,1)} %broadcast_in_dim.2), calls=%async_computation | async-start | bytes 2097152 | tf_op jit(solution)/shard_map/all_to_all | solution.py:113
  40.5 4.7 %collective-permute-start.3 = (bf16[4,2,128,128]{3,2,1,0:T(8,128)(2,1)S(1)}, bf16[4,2,128,128]{3,2,1,0:T(8,128)(2,1)S(1)}, u32[]{:S(2)}, u32[]{:S(2)}) collective-permute-start(bf16[4,2,128,128]{3,2,1,0:T(8,128)(2,1)S(1)} %bitcast.33), channel_id=1, source_target_pairs={{0,6},{2,4},{4,2},{6,0},{1,7},{3,5},{5,3},{7,1},{8,14},{10,12},{12... | collective-permute-start | bytes 786440 | tf_op jit(solution)/shard_map/ppermute | solution.py:117
  45.1 2.7 %collective-permute-start.2 = (bf16[4,2,128,128]{3,2,1,0:T(8,128)(2,1)S(1)}, bf16[4,2,128,128]{3,2,1,0:T(8,128)(2,1)S(1)}, u32[]{:S(2)}, u32[]{:S(2)}) collective-permute-start(bf16[4,2,128,128]{3,2,1,0:T(8,128)(2,1)S(1)} %bitcast.34), channel_id=1, source_target_pairs={{0,4},{2,6},{4,0},{6,2},{1,5},{3,7},{5,1},{7,3},{8,12},{10,14},{12... | collective-permute-start | bytes 786440 | tf_op jit(solution)/shard_map/ppermute | solution.py:117
  47.9 2.4 %collective-permute-start.1 = (bf16[4,2,128,128]{3,2,1,0:T(8,128)(2,1)S(1)}, bf16[4,2,128,128]{3,2,1,0:T(8,128)(2,1)S(1)}, u32[]{:S(2)}, u32[]{:S(2)}) collective-permute-start(bf16[4,2,128,128]{3,2,1,0:T(8,128)(2,1)S(1)} %bitcast.35), channel_id=1, source_target_pairs={{0,2},{2,0},{4,6},{6,4},{1,3},{3,1},{5,7},{7,5},{8,10},{10,8},{12,... | collective-permute-start | bytes 786440 | tf_op jit(solution)/shard_map/ppermute | solution.py:117
  50.3 3.0 %collective-permute-done.3.kv3 = bf16[4,2,128,128]{3,2,1,0:T(8,128)(2,1)S(1)} collective-permute-done((bf16[4,2,128,128]{3,2,1,0:T(8,128)(2,1)S(1)}, bf16[4,2,128,128]{3,2,1,0:T(8,128)(2,1)S(1)}, u32[]{:S(2)}, u32[]{:S(2)}) %collective-permute-start.3) | collective-permute-done | bytes 262176 | tf_op jit(solution)/shard_map/ppermute | solution.py:117
  53.3 2.6 %collective-permute-done.2.kv2 = bf16[4,2,128,128]{3,2,1,0:T(8,128)(2,1)S(1)} collective-permute-done((bf16[4,2,128,128]{3,2,1,0:T(8,128)(2,1)S(1)}, bf16[4,2,128,128]{3,2,1,0:T(8,128)(2,1)S(1)}, u32[]{:S(2)}, u32[]{:S(2)}) %collective-permute-start.2) | collective-permute-done | bytes 262176 | tf_op jit(solution)/shard_map/ppermute | solution.py:117
  56.0 0.9 collective-permute-done.1.kv1
  56.9 6.2 %all-to-all-done.cot_ref = bf16[16,256,128]{2,1,0:T(8,128)(2,1)S(1)} async-done(((bf16[16,256,128]{2,1,0:T(8,128)(2,1)}), bf16[16,256,128]{2,1,0:T(8,128)(2,1)S(1)}, u32[]{:S(2)}, u32[]{:S(2)}) %all-to-all-start) | async-done | bytes 1048608 | tf_op jit(solution)/shard_map/all_to_all | solution.py:113
  63.0 0.0 copy-done
  63.0 0.0 copy-done.2
  63.0 2.0 %forward.1.mine_ref = f32[256,384]{1,0:T(8,128)S(1)} custom-call(s32[4]{0:T(128)S(1)} %pad_add_fusion.place_ref, bf16[128,128]{1,0:T(8,128)(2,1)S(1)} %copy-done.2, bf16[2,128,128]{2,1,0:T(8,128)(2,1)S(1)} %collective-permute-done.other_ref, bf16[4,2,128,128]{3,2,1,0:T(8,128)(2,1)S(1)} %bitcast.36, bf16[4,2,128,128]{3,2,1,0:T(8,128)(2,1)S(1)} %collective-permute-done.1.kv1, ...), custom_call_target="tpu_custom_call" | custom-call | flops 402653184 | bytes 5242880 | tf_op jit(solution)/shard_map/forward/pallas_call | solution.py:155
  65.0 1.9 %collective-permute-start.4 = (f32[256,384]{1,0:T(8,128)S(1)}, f32[256,384]{1,0:T(8,128)S(1)}, u32[]{:S(2)}, u32[]{:S(2)}) collective-permute-start(f32[256,384]{1,0:T(8,128)S(1)} %forward.1.mine_ref), channel_id=1, source_target_pairs={{0,1},{1,0},{2,3},{3,2},{4,5},{5,4},{6,7},{7,6},{8,9},{9,8},{10,11... | collective-permute-start | bytes 1179656 | tf_op jit(solution)/shard_map/ppermute | solution.py:117
  67.0 1.7 %collective-permute-done.4.theirs_ref = f32[256,384]{1,0:T(8,128)S(1)} collective-permute-done((f32[256,384]{1,0:T(8,128)S(1)}, f32[256,384]{1,0:T(8,128)S(1)}, u32[]{:S(2)}, u32[]{:S(2)}) %collective-permute-start.4) | collective-permute-done | bytes 393248 | tf_op jit(solution)/shard_map/ppermute | solution.py:117
  68.7 2.7 %backward.1 = (f32[2,128,128]{2,1,0:T(8,128)S(1)}, bf16[4,4,3,128,128]{4,3,2,1,0:T(8,128)(2,1)S(1)}, bf16[128,128]{1,0:T(8,128)(2,1)S(1)}) custom-call(s32[4]{0:T(128)S(1)} %pad_add_fusion.place_ref, bf16[128,128]{1,0:T(8,128)(2,1)S(1)} %copy-done.2, bf16[2,128,128]{2,1,0:T(8,128)(2,1)S(1)} %collective-permute-done.other_ref, ...), custom_call_target="tpu_custom_call" | custom-call | flops 805306368 | bytes 7340032 | tf_op jit(solution)/shard_map/backward/pallas_call | solution.py:167
  71.3 0.0 copy-start.1
  71.3 1.1 copy-done.1
  72.5 4.3 %all-to-all-start.1 = ((bf16[4,4,3,128,128]{4,3,2,1,0:T(8,128)(2,1)}), bf16[4,4,3,128,128]{4,3,2,1,0:T(8,128)(2,1)}, u32[]{:S(2)}, u32[]{:S(2)}) async-start(bf16[4,4,3,128,128]{4,3,2,1,0:T(8,128)(2,1)} %copy-done.1), calls=%async_computation.1 | async-start | bytes 3145728 | tf_op jit(solution)/shard_map/all_to_all | solution.py:113
  76.8 2.0 %collective-permute-start.5 = (f32[128,128]{1,0:T(8,128)S(1)}, f32[128,128]{1,0:T(8,128)S(1)}, u32[]{:S(2)}, u32[]{:S(2)}) collective-permute-start(f32[128,128]{1,0:T(8,128)S(1)} %slice_bitcast_fusion.4), channel_id=1, source_target_pairs={{0,1},{1,0},{2,3},{3,2},{4,5},{5,4},{6,7},{7,6},{8,9},{9,8},{10,11... | collective-permute-start | bytes 196616 | tf_op jit(solution)/shard_map/ppermute | solution.py:117
  78.9 1.1 collective-permute-done.5
  80.0 1.0 project.1
  81.0 4.6 %collective-permute-start.6 = (bf16[4,128,256]{2,1,0:T(8,128)(2,1)S(1)}, bf16[4,128,256]{2,1,0:T(8,128)(2,1)S(1)}, u32[]{:S(2)}, u32[]{:S(2)}) collective-permute-start(bf16[4,128,256]{2,1,0:T(8,128)(2,1)S(1)} %get-tuple-element.39), channel_id=1, source_target_pairs={{0,128},{128,0},{256,384},{384,256},{1,129},{129,1},{257,385},{385... | collective-permute-start | bytes 786440 | tf_op jit(solution)/shard_map/ppermute | solution.py:117
  85.5 2.2 %collective-permute-start.7 = (bf16[4,128,256]{2,1,0:T(8,128)(2,1)S(1)}, bf16[4,128,256]{2,1,0:T(8,128)(2,1)S(1)}, u32[]{:S(2)}, u32[]{:S(2)}) collective-permute-start(bf16[4,128,256]{2,1,0:T(8,128)(2,1)S(1)} %get-tuple-element.40), channel_id=1, source_target_pairs={{0,256},{128,384},{256,0},{384,128},{1,257},{129,385},{257,1},{385... | collective-permute-start | bytes 786440 | tf_op jit(solution)/shard_map/ppermute | solution.py:117
  87.7 3.1 %collective-permute-start.8 = (bf16[4,128,256]{2,1,0:T(8,128)(2,1)S(1)}, bf16[4,128,256]{2,1,0:T(8,128)(2,1)S(1)}, u32[]{:S(2)}, u32[]{:S(2)}) collective-permute-start(bf16[4,128,256]{2,1,0:T(8,128)(2,1)S(1)} %get-tuple-element.41), channel_id=1, source_target_pairs={{0,384},{128,256},{256,128},{384,0},{1,385},{129,257},{257,129},{3... | collective-permute-start | bytes 786440 | tf_op jit(solution)/shard_map/ppermute | solution.py:117
  90.9 7.3 %all-to-all-done.1 = bf16[4,4,3,128,128]{4,3,2,1,0:T(8,128)(2,1)} async-done(((bf16[4,4,3,128,128]{4,3,2,1,0:T(8,128)(2,1)}), bf16[4,4,3,128,128]{4,3,2,1,0:T(8,128)(2,1)}, u32[]{:S(2)}, u32[]{:S(2)}) %all-to-all-start.1) | async-done | bytes 1572896 | tf_op jit(solution)/shard_map/all_to_all | solution.py:113
  98.2 2.4 %fusion = bf16[4,3,128,128]{3,2,1,0:T(8,128)(2,1)} fusion(bf16[4,4,3,128,128]{4,3,2,1,0:T(8,128)(2,1)} %all-to-all-done.1), kind=kLoop, calls=%fused_computation.2 | loop fusion | flops 1572864 | bytes 1966080 | tf_op jit(solution)/shard_map/add | solution.py:123
  100.5 6.7 %all-to-all-start.2 = ((bf16[4,3,128,128]{3,2,1,0:T(8,128)(2,1)}), bf16[4,3,128,128]{3,2,1,0:T(8,128)(2,1)S(1)}, u32[]{:S(2)}, u32[]{:S(2)}) async-start(bf16[4,3,128,128]{3,2,1,0:T(8,128)(2,1)} %fusion), calls=%async_computation.2 | async-start | bytes 786432 | tf_op jit(solution)/shard_map/all_to_all | solution.py:113
  107.2 0.0 collective-permute-done.6
  107.2 0.0 collective-permute-done.7
  107.3 0.0 collective-permute-done.8
  107.3 0.1 add_convert_fusion.1
  107.4 1.9 %collective-permute-start.9 = (bf16[128,256]{1,0:T(8,128)(2,1)S(1)}, bf16[128,256]{1,0:T(8,128)(2,1)S(1)}, u32[]{:S(2)}, u32[]{:S(2)}) collective-permute-start(bf16[128,256]{1,0:T(8,128)(2,1)S(1)} %get-tuple-element.47), channel_id=1, source_target_pairs={{0,32},{32,0},{64,96},{96,64},{1,33},{33,1},{65,97},{97,65},{2,34}... | collective-permute-start | bytes 196616 | tf_op jit(solution)/shard_map/ppermute | solution.py:117
  109.4 4.2 %collective-permute-start.11 = (bf16[128,256]{1,0:T(8,128)(2,1)S(1)}, bf16[128,256]{1,0:T(8,128)(2,1)S(1)}, u32[]{:S(2)}, u32[]{:S(2)}) collective-permute-start(bf16[128,256]{1,0:T(8,128)(2,1)S(1)} %get-tuple-element.48), channel_id=1, source_target_pairs={{0,96},{32,64},{64,32},{96,0},{1,97},{33,65},{65,33},{97,1},{2,98}... | collective-permute-start | bytes 196616 | tf_op jit(solution)/shard_map/ppermute | solution.py:117
  113.6 3.1 %collective-permute-start.10 = (bf16[128,256]{1,0:T(8,128)(2,1)S(1)}, bf16[128,256]{1,0:T(8,128)(2,1)S(1)}, u32[]{:S(2)}, u32[]{:S(2)}) collective-permute-start(bf16[128,256]{1,0:T(8,128)(2,1)S(1)} %get-tuple-element.49), channel_id=1, source_target_pairs={{0,64},{32,96},{64,0},{96,32},{1,65},{33,97},{65,1},{97,33},{2,66}... | collective-permute-start | bytes 196616 | tf_op jit(solution)/shard_map/ppermute | solution.py:117
  116.7 0.6 fusion.5
  117.3 8.8 %collective-permute-done.9 = bf16[128,256]{1,0:T(8,128)(2,1)S(1)} collective-permute-done((bf16[128,256]{1,0:T(8,128)(2,1)S(1)}, bf16[128,256]{1,0:T(8,128)(2,1)S(1)}, u32[]{:S(2)}, u32[]{:S(2)}) %collective-permute-start.9) | collective-permute-done | bytes 65568 | tf_op jit(solution)/shard_map/ppermute | solution.py:117
  126.1 2.2 %collective-permute-done.11 = bf16[128,256]{1,0:T(8,128)(2,1)S(1)} collective-permute-done((bf16[128,256]{1,0:T(8,128)(2,1)S(1)}, bf16[128,256]{1,0:T(8,128)(2,1)S(1)}, u32[]{:S(2)}, u32[]{:S(2)}) %collective-permute-start.11) | collective-permute-done | bytes 65568 | tf_op jit(solution)/shard_map/ppermute | solution.py:117
  128.3 1.8 %collective-permute-done.10 = bf16[128,256]{1,0:T(8,128)(2,1)S(1)} collective-permute-done((bf16[128,256]{1,0:T(8,128)(2,1)S(1)}, bf16[128,256]{1,0:T(8,128)(2,1)S(1)}, u32[]{:S(2)}, u32[]{:S(2)}) %collective-permute-start.10) | collective-permute-done | bytes 65568 | tf_op jit(solution)/shard_map/ppermute | solution.py:117
  130.1 0.7 fusion.3
  130.8 3.9 %all-to-all-done.2.parts_ref = bf16[4,3,128,128]{3,2,1,0:T(8,128)(2,1)S(1)} async-done(((bf16[4,3,128,128]{3,2,1,0:T(8,128)(2,1)}), bf16[4,3,128,128]{3,2,1,0:T(8,128)(2,1)S(1)}, u32[]{:S(2)}, u32[]{:S(2)}) %all-to-all-start.2) | async-done | bytes 393248 | tf_op jit(solution)/shard_map/all_to_all | solution.py:113
  134.7 0.8 finish.1
  (4 shorter events, 0.0 us)
Async XLA Ops:
  2.3 30.3 %collective-permute-start = (bf16[2,128,128]{2,1,0:T(8,128)(2,1)S(1)}, bf16[2,128,128]{2,1,0:T(8,128)(2,1)S(1)}, u32[]{:S(2)}, u32[]{:S(2)}) collective-permute-start(bf16[2,128,128]{2,1,0:T(8,128)(2,1)S(1)} %pad_maximum_fusion), channel_id=1, source_target_pairs={{0,1},{1,0},{2,3},{3,2},{4,5},{5,4},{6,7},{7,6},{8,9},{9,8},{10,11... | collective-permute-start | bytes 196616 | tf_op jit(solution)/shard_map/ppermute | solution.py:117
  32.7 30.4 %copy-start = (bf16[128,4096]{1,0:T(8,128)(2,1)S(1)}, bf16[128,4096]{1,0:T(8,128)(2,1)}, u32[]{:S(2)}) copy-start(bf16[128,4096]{1,0:T(8,128)(2,1)} %w_ref.3) | copy-start | bytes 3145732
  32.7 30.4 %copy-start.2 = (bf16[128,128]{1,0:T(8,128)(2,1)S(1)}, bf16[128,128]{1,0:T(8,128)(2,1)}, u32[]{:S(2)}) copy-start(bf16[128,128]{1,0:T(8,128)(2,1)} %q_ref.3) | copy-start | bytes 98308
  33.9 29.1 %all-to-all-start = ((bf16[16,256,128]{2,1,0:T(8,128)(2,1)}), bf16[16,256,128]{2,1,0:T(8,128)(2,1)S(1)}, u32[]{:S(2)}, u32[]{:S(2)}) async-start(bf16[16,256,128]{2,1,0:T(8,128)(2,1)} %broadcast_in_dim.2), calls=%async_computation | async-start | bytes 2097152 | tf_op jit(solution)/shard_map/all_to_all | solution.py:113
  40.5 12.9 %collective-permute-start.3 = (bf16[4,2,128,128]{3,2,1,0:T(8,128)(2,1)S(1)}, bf16[4,2,128,128]{3,2,1,0:T(8,128)(2,1)S(1)}, u32[]{:S(2)}, u32[]{:S(2)}) collective-permute-start(bf16[4,2,128,128]{3,2,1,0:T(8,128)(2,1)S(1)} %bitcast.33), channel_id=1, source_target_pairs={{0,6},{2,4},{4,2},{6,0},{1,7},{3,5},{5,3},{7,1},{8,14},{10,12},{12... | collective-permute-start | bytes 786440 | tf_op jit(solution)/shard_map/ppermute | solution.py:117
  45.1 10.8 %collective-permute-start.2 = (bf16[4,2,128,128]{3,2,1,0:T(8,128)(2,1)S(1)}, bf16[4,2,128,128]{3,2,1,0:T(8,128)(2,1)S(1)}, u32[]{:S(2)}, u32[]{:S(2)}) collective-permute-start(bf16[4,2,128,128]{3,2,1,0:T(8,128)(2,1)S(1)} %bitcast.34), channel_id=1, source_target_pairs={{0,4},{2,6},{4,0},{6,2},{1,5},{3,7},{5,1},{7,3},{8,12},{10,14},{12... | collective-permute-start | bytes 786440 | tf_op jit(solution)/shard_map/ppermute | solution.py:117
  47.9 9.0 %collective-permute-start.1 = (bf16[4,2,128,128]{3,2,1,0:T(8,128)(2,1)S(1)}, bf16[4,2,128,128]{3,2,1,0:T(8,128)(2,1)S(1)}, u32[]{:S(2)}, u32[]{:S(2)}) collective-permute-start(bf16[4,2,128,128]{3,2,1,0:T(8,128)(2,1)S(1)} %bitcast.35), channel_id=1, source_target_pairs={{0,2},{2,0},{4,6},{6,4},{1,3},{3,1},{5,7},{7,5},{8,10},{10,8},{12,... | collective-permute-start | bytes 786440 | tf_op jit(solution)/shard_map/ppermute | solution.py:117
  65.0 3.6 %collective-permute-start.4 = (f32[256,384]{1,0:T(8,128)S(1)}, f32[256,384]{1,0:T(8,128)S(1)}, u32[]{:S(2)}, u32[]{:S(2)}) collective-permute-start(f32[256,384]{1,0:T(8,128)S(1)} %forward.1.mine_ref), channel_id=1, source_target_pairs={{0,1},{1,0},{2,3},{3,2},{4,5},{5,4},{6,7},{7,6},{8,9},{9,8},{10,11... | collective-permute-start | bytes 1179656 | tf_op jit(solution)/shard_map/ppermute | solution.py:117
  71.3 1.1 copy-start.1
  72.5 25.7 %all-to-all-start.1 = ((bf16[4,4,3,128,128]{4,3,2,1,0:T(8,128)(2,1)}), bf16[4,4,3,128,128]{4,3,2,1,0:T(8,128)(2,1)}, u32[]{:S(2)}, u32[]{:S(2)}) async-start(bf16[4,4,3,128,128]{4,3,2,1,0:T(8,128)(2,1)} %copy-done.1), calls=%async_computation.1 | async-start | bytes 3145728 | tf_op jit(solution)/shard_map/all_to_all | solution.py:113
  76.8 3.1 %collective-permute-start.5 = (f32[128,128]{1,0:T(8,128)S(1)}, f32[128,128]{1,0:T(8,128)S(1)}, u32[]{:S(2)}, u32[]{:S(2)}) collective-permute-start(f32[128,128]{1,0:T(8,128)S(1)} %slice_bitcast_fusion.4), channel_id=1, source_target_pairs={{0,1},{1,0},{2,3},{3,2},{4,5},{5,4},{6,7},{7,6},{8,9},{9,8},{10,11... | collective-permute-start | bytes 196616 | tf_op jit(solution)/shard_map/ppermute | solution.py:117
  81.0 26.3 %collective-permute-start.6 = (bf16[4,128,256]{2,1,0:T(8,128)(2,1)S(1)}, bf16[4,128,256]{2,1,0:T(8,128)(2,1)S(1)}, u32[]{:S(2)}, u32[]{:S(2)}) collective-permute-start(bf16[4,128,256]{2,1,0:T(8,128)(2,1)S(1)} %get-tuple-element.39), channel_id=1, source_target_pairs={{0,128},{128,0},{256,384},{384,256},{1,129},{129,1},{257,385},{385... | collective-permute-start | bytes 786440 | tf_op jit(solution)/shard_map/ppermute | solution.py:117
  85.5 21.7 %collective-permute-start.7 = (bf16[4,128,256]{2,1,0:T(8,128)(2,1)S(1)}, bf16[4,128,256]{2,1,0:T(8,128)(2,1)S(1)}, u32[]{:S(2)}, u32[]{:S(2)}) collective-permute-start(bf16[4,128,256]{2,1,0:T(8,128)(2,1)S(1)} %get-tuple-element.40), channel_id=1, source_target_pairs={{0,256},{128,384},{256,0},{384,128},{1,257},{129,385},{257,1},{385... | collective-permute-start | bytes 786440 | tf_op jit(solution)/shard_map/ppermute | solution.py:117
  87.7 19.5 %collective-permute-start.8 = (bf16[4,128,256]{2,1,0:T(8,128)(2,1)S(1)}, bf16[4,128,256]{2,1,0:T(8,128)(2,1)S(1)}, u32[]{:S(2)}, u32[]{:S(2)}) collective-permute-start(bf16[4,128,256]{2,1,0:T(8,128)(2,1)S(1)} %get-tuple-element.41), channel_id=1, source_target_pairs={{0,384},{128,256},{256,128},{384,0},{1,385},{129,257},{257,129},{3... | collective-permute-start | bytes 786440 | tf_op jit(solution)/shard_map/ppermute | solution.py:117
  100.5 34.2 %all-to-all-start.2 = ((bf16[4,3,128,128]{3,2,1,0:T(8,128)(2,1)}), bf16[4,3,128,128]{3,2,1,0:T(8,128)(2,1)S(1)}, u32[]{:S(2)}, u32[]{:S(2)}) async-start(bf16[4,3,128,128]{3,2,1,0:T(8,128)(2,1)} %fusion), calls=%async_computation.2 | async-start | bytes 786432 | tf_op jit(solution)/shard_map/all_to_all | solution.py:113
  107.4 18.7 %collective-permute-start.9 = (bf16[128,256]{1,0:T(8,128)(2,1)S(1)}, bf16[128,256]{1,0:T(8,128)(2,1)S(1)}, u32[]{:S(2)}, u32[]{:S(2)}) collective-permute-start(bf16[128,256]{1,0:T(8,128)(2,1)S(1)} %get-tuple-element.47), channel_id=1, source_target_pairs={{0,32},{32,0},{64,96},{96,64},{1,33},{33,1},{65,97},{97,65},{2,34}... | collective-permute-start | bytes 196616 | tf_op jit(solution)/shard_map/ppermute | solution.py:117
  109.4 19.0 %collective-permute-start.11 = (bf16[128,256]{1,0:T(8,128)(2,1)S(1)}, bf16[128,256]{1,0:T(8,128)(2,1)S(1)}, u32[]{:S(2)}, u32[]{:S(2)}) collective-permute-start(bf16[128,256]{1,0:T(8,128)(2,1)S(1)} %get-tuple-element.48), channel_id=1, source_target_pairs={{0,96},{32,64},{64,32},{96,0},{1,97},{33,65},{65,33},{97,1},{2,98}... | collective-permute-start | bytes 196616 | tf_op jit(solution)/shard_map/ppermute | solution.py:117
  113.6 16.6 %collective-permute-start.10 = (bf16[128,256]{1,0:T(8,128)(2,1)S(1)}, bf16[128,256]{1,0:T(8,128)(2,1)S(1)}, u32[]{:S(2)}, u32[]{:S(2)}) collective-permute-start(bf16[128,256]{1,0:T(8,128)(2,1)S(1)} %get-tuple-element.49), channel_id=1, source_target_pairs={{0,64},{32,96},{64,0},{96,32},{1,65},{33,97},{65,1},{97,33},{2,66}... | collective-permute-start | bytes 196616 | tf_op jit(solution)/shard_map/ppermute | solution.py:117

commit v4 on v3

--- a/solution.py
+++ b/solution.py
@@ -13,19 +13,12 @@
 BF16 = jnp.bfloat16
 VMEM = pl.BlockSpec(memory_space=pltpu.VMEM)
 SMEM = pl.BlockSpec(memory_space=pltpu.SMEM)
+HBM = pl.BlockSpec(memory_space=pltpu.HBM)
 shape = jax.ShapeDtypeStruct
 
 
 def dot(a, b, dims=((1,), (0,))):
     return lax.dot_general(a, b, (dims, ((), ())), preferred_element_type=F32)
-
-
-def project_kernel(place_ref, attn_ref, w_ref, *out_refs):
-    for r, out_ref in enumerate(out_refs):
-        for t in range(4):
-            o = lax.bitwise_xor(place_ref[2], r) * 4 + lax.bitwise_xor(place_ref[3], t)
-            cols = pl.ds(pl.multiple_of(o * 256, 256), 256)
-            out_ref[t] = dot(attn_ref[...], w_ref[:, cols]).astype(BF16)
 
 
 def forward_kernel(place_ref, q_ref, other_ref, kv0, kv1, kv2, kv3, w_ref, cot_ref, part_ref, s_ref):
@@ -70,18 +63,28 @@
     return grad, attn, lse[:, :1], dots
 
 
-def backward_kernel(place_ref, q_ref, other_ref, kv0, kv1, kv2, kv3, cot_ref, mine_ref, theirs_ref, *refs):
+def backward_kernel(
+    place_ref, q_ref, other_ref, kv0, kv1, kv2, kv3, cot_ref, w_ref, mine_ref, theirs_ref, *refs
+):
     pieces = (kv0, kv1, kv2, kv3)
-    dq_ref, pay_ref, attn_ref = refs
+    dq_ref, pay_hbm, *out_hbm, pay_ref, out_ref, sems = refs
     halves = [merged(mine_ref, theirs_ref, half) for half in range(2)]
     grad, attn, lse, dots = (jnp.concatenate(pair, axis=0) for pair in zip(*halves))
-    attn_ref[...] = halves[0][1]
+    copies = []
+    for r in range(4):
+        for t in range(4):
+            o = lax.bitwise_xor(place_ref[2], t) * 4 + lax.bitwise_xor(place_ref[3], r)
+            cols = pl.ds(pl.multiple_of(o * 256, 256), 256)
+            out_ref[r, t] = dot(halves[0][1], w_ref[:, cols]).astype(BF16)
+        copies.append(pltpu.make_async_copy(out_ref.at[r], out_hbm[r], sems.at[r]))
+        copies[r].start()
     q = jnp.concatenate([q_ref[...], other_ref[0]], axis=0)
     q_t = q.T
     grad_t = grad.T
     attn_t = attn.T
     dq = jnp.zeros((2 * BLK, HDIM), F32)
     for j in range(4):
+        x = lax.bitwise_xor(place_ref[1], j)
         k = pieces[j][:, 0].reshape(WIDTH, HDIM)
         v = pieces[j][:, 1].reshape(WIDTH, HDIM)
         s = dot(q, k, ((1,), (1,))) * SCALE
@@ -91,15 +94,16 @@
         dq = dq + dot(ds, k)
         dk_t = dot(q_t, ds).astype(BF16)
         dv_t = dot(grad_t, p.astype(BF16)).astype(BF16)
-        x = lax.bitwise_xor(place_ref[1], j)
         for z in range(4):
-            pay_ref[x, z, 0] = dk_t[:, z * BLK : (z + 1) * BLK]
-            pay_ref[x, z, 1] = dv_t[:, z * BLK : (z + 1) * BLK]
+            pay_ref[j, z, 0] = dk_t[:, z * BLK : (z + 1) * BLK]
+            pay_ref[j, z, 1] = dv_t[:, z * BLK : (z + 1) * BLK]
+            pay_ref[j, z, 2] = dot(attn_t, cot_ref[z * 4 + x]).astype(BF16)
+        copies.append(pltpu.make_async_copy(pay_ref.at[j], pay_hbm.at[x], sems.at[4 + j]))
+        copies[4 + j].start()
     dq_ref[0] = dq[:BLK]
     dq_ref[1] = dq[BLK:]
-    for x in range(4):
-        for z in range(4):
-            pay_ref[x, z, 2] = dot(attn_t, cot_ref[z * 4 + x]).astype(BF16)
+    for copy in copies:
+        copy.wait()
 
 
 def finish_kernel(parts_ref, dk_ref, dv_ref, dw_ref):
@@ -124,12 +128,12 @@
     return total
 
 
-def call(kernel, name, out_shape, in_specs, limit, flops, nbytes, exps=0, scratch=()):
+def call(kernel, name, out_shape, in_specs, limit, flops, nbytes, exps=0, scratch=(), out_specs=None):
     return pl.pallas_call(
         kernel,
         out_shape=out_shape,
         in_specs=in_specs,
-        out_specs=jax.tree.map(lambda _: VMEM, out_shape),
+        out_specs=jax.tree.map(lambda _: VMEM, out_shape) if out_specs is None else out_specs,
         scratch_shapes=scratch,
         compiler_params=pltpu.CompilerParams(vmem_limit_bytes=limit << 20),
         cost_estimate=pl.CostEstimate(flops=flops, bytes_accessed=nbytes, transcendentals=exps),
@@ -164,29 +168,34 @@
         [pltpu.VMEM((2 * BLK, 16 * BLK), F32)],
     )(place, queries, other, *pieces, w_out, cot)
     theirs = trade(part, "c", 1)
-    dq, pay, attn = call(
+    dq, pay, *outs = call(
         backward_kernel,
         "backward",
-        (shape((2, BLK, HDIM), F32), shape((4, 4, 3, BLK, BLK), BF16), tile),
-        [SMEM] + [VMEM] * 9,
-        8,
-        12 * unit,
-        7 << 20,
+        (shape((2, BLK, HDIM), F32), pltpu.HBM((4, 4, 3, BLK, BLK), BF16))
+        + (pltpu.HBM((4, BLK, 256), BF16),) * 4,
+        [SMEM] + [VMEM] * 10,
+        12,
+        14 * unit,
+        8 << 20,
         unit // BLK,
-    )(place, queries, other, *pieces, cot, part, theirs)
-    dq, pay, attn = lax.optimization_barrier((dq, pay, attn))
+        [
+            pltpu.VMEM((4, 4, 3, BLK, BLK), BF16),
+            pltpu.VMEM((4, 4, BLK, 256), BF16),
+            pltpu.SemaphoreType.DMA((8,)),
+        ],
+        (VMEM,) + (HBM,) * 5,
+    )(place, queries, other, *pieces, cot, w_out, part, theirs)
+    pay, *outs = lax.optimization_barrier((pay, *outs))
     pay = exchange(pay, "x")
+    passing = trade(outs[3], "zl", 1)
+    near = trade(outs[1], "zl", 1)
     dq_got = trade(dq[1], "c", 1)
-    attn, dq_got = lax.optimization_barrier((attn, dq_got))
-    quarter = shape((4, BLK, 256), BF16)
-    outs = call(
-        project_kernel, "project", (quarter,) * 4, [SMEM] + [VMEM] * 2, 8, 2 * unit, 2 << 20
-    )(place, attn, w_out)
-    outs = [outs[0]] + [trade(outs[r], "y", r) for r in (1, 2, 3)]
+    passing, dq_got = lax.optimization_barrier((passing, dq_got))
+    far = trade(add_all([outs[2], passing]).astype(BF16), "zl", 2)
     pay = add_all([pay[r] for r in range(4)]).astype(BF16)
-    out = add_all(outs).astype(BF16)
     pay = exchange(pay, "zh")
-    out = add_all([out[0]] + [trade(out[t], "zl", t) for t in (1, 2, 3)]).astype(BF16)
+    out = add_all([outs[0], near, far]).astype(BF16)
+    out = add_all([out[0]] + [trade(out[t], "y", t) for t in (1, 2, 3)]).astype(BF16)
     dq = ((dq[0] + dq_got) * SCALE).astype(BF16)
     dk, dv, dw = call(
         finish_kernel, "finish", (tile, tile, shape((BLK, BLK), F32)), [VMEM], 4, 0, 1 << 20

time: 136 us -> 132 us (0.971)
  the two profiles are of different devices: /device:TPU:8 before, /device:TPU:1 now
where the time goes in v4:
time: 132 us; the launch traced here: 131 us
  starting transfers between devices  57.2 us (43%)
  waiting for transfers between devices  41.2 us (31%)
  blocking collectives  19.1 us (14%)
  Pallas kernels  6.4 us (5%)
  other arithmetic  4.84 us (4%)
    ppermute x12, starting transfers between devices, trade(): lax.ppermute(block, axis, [(i, i ^ step) for i in range(2 if axis == 'c'...  40.8 us
    all_to_all x3, waiting for transfers between devices, exchange(): return lax.all_to_all(blocks, axis, 0, 0, tiled=True)  30.6 us
    all_gather x1, blocking collectives, body(): lax.all_gather(jnp.concatenate([keys, values]), 'zh', axis=0, tiled=True)  19.1 us
    all_to_all x3, starting transfers between devices, exchange(): return lax.all_to_all(blocks, axis, 0, 0, tiled=True)  16.4 us
    ppermute x12, waiting for transfers between devices, trade(): lax.ppermute(block, axis, [(i, i ^ step) for i in range(2 if axis == 'c'...  10.6 us
    pallas_call x1, Pallas kernels, body(): call(backward_kernel, 'backward', (shape((2, BLK, HDIM), F32), pltpu.HBM(...  3.63 us
  transfers between devices with their start and end apart: 15, of which 9 were waited for; matrix products, arithmetic and copies ran while one was open for 2% of the time, Pallas kernels for 0%

profile of v4, /device:TPU:1, one launch (start us, length us, event | category | flops | bytes accessed | tf_op | source)
XLA Modules:
  0.0 130.9 jit_solution(4021796114939813895)
XLA Ops:
  0.6 0.1 pad_add_fusion.place_ref
  0.8 0.8 broadcast_select_fusion
  1.5 0.8 pad_maximum_fusion
  2.3 8.8 %collective-permute-start = (bf16[2,128,128]{2,1,0:T(8,128)(2,1)S(1)}, bf16[2,128,128]{2,1,0:T(8,128)(2,1)S(1)}, u32[]{:S(2)}, u32[]{:S(2)}) collective-permute-start(bf16[2,128,128]{2,1,0:T(8,128)(2,1)S(1)} %pad_maximum_fusion), channel_id=1, source_target_pairs={{0,1},{1,0},{2,3},{3,2},{4,5},{5,4},{6,7},{7,6},{8,9},{9,8},{10,11... | collective-permute-start | bytes 196616 | tf_op jit(solution)/shard_map/ppermute | solution.py:121
  11.1 0.8 pad_maximum_fusion.1
  11.9 19.1 %all_gather.3 = bf16[1024,128]{1,0:T(8,128)(2,1)S(1)} all-gather(bf16[256,128]{1,0:T(8,128)(2,1)S(1)} %pad_maximum_fusion.1), channel_id=1, replica_groups=mesh['y'=4,'zl'=4,'zh'=4,'x'=4,'c'=2] {'zh'}, dimensions={0}, use_global_device_ids=true | all-gather | bytes 327680 | tf_op jit(solution)/shard_map/all_gather | solution.py:153
  31.0 0.0 collective-permute-done.other_ref
  31.0 0.0 copy-start
  31.0 0.0 copy-start.1
  31.0 1.2 broadcast_in_dim.2
  32.3 5.8 %all-to-all-start = ((bf16[16,256,128]{2,1,0:T(8,128)(2,1)}), bf16[16,256,128]{2,1,0:T(8,128)(2,1)S(1)}, u32[]{:S(2)}, u32[]{:S(2)}) async-start(bf16[16,256,128]{2,1,0:T(8,128)(2,1)} %broadcast_in_dim.2), calls=%async_computation | async-start | bytes 2097152 | tf_op jit(solution)/shard_map/all_to_all | solution.py:117
  38.0 4.4 %collective-permute-start.3 = (bf16[4,2,128,128]{3,2,1,0:T(8,128)(2,1)S(1)}, bf16[4,2,128,128]{3,2,1,0:T(8,128)(2,1)S(1)}, u32[]{:S(2)}, u32[]{:S(2)}) collective-permute-start(bf16[4,2,128,128]{3,2,1,0:T(8,128)(2,1)S(1)} %bitcast.33), channel_id=1, source_target_pairs={{0,6},{2,4},{4,2},{6,0},{1,7},{3,5},{5,3},{7,1},{8,14},{10,12},{12... | collective-permute-start | bytes 786440 | tf_op jit(solution)/shard_map/ppermute | solution.py:121
  42.4 2.4 %collective-permute-start.2 = (bf16[4,2,128,128]{3,2,1,0:T(8,128)(2,1)S(1)}, bf16[4,2,128,128]{3,2,1,0:T(8,128)(2,1)S(1)}, u32[]{:S(2)}, u32[]{:S(2)}) collective-permute-start(bf16[4,2,128,128]{3,2,1,0:T(8,128)(2,1)S(1)} %bitcast.34), channel_id=1, source_target_pairs={{0,4},{2,6},{4,0},{6,2},{1,5},{3,7},{5,1},{7,3},{8,12},{10,14},{12... | collective-permute-start | bytes 786440 | tf_op jit(solution)/shard_map/ppermute | solution.py:121
  44.9 2.2 %collective-permute-start.1 = (bf16[4,2,128,128]{3,2,1,0:T(8,128)(2,1)S(1)}, bf16[4,2,128,128]{3,2,1,0:T(8,128)(2,1)S(1)}, u32[]{:S(2)}, u32[]{:S(2)}) collective-permute-start(bf16[4,2,128,128]{3,2,1,0:T(8,128)(2,1)S(1)} %bitcast.35), channel_id=1, source_target_pairs={{0,2},{2,0},{4,6},{6,4},{1,3},{3,1},{5,7},{7,5},{8,10},{10,8},{12,... | collective-permute-start | bytes 786440 | tf_op jit(solution)/shard_map/ppermute | solution.py:121
  47.0 1.6 %collective-permute-done.3.kv3 = bf16[4,2,128,128]{3,2,1,0:T(8,128)(2,1)S(1)} collective-permute-done((bf16[4,2,128,128]{3,2,1,0:T(8,128)(2,1)S(1)}, bf16[4,2,128,128]{3,2,1,0:T(8,128)(2,1)S(1)}, u32[]{:S(2)}, u32[]{:S(2)}) %collective-permute-start.3) | collective-permute-done | bytes 262176 | tf_op jit(solution)/shard_map/ppermute | solution.py:121
  48.6 2.8 %collective-permute-done.2.kv2 = bf16[4,2,128,128]{3,2,1,0:T(8,128)(2,1)S(1)} collective-permute-done((bf16[4,2,128,128]{3,2,1,0:T(8,128)(2,1)S(1)}, bf16[4,2,128,128]{3,2,1,0:T(8,128)(2,1)S(1)}, u32[]{:S(2)}, u32[]{:S(2)}) %collective-permute-start.2) | collective-permute-done | bytes 262176 | tf_op jit(solution)/shard_map/ppermute | solution.py:121
  51.4 2.5 %collective-permute-done.1.kv1 = bf16[4,2,128,128]{3,2,1,0:T(8,128)(2,1)S(1)} collective-permute-done((bf16[4,2,128,128]{3,2,1,0:T(8,128)(2,1)S(1)}, bf16[4,2,128,128]{3,2,1,0:T(8,128)(2,1)S(1)}, u32[]{:S(2)}, u32[]{:S(2)}) %collective-permute-start.1) | collective-permute-done | bytes 262176 | tf_op jit(solution)/shard_map/ppermute | solution.py:121
  53.9 10.9 %all-to-all-done.cot_ref = bf16[16,256,128]{2,1,0:T(8,128)(2,1)S(1)} async-done(((bf16[16,256,128]{2,1,0:T(8,128)(2,1)}), bf16[16,256,128]{2,1,0:T(8,128)(2,1)S(1)}, u32[]{:S(2)}, u32[]{:S(2)}) %all-to-all-start) | async-done | bytes 1048608 | tf_op jit(solution)/shard_map/all_to_all | solution.py:117
  64.8 0.0 copy-done
  64.8 0.0 copy-done.1
  64.8 2.0 %forward.1.mine_ref = f32[256,384]{1,0:T(8,128)S(1)} custom-call(s32[4]{0:T(128)S(1)} %pad_add_fusion.place_ref, bf16[128,128]{1,0:T(8,128)(2,1)S(1)} %copy-done.1, bf16[2,128,128]{2,1,0:T(8,128)(2,1)S(1)} %collective-permute-done.other_ref, bf16[4,2,128,128]{3,2,1,0:T(8,128)(2,1)S(1)} %bitcast.36, bf16[4,2,128,128]{3,2,1,0:T(8,128)(2,1)S(1)} %collective-permute-done.1.kv1, ...), custom_call_target="tpu_custom_call" | custom-call | flops 402653184 | bytes 5242880 | tf_op jit(solution)/shard_map/forward/pallas_call | solution.py:159
  66.8 3.9 %collective-permute-start.4 = (f32[256,384]{1,0:T(8,128)S(1)}, f32[256,384]{1,0:T(8,128)S(1)}, u32[]{:S(2)}, u32[]{:S(2)}) collective-permute-start(f32[256,384]{1,0:T(8,128)S(1)} %forward.1.mine_ref), channel_id=1, source_target_pairs={{0,1},{1,0},{2,3},{3,2},{4,5},{5,4},{6,7},{7,6},{8,9},{9,8},{10,11... | collective-permute-start | bytes 1179656 | tf_op jit(solution)/shard_map/ppermute | solution.py:121
  70.7 1.3 %collective-permute-done.4.theirs_ref = f32[256,384]{1,0:T(8,128)S(1)} collective-permute-done((f32[256,384]{1,0:T(8,128)S(1)}, f32[256,384]{1,0:T(8,128)S(1)}, u32[]{:S(2)}, u32[]{:S(2)}) %collective-permute-start.4) | collective-permute-done | bytes 393248 | tf_op jit(solution)/shard_map/ppermute | solution.py:121
  72.0 3.6 %backward.1 = (f32[2,128,128]{2,1,0:T(8,128)S(1)}, bf16[4,4,3,128,128]{4,3,2,1,0:T(8,128)(2,1)}, bf16[4,128,256]{2,1,0:T(8,128)(2,1)}, bf16[4,128,256]{2,1,0:T(8...) custom-call(s32[4]{0:T(128)S(1)} %pad_add_fusion.place_ref, bf16[128,128]{1,0:T(8,128)(2,1)S(1)} %copy-done.1, ...), custom_call_target="tpu_custom_call" | custom-call | flops 939524096 | bytes 8388608 | tf_op jit(solution)/shard_map/backward/pallas_call | solution.py:171
  75.7 0.0 copy-start.5
  75.7 0.0 copy-start.4
  75.7 0.0 copy-start.2
  75.7 4.1 %all-to-all-start.1 = ((bf16[4,4,3,128,128]{4,3,2,1,0:T(8,128)(2,1)}), bf16[4,4,3,128,128]{4,3,2,1,0:T(8,128)(2,1)S(1)}, u32[]{:S(2)}, u32[]{:S(2)}) async-start(bf16[4,4,3,128,128]{4,3,2,1,0:T(8,128)(2,1)} %get-tuple-element.51), calls=%async_computation.1 | async-start | bytes 3145728 | tf_op jit(solution)/shard_map/all_to_all | solution.py:117
  79.8 0.0 copy-done.5
  79.9 1.9 %collective-permute-start.6 = (bf16[4,128,256]{2,1,0:T(8,128)(2,1)S(1)}, bf16[4,128,256]{2,1,0:T(8,128)(2,1)S(1)}, u32[]{:S(2)}, u32[]{:S(2)}) collective-permute-start(bf16[4,128,256]{2,1,0:T(8,128)(2,1)S(1)} %copy-done.5), channel_id=1, source_target_pairs={{0,32},{32,0},{64,96},{96,64},{1,33},{33,1},{65,97},{97,65},{2,34}... | collective-permute-start | bytes 786440 | tf_op jit(solution)/shard_map/ppermute | solution.py:121
  81.8 2.6 %collective-permute-start.7 = (f32[128,128]{1,0:T(8,128)S(1)}, f32[128,128]{1,0:T(8,128)S(1)}, u32[]{:S(2)}, u32[]{:S(2)}) collective-permute-start(f32[128,128]{1,0:T(8,128)S(1)} %slice_bitcast_fusion.4), channel_id=1, source_target_pairs={{0,1},{1,0},{2,3},{3,2},{4,5},{5,4},{6,7},{7,6},{8,9},{9,8},{10,11... | collective-permute-start | bytes 196616 | tf_op jit(solution)/shard_map/ppermute | solution.py:121
  84.3 0.0 copy-done.4
  84.4 3.6 %collective-permute-start.5 = (bf16[4,128,256]{2,1,0:T(8,128)(2,1)S(1)}, bf16[4,128,256]{2,1,0:T(8,128)(2,1)S(1)}, u32[]{:S(2)}, u32[]{:S(2)}) collective-permute-start(bf16[4,128,256]{2,1,0:T(8,128)(2,1)S(1)} %copy-done.4), channel_id=1, source_target_pairs={{0,32},{32,0},{64,96},{96,64},{1,33},{33,1},{65,97},{97,65},{2,34}... | collective-permute-start | bytes 786440 | tf_op jit(solution)/shard_map/ppermute | solution.py:121
  88.0 0.0 collective-permute-done.7
  88.0 0.9 collective-permute-done.6
  88.9 0.0 copy-done.2
  89.0 0.1 add_convert_fusion.2
  89.0 0.0 copy-start.3
  89.0 2.1 %collective-permute-start.8 = (bf16[4,128,256]{2,1,0:T(8,128)(2,1)S(1)}, bf16[4,128,256]{2,1,0:T(8,128)(2,1)S(1)}, u32[]{:S(2)}, u32[]{:S(2)}) collective-permute-start(bf16[4,128,256]{2,1,0:T(8,128)(2,1)S(1)} %add_convert_fusion.2), channel_id=1, source_target_pairs={{0,64},{32,96},{64,0},{96,32},{1,65},{33,97},{65,1},{97,33},{2,66}... | collective-permute-start | bytes 786440 | tf_op jit(solution)/shard_map/ppermute | solution.py:121
  91.1 8.9 %all-to-all-done.1 = bf16[4,4,3,128,128]{4,3,2,1,0:T(8,128)(2,1)S(1)} async-done(((bf16[4,4,3,128,128]{4,3,2,1,0:T(8,128)(2,1)}), bf16[4,4,3,128,128]{4,3,2,1,0:T(8,128)(2,1)S(1)}, u32[]{:S(2)}, u32[]{:S(2)}) %all-to-all-start.1) | async-done | bytes 1572896 | tf_op jit(solution)/shard_map/all_to_all | solution.py:117
  100.0 1.0 fusion
  101.0 6.4 %all-to-all-start.2 = ((bf16[4,3,128,128]{3,2,1,0:T(8,128)(2,1)}), bf16[4,3,128,128]{3,2,1,0:T(8,128)(2,1)S(1)}, u32[]{:S(2)}, u32[]{:S(2)}) async-start(bf16[4,3,128,128]{3,2,1,0:T(8,128)(2,1)} %fusion), calls=%async_computation.2 | async-start | bytes 786432 | tf_op jit(solution)/shard_map/all_to_all | solution.py:117
  107.4 0.0 collective-permute-done.5
  107.4 0.0 collective-permute-done.8
  107.4 0.0 copy-done.3
  107.4 0.1 add_convert_fusion.1
  107.6 1.9 %collective-permute-start.9 = (bf16[128,256]{1,0:T(8,128)(2,1)S(1)}, bf16[128,256]{1,0:T(8,128)(2,1)S(1)}, u32[]{:S(2)}, u32[]{:S(2)}) collective-permute-start(bf16[128,256]{1,0:T(8,128)(2,1)S(1)} %get-tuple-element.55), channel_id=1, source_target_pairs={{0,128},{128,0},{256,384},{384,256},{1,129},{129,1},{257,385},{385... | collective-permute-start | bytes 196616 | tf_op jit(solution)/shard_map/ppermute | solution.py:121
  109.5 2.7 %collective-permute-start.11 = (bf16[128,256]{1,0:T(8,128)(2,1)S(1)}, bf16[128,256]{1,0:T(8,128)(2,1)S(1)}, u32[]{:S(2)}, u32[]{:S(2)}) collective-permute-start(bf16[128,256]{1,0:T(8,128)(2,1)S(1)} %get-tuple-element.56), channel_id=1, source_target_pairs={{0,384},{128,256},{256,128},{384,0},{1,385},{129,257},{257,129},{3... | collective-permute-start | bytes 196616 | tf_op jit(solution)/shard_map/ppermute | solution.py:121
  112.2 4.3 %collective-permute-start.10 = (bf16[128,256]{1,0:T(8,128)(2,1)S(1)}, bf16[128,256]{1,0:T(8,128)(2,1)S(1)}, u32[]{:S(2)}, u32[]{:S(2)}) collective-permute-start(bf16[128,256]{1,0:T(8,128)(2,1)S(1)} %get-tuple-element.57), channel_id=1, source_target_pairs={{0,256},{128,384},{256,0},{384,128},{1,257},{129,385},{257,1},{385... | collective-permute-start | bytes 196616 | tf_op jit(solution)/shard_map/ppermute | solution.py:121
  116.6 0.6 fusion.5
  117.2 0.0 collective-permute-done.9
  117.2 0.0 collective-permute-done.11
  117.2 1.6 %collective-permute-done.10 = bf16[128,256]{1,0:T(8,128)(2,1)S(1)} collective-permute-done((bf16[128,256]{1,0:T(8,128)(2,1)S(1)}, bf16[128,256]{1,0:T(8,128)(2,1)S(1)}, u32[]{:S(2)}, u32[]{:S(2)}) %collective-permute-start.10) | collective-permute-done | bytes 65568 | tf_op jit(solution)/shard_map/ppermute | solution.py:121
  118.8 0.7 fusion.3
  119.4 10.7 %all-to-all-done.2.parts_ref = bf16[4,3,128,128]{3,2,1,0:T(8,128)(2,1)S(1)} async-done(((bf16[4,3,128,128]{3,2,1,0:T(8,128)(2,1)}), bf16[4,3,128,128]{3,2,1,0:T(8,128)(2,1)S(1)}, u32[]{:S(2)}, u32[]{:S(2)}) %all-to-all-start.2) | async-done | bytes 393248 | tf_op jit(solution)/shard_map/all_to_all | solution.py:117
  130.1 0.8 finish.1
  (4 shorter events, 0.0 us)
Async XLA Ops:
  2.3 28.7 %collective-permute-start = (bf16[2,128,128]{2,1,0:T(8,128)(2,1)S(1)}, bf16[2,128,128]{2,1,0:T(8,128)(2,1)S(1)}, u32[]{:S(2)}, u32[]{:S(2)}) collective-permute-start(bf16[2,128,128]{2,1,0:T(8,128)(2,1)S(1)} %pad_maximum_fusion), channel_id=1, source_target_pairs={{0,1},{1,0},{2,3},{3,2},{4,5},{5,4},{6,7},{7,6},{8,9},{9,8},{10,11... | collective-permute-start | bytes 196616 | tf_op jit(solution)/shard_map/ppermute | solution.py:121
  31.0 33.8 %copy-start = (bf16[128,4096]{1,0:T(8,128)(2,1)S(1)}, bf16[128,4096]{1,0:T(8,128)(2,1)}, u32[]{:S(2)}) copy-start(bf16[128,4096]{1,0:T(8,128)(2,1)} %w_ref.3) | copy-start | bytes 3145732
  31.0 33.7 %copy-start.1 = (bf16[128,128]{1,0:T(8,128)(2,1)S(1)}, bf16[128,128]{1,0:T(8,128)(2,1)}, u32[]{:S(2)}) copy-start(bf16[128,128]{1,0:T(8,128)(2,1)} %q_ref.3) | copy-start | bytes 98308
  32.3 32.5 %all-to-all-start = ((bf16[16,256,128]{2,1,0:T(8,128)(2,1)}), bf16[16,256,128]{2,1,0:T(8,128)(2,1)S(1)}, u32[]{:S(2)}, u32[]{:S(2)}) async-start(bf16[16,256,128]{2,1,0:T(8,128)(2,1)} %broadcast_in_dim.2), calls=%async_computation | async-start | bytes 2097152 | tf_op jit(solution)/shard_map/all_to_all | solution.py:117
  38.0 10.6 %collective-permute-start.3 = (bf16[4,2,128,128]{3,2,1,0:T(8,128)(2,1)S(1)}, bf16[4,2,128,128]{3,2,1,0:T(8,128)(2,1)S(1)}, u32[]{:S(2)}, u32[]{:S(2)}) collective-permute-start(bf16[4,2,128,128]{3,2,1,0:T(8,128)(2,1)S(1)} %bitcast.33), channel_id=1, source_target_pairs={{0,6},{2,4},{4,2},{6,0},{1,7},{3,5},{5,3},{7,1},{8,14},{10,12},{12... | collective-permute-start | bytes 786440 | tf_op jit(solution)/shard_map/ppermute | solution.py:121
  42.4 9.0 %collective-permute-start.2 = (bf16[4,2,128,128]{3,2,1,0:T(8,128)(2,1)S(1)}, bf16[4,2,128,128]{3,2,1,0:T(8,128)(2,1)S(1)}, u32[]{:S(2)}, u32[]{:S(2)}) collective-permute-start(bf16[4,2,128,128]{3,2,1,0:T(8,128)(2,1)S(1)} %bitcast.34), channel_id=1, source_target_pairs={{0,4},{2,6},{4,0},{6,2},{1,5},{3,7},{5,1},{7,3},{8,12},{10,14},{12... | collective-permute-start | bytes 786440 | tf_op jit(solution)/shard_map/ppermute | solution.py:121
  44.9 9.0 %collective-permute-start.1 = (bf16[4,2,128,128]{3,2,1,0:T(8,128)(2,1)S(1)}, bf16[4,2,128,128]{3,2,1,0:T(8,128)(2,1)S(1)}, u32[]{:S(2)}, u32[]{:S(2)}) collective-permute-start(bf16[4,2,128,128]{3,2,1,0:T(8,128)(2,1)S(1)} %bitcast.35), channel_id=1, source_target_pairs={{0,2},{2,0},{4,6},{6,4},{1,3},{3,1},{5,7},{7,5},{8,10},{10,8},{12,... | collective-permute-start | bytes 786440 | tf_op jit(solution)/shard_map/ppermute | solution.py:121
  66.8 5.2 %collective-permute-start.4 = (f32[256,384]{1,0:T(8,128)S(1)}, f32[256,384]{1,0:T(8,128)S(1)}, u32[]{:S(2)}, u32[]{:S(2)}) collective-permute-start(f32[256,384]{1,0:T(8,128)S(1)} %forward.1.mine_ref), channel_id=1, source_target_pairs={{0,1},{1,0},{2,3},{3,2},{4,5},{5,4},{6,7},{7,6},{8,9},{9,8},{10,11... | collective-permute-start | bytes 1179656 | tf_op jit(solution)/shard_map/ppermute | solution.py:121
  75.7 4.2 %copy-start.5 = (bf16[4,128,256]{2,1,0:T(8,128)(2,1)S(1)}, bf16[4,128,256]{2,1,0:T(8,128)(2,1)}, u32[]{:S(2)}) copy-start(bf16[4,128,256]{2,1,0:T(8,128)(2,1)} %get-tuple-element.47) | copy-start | bytes 786436
  75.7 8.7 %copy-start.4 = (bf16[4,128,256]{2,1,0:T(8,128)(2,1)S(1)}, bf16[4,128,256]{2,1,0:T(8,128)(2,1)}, u32[]{:S(2)}) copy-start(bf16[4,128,256]{2,1,0:T(8,128)(2,1)} %get-tuple-element.45) | copy-start | bytes 786436
  75.7 13.3 %copy-start.2 = (bf16[4,128,256]{2,1,0:T(8,128)(2,1)S(1)}, bf16[4,128,256]{2,1,0:T(8,128)(2,1)}, u32[]{:S(2)}) copy-start(bf16[4,128,256]{2,1,0:T(8,128)(2,1)} %get-tuple-element.46) | copy-start | bytes 786436
  75.7 24.3 %all-to-all-start.1 = ((bf16[4,4,3,128,128]{4,3,2,1,0:T(8,128)(2,1)}), bf16[4,4,3,128,128]{4,3,2,1,0:T(8,128)(2,1)S(1)}, u32[]{:S(2)}, u32[]{:S(2)}) async-start(bf16[4,4,3,128,128]{4,3,2,1,0:T(8,128)(2,1)} %get-tuple-element.51), calls=%async_computation.1 | async-start | bytes 3145728 | tf_op jit(solution)/shard_map/all_to_all | solution.py:117
  79.9 9.1 %collective-permute-start.6 = (bf16[4,128,256]{2,1,0:T(8,128)(2,1)S(1)}, bf16[4,128,256]{2,1,0:T(8,128)(2,1)S(1)}, u32[]{:S(2)}, u32[]{:S(2)}) collective-permute-start(bf16[4,128,256]{2,1,0:T(8,128)(2,1)S(1)} %copy-done.5), channel_id=1, source_target_pairs={{0,32},{32,0},{64,96},{96,64},{1,33},{33,1},{65,97},{97,65},{2,34}... | collective-permute-start | bytes 786440 | tf_op jit(solution)/shard_map/ppermute | solution.py:121
  81.8 6.2 %collective-permute-start.7 = (f32[128,128]{1,0:T(8,128)S(1)}, f32[128,128]{1,0:T(8,128)S(1)}, u32[]{:S(2)}, u32[]{:S(2)}) collective-permute-start(f32[128,128]{1,0:T(8,128)S(1)} %slice_bitcast_fusion.4), channel_id=1, source_target_pairs={{0,1},{1,0},{2,3},{3,2},{4,5},{5,4},{6,7},{7,6},{8,9},{9,8},{10,11... | collective-permute-start | bytes 196616 | tf_op jit(solution)/shard_map/ppermute | solution.py:121
  84.4 23.1 %collective-permute-start.5 = (bf16[4,128,256]{2,1,0:T(8,128)(2,1)S(1)}, bf16[4,128,256]{2,1,0:T(8,128)(2,1)S(1)}, u32[]{:S(2)}, u32[]{:S(2)}) collective-permute-start(bf16[4,128,256]{2,1,0:T(8,128)(2,1)S(1)} %copy-done.4), channel_id=1, source_target_pairs={{0,32},{32,0},{64,96},{96,64},{1,33},{33,1},{65,97},{97,65},{2,34}... | collective-permute-start | bytes 786440 | tf_op jit(solution)/shard_map/ppermute | solution.py:121
  89.0 18.4 %copy-start.3 = (bf16[4,128,256]{2,1,0:T(8,128)(2,1)S(1)}, bf16[4,128,256]{2,1,0:T(8,128)(2,1)}, u32[]{:S(2)}) copy-start(bf16[4,128,256]{2,1,0:T(8,128)(2,1)} %get-tuple-element.44) | copy-start | bytes 786436
  89.0 18.4 %collective-permute-start.8 = (bf16[4,128,256]{2,1,0:T(8,128)(2,1)S(1)}, bf16[4,128,256]{2,1,0:T(8,128)(2,1)S(1)}, u32[]{:S(2)}, u32[]{:S(2)}) collective-permute-start(bf16[4,128,256]{2,1,0:T(8,128)(2,1)S(1)} %add_convert_fusion.2), channel_id=1, source_target_pairs={{0,64},{32,96},{64,0},{96,32},{1,65},{33,97},{65,1},{97,33},{2,66}... | collective-permute-start | bytes 786440 | tf_op jit(solution)/shard_map/ppermute | solution.py:121
  101.0 29.2 %all-to-all-start.2 = ((bf16[4,3,128,128]{3,2,1,0:T(8,128)(2,1)}), bf16[4,3,128,128]{3,2,1,0:T(8,128)(2,1)S(1)}, u32[]{:S(2)}, u32[]{:S(2)}) async-start(bf16[4,3,128,128]{3,2,1,0:T(8,128)(2,1)} %fusion), calls=%async_computation.2 | async-start | bytes 786432 | tf_op jit(solution)/shard_map/all_to_all | solution.py:117
  107.6 9.6 %collective-permute-start.9 = (bf16[128,256]{1,0:T(8,128)(2,1)S(1)}, bf16[128,256]{1,0:T(8,128)(2,1)S(1)}, u32[]{:S(2)}, u32[]{:S(2)}) collective-permute-start(bf16[128,256]{1,0:T(8,128)(2,1)S(1)} %get-tuple-element.55), channel_id=1, source_target_pairs={{0,128},{128,0},{256,384},{384,256},{1,129},{129,1},{257,385},{385... | collective-permute-start | bytes 196616 | tf_op jit(solution)/shard_map/ppermute | solution.py:121
  109.5 7.7 %collective-permute-start.11 = (bf16[128,256]{1,0:T(8,128)(2,1)S(1)}, bf16[128,256]{1,0:T(8,128)(2,1)S(1)}, u32[]{:S(2)}, u32[]{:S(2)}) collective-permute-start(bf16[128,256]{1,0:T(8,128)(2,1)S(1)} %get-tuple-element.56), channel_id=1, source_target_pairs={{0,384},{128,256},{256,128},{384,0},{1,385},{129,257},{257,129},{3... | collective-permute-start | bytes 196616 | tf_op jit(solution)/shard_map/ppermute | solution.py:121
  112.2 6.5 %collective-permute-start.10 = (bf16[128,256]{1,0:T(8,128)(2,1)S(1)}, bf16[128,256]{1,0:T(8,128)(2,1)S(1)}, u32[]{:S(2)}, u32[]{:S(2)}) collective-permute-start(bf16[128,256]{1,0:T(8,128)(2,1)S(1)} %get-tuple-element.57), channel_id=1, source_target_pairs={{0,256},{128,384},{256,0},{384,128},{1,257},{129,385},{257,1},{385... | collective-permute-start | bytes 196616 | tf_op jit(solution)/shard_map/ppermute | solution.py:121

commit v5 on v4

--- a/solution.py
+++ b/solution.py
@@ -21,13 +21,44 @@
     return lax.dot_general(a, b, (dims, ((), ())), preferred_element_type=F32)
 
 
-def forward_kernel(place_ref, q_ref, other_ref, kv0, kv1, kv2, kv3, w_ref, cot_ref, part_ref, s_ref):
-    pieces = (kv0, kv1, kv2, kv3)
+def pack_kernel(place_ref, q_hbm, k_hbm, v_hbm, grad_hbm, kv_ref, gift_ref, mine_ref, grad_ref, sems):
+    copies = [
+        pltpu.make_async_copy(grad_hbm, grad_ref, sems.at[0]),
+        pltpu.make_async_copy(q_hbm, gift_ref.at[0], sems.at[1]),
+        pltpu.make_async_copy(k_hbm, kv_ref.at[pl.ds(0, BLK)], sems.at[2]),
+        pltpu.make_async_copy(v_hbm, kv_ref.at[pl.ds(BLK, BLK)], sems.at[3]),
+    ]
+    for copy in copies:
+        copy.start()
+    for copy in copies:
+        copy.wait()
+    first = place_ref[0] == 0
+    left, right = grad_ref[:, :BLK], grad_ref[:, BLK:]
+    mine_ref[...] = jnp.where(first, left, right)
+    gift_ref[1] = jnp.where(first, right, left)
+
+
+def copies_kernel(mine_ref, other_ref, cot_hbm, pair_ref, sems):
+    pair_ref[:BLK] = mine_ref[...]
+    pair_ref[BLK:] = other_ref[1]
+    copies = [pltpu.make_async_copy(pair_ref, cot_hbm.at[o], sems.at[o]) for o in range(16)]
+    for copy in copies:
+        copy.start()
+    for copy in copies:
+        copy.wait()
+
+
+def cotangent_kernel(place_ref, w_ref, cot_ref, part_in, part_ref):
     grad = jnp.zeros((2 * BLK, HDIM), F32)
     for o in range(16):
         start = pl.multiple_of(o * 256 + place_ref[0] * BLK, BLK)
         grad = grad + dot(cot_ref[o], w_ref[:, pl.ds(start, BLK)], ((1,), (1,)))
     part_ref[:, :HDIM] = grad
+    part_ref[:, HDIM:] = part_in[...]
+
+
+def forward_kernel(q_ref, other_ref, kv0, kv1, kv2, kv3, part_ref, s_ref):
+    pieces = (kv0, kv1, kv2, kv3)
     q = jnp.concatenate([q_ref[...], other_ref[0]], axis=0)
     top = jnp.full((2 * BLK, BLK), -jnp.inf, F32)
     for j in range(4):
@@ -46,8 +77,8 @@
         v = pieces[j][:, 1].reshape(WIDTH, HDIM)
         acc = acc + dot(p.astype(BF16), v)
     totals = jnp.sum(sums, axis=1, keepdims=True)
-    part_ref[:, HDIM : 2 * HDIM] = acc / totals
-    part_ref[:, 2 * HDIM :] = jnp.broadcast_to(row_max + jnp.log(totals), (2 * BLK, BLK))
+    part_ref[:, :HDIM] = acc / totals
+    part_ref[:, HDIM:] = jnp.broadcast_to(row_max + jnp.log(totals), (2 * BLK, BLK))
 
 
 def merged(mine_ref, theirs_ref, half):
@@ -121,6 +152,10 @@
     return lax.ppermute(block, axis, [(i, i ^ step) for i in range(2 if axis == "c" else 4)])
 
 
+def in_hbm(block):
+    return pltpu.with_memory_space_constraint(block, pltpu.HBM)
+
+
 def add_all(blocks):
     total = blocks[0].astype(F32)
     for block in blocks[1:]:
@@ -145,28 +180,44 @@
     unit = BLK * BLK * 4096
     tile = shape((BLK, BLK), BF16)
     place = jnp.stack([lax.axis_index(a) for a in ("c", "x", "y", "zl")]).astype(jnp.int32)
-    place, keys = lax.optimization_barrier((place, keys))
-    first = place[0] == 0
-    left, right = grad_out[:, :BLK], grad_out[:, BLK:]
-    other = trade(jnp.stack([queries, jnp.where(first, right, left)]), "c", 1)
-    cot = jnp.concatenate([jnp.where(first, left, right), other[1]], axis=0)
-    kv = lax.all_gather(jnp.concatenate([keys, values]), "zh", axis=0, tiled=True)
-    kv = kv.reshape(4, 2, BLK, HDIM)
-    kv, cot = lax.optimization_barrier((kv, cot))
+    kv, gift, mine = call(
+        pack_kernel,
+        "pack",
+        (shape((2 * BLK, HDIM), BF16), shape((2, BLK, BLK), BF16), tile),
+        [SMEM] + [HBM] * 4,
+        4,
+        0,
+        1 << 19,
+        scratch=[pltpu.VMEM((BLK, 2 * BLK), BF16), pltpu.SemaphoreType.DMA((4,))],
+    )(place, *[in_hbm(block) for block in (queries, keys, values, grad_out)])
+    place, kv, gift, mine = lax.optimization_barrier((place, kv, gift, mine))
+    other = trade(gift, "c", 1)
+    kv = lax.all_gather(kv, "zh", axis=0, tiled=True).reshape(4, 2, BLK, HDIM)
+    kv, other = lax.optimization_barrier((kv, other))
+    cot = jnp.concatenate([mine, other[1]], axis=0)
     cot = exchange(jnp.broadcast_to(cot[None], (16, 2 * BLK, BLK)), ("y", "zl"))
     pieces = [kv] + [trade(kv, "x", r) for r in (1, 2, 3)]
-    cot, pieces = lax.optimization_barrier((cot, pieces))
     part = call(
         forward_kernel,
         "forward",
-        shape((2 * BLK, 3 * BLK), F32),
-        [SMEM] + [VMEM] * 8,
+        shape((2 * BLK, 2 * BLK), F32),
+        [VMEM] * 6,
         8,
-        6 * unit,
-        5 << 20,
+        4 * unit,
+        4 << 20,
         unit // BLK,
         [pltpu.VMEM((2 * BLK, 16 * BLK), F32)],
-    )(place, queries, other, *pieces, w_out, cot)
+    )(queries, other, *pieces)
+    cot, part = lax.optimization_barrier((cot, part))
+    part = call(
+        cotangent_kernel,
+        "cotangent",
+        shape((2 * BLK, 3 * BLK), F32),
+        [SMEM] + [VMEM] * 3,
+        8,
+        2 * unit,
+        2 << 20,
+    )(place, w_out, cot, part)
     theirs = trade(part, "c", 1)
     dq, pay, *outs = call(
         backward_kernel,

time: 132 us -> 130 us (0.985)
  other arithmetic: 4.84 us -> 2.5 us
  Pallas kernels: 6.4 us -> 7.97 us
    pallas_call x1 -> x3, Pallas kernels: 2 us -> 3.6 us  [the longest x1 1.44 us: body(): call(pack_kernel, 'pack', (shape((2 * BLK, HDIM), BF16), shape((2, BLK, B...]
  transfers between devices with their start and end apart: 15 -> 15, of which waited for: 9 -> 9; matrix products, arithmetic and copies ran while one was open for 2% -> 2% of each run, Pallas kernels for 0% -> 1%
where the time goes in v5:
time: 130 us; the launch traced here: 129 us
  starting transfers between devices  57.3 us (44%)
  waiting for transfers between devices  40.4 us (31%)
  blocking collectives  19.1 us (15%)
  Pallas kernels  7.97 us (6%)
  other arithmetic  2.5 us (2%)
    ppermute x12, starting transfers between devices, trade(): lax.ppermute(block, axis, [(i, i ^ step) for i in range(2 if axis == 'c'...  40.8 us
    all_to_all x3, waiting for transfers between devices, exchange(): return lax.all_to_all(blocks, axis, 0, 0, tiled=True)  29.8 us
    all_gather x1, blocking collectives, body(): kv = lax.all_gather(kv, 'zh', axis=0, tiled=True).reshape(4, 2, BLK, HDIM)  19.1 us
    all_to_all x3, starting transfers between devices, exchange(): return lax.all_to_all(blocks, axis, 0, 0, tiled=True)  16.5 us
    ppermute x12, waiting for transfers between devices, trade(): lax.ppermute(block, axis, [(i, i ^ step) for i in range(2 if axis == 'c'...  10.6 us
    pallas_call x1, Pallas kernels, body(): call(backward_kernel, 'backward', (shape((2, BLK, HDIM), F32), pltpu.HBM(...  3.62 us
  transfers between devices with their start and end apart: 15, of which 9 were waited for; matrix products, arithmetic and copies ran while one was open for 2% of the time, Pallas kernels for 1%

profile of v5, /device:TPU:1, one launch (start us, length us, event | category | flops | bytes accessed | tf_op | source)
XLA Modules:
  0.0 129.5 jit_solution(10234261994620477683)
XLA Ops:
  0.6 0.1 pad_add_fusion.place_ref
  0.7 1.4 %pack.1 = (bf16[256,128]{1,0:T(8,128)(2,1)S(1)}, bf16[2,128,128]{2,1,0:T(8,128)(2,1)S(1)}, bf16[128,128]{1,0:T(8,128)(2,1)S(1)}) custom-call(s32[4]{0:T(128)S(1)} %pad_add_fusion.place_ref, bf16[128,128]{1,0:T(8,128)(2,1)} %q_ref.3, bf16[128,128]{1,0:T(8,128)(2,1)} %k_hbm.1, bf16[128,128]{1,0:T(8,128)(2,1)} %v_hbm.1, bf16[128,256]{1,0:T(8,128)(2,1)} %grad_hbm.1), custom_call_target="tpu_custom_call" | custom-call | bytes 524288 | tf_op jit(solution)/shard_map/pack/pallas_call | solution.py:183
  2.2 8.8 %collective-permute-start = (bf16[2,128,128]{2,1,0:T(8,128)(2,1)S(1)}, bf16[2,128,128]{2,1,0:T(8,128)(2,1)S(1)}, u32[]{:S(2)}, u32[]{:S(2)}) collective-permute-start(bf16[2,128,128]{2,1,0:T(8,128)(2,1)S(1)} %get-tuple-element.37), channel_id=1, source_target_pairs={{0,1},{1,0},{2,3},{3,2},{4,5},{5,4},{6,7},{7,6},{8,9},{9,8},{10,11... | collective-permute-start | bytes 196616 | tf_op jit(solution)/shard_map/ppermute | solution.py:152
  11.0 19.1 %all_gather.3 = bf16[1024,128]{1,0:T(8,128)(2,1)S(1)} all-gather(bf16[256,128]{1,0:T(8,128)(2,1)S(1)} %get-tuple-element.36), channel_id=1, replica_groups=mesh['y'=4,'zl'=4,'zh'=4,'x'=4,'c'=2] {'zh'}, dimensions={0}, use_global_device_ids=true | all-gather | bytes 327680 | tf_op jit(solution)/shard_map/all_gather | solution.py:195
  30.1 0.0 collective-permute-done.other_ref
  30.1 0.0 copy-start.1
  30.1 1.2 broadcast_in_dim.2
  31.3 0.0 copy-start
  31.3 5.9 %all-to-all-start = ((bf16[16,256,128]{2,1,0:T(8,128)(2,1)}), bf16[16,256,128]{2,1,0:T(8,128)(2,1)S(1)}, u32[]{:S(2)}, u32[]{:S(2)}) async-start(bf16[16,256,128]{2,1,0:T(8,128)(2,1)} %broadcast_in_dim.2), calls=%async_computation | async-start | bytes 2097152 | tf_op jit(solution)/shard_map/all_to_all | solution.py:148
  37.2 4.4 %collective-permute-start.3 = (bf16[4,2,128,128]{3,2,1,0:T(8,128)(2,1)S(1)}, bf16[4,2,128,128]{3,2,1,0:T(8,128)(2,1)S(1)}, u32[]{:S(2)}, u32[]{:S(2)}) collective-permute-start(bf16[4,2,128,128]{3,2,1,0:T(8,128)(2,1)S(1)} %bitcast.28), channel_id=1, source_target_pairs={{0,6},{2,4},{4,2},{6,0},{1,7},{3,5},{5,3},{7,1},{8,14},{10,12},{12... | collective-permute-start | bytes 786440 | tf_op jit(solution)/shard_map/ppermute | solution.py:152
  41.6 2.4 %collective-permute-start.2 = (bf16[4,2,128,128]{3,2,1,0:T(8,128)(2,1)S(1)}, bf16[4,2,128,128]{3,2,1,0:T(8,128)(2,1)S(1)}, u32[]{:S(2)}, u32[]{:S(2)}) collective-permute-start(bf16[4,2,128,128]{3,2,1,0:T(8,128)(2,1)S(1)} %bitcast.29), channel_id=1, source_target_pairs={{0,4},{2,6},{4,0},{6,2},{1,5},{3,7},{5,1},{7,3},{8,12},{10,14},{12... | collective-permute-start | bytes 786440 | tf_op jit(solution)/shard_map/ppermute | solution.py:152
  44.1 2.2 %collective-permute-start.1 = (bf16[4,2,128,128]{3,2,1,0:T(8,128)(2,1)S(1)}, bf16[4,2,128,128]{3,2,1,0:T(8,128)(2,1)S(1)}, u32[]{:S(2)}, u32[]{:S(2)}) collective-permute-start(bf16[4,2,128,128]{3,2,1,0:T(8,128)(2,1)S(1)} %bitcast.30), channel_id=1, source_target_pairs={{0,2},{2,0},{4,6},{6,4},{1,3},{3,1},{5,7},{7,5},{8,10},{10,8},{12,... | collective-permute-start | bytes 786440 | tf_op jit(solution)/shard_map/ppermute | solution.py:152
  46.3 1.6 %collective-permute-done.3.kv3 = bf16[4,2,128,128]{3,2,1,0:T(8,128)(2,1)S(1)} collective-permute-done((bf16[4,2,128,128]{3,2,1,0:T(8,128)(2,1)S(1)}, bf16[4,2,128,128]{3,2,1,0:T(8,128)(2,1)S(1)}, u32[]{:S(2)}, u32[]{:S(2)}) %collective-permute-start.3) | collective-permute-done | bytes 262176 | tf_op jit(solution)/shard_map/ppermute | solution.py:152
  47.8 2.8 %collective-permute-done.2.kv2 = bf16[4,2,128,128]{3,2,1,0:T(8,128)(2,1)S(1)} collective-permute-done((bf16[4,2,128,128]{3,2,1,0:T(8,128)(2,1)S(1)}, bf16[4,2,128,128]{3,2,1,0:T(8,128)(2,1)S(1)}, u32[]{:S(2)}, u32[]{:S(2)}) %collective-permute-start.2) | collective-permute-done | bytes 262176 | tf_op jit(solution)/shard_map/ppermute | solution.py:152
  50.6 2.5 %collective-permute-done.1.kv1 = bf16[4,2,128,128]{3,2,1,0:T(8,128)(2,1)S(1)} collective-permute-done((bf16[4,2,128,128]{3,2,1,0:T(8,128)(2,1)S(1)}, bf16[4,2,128,128]{3,2,1,0:T(8,128)(2,1)S(1)}, u32[]{:S(2)}, u32[]{:S(2)}) %collective-permute-start.1) | collective-permute-done | bytes 262176 | tf_op jit(solution)/shard_map/ppermute | solution.py:152
  53.1 0.0 copy-done.1
  53.1 1.2 forward.1.part_in
  54.2 9.7 %all-to-all-done.cot_ref = bf16[16,256,128]{2,1,0:T(8,128)(2,1)S(1)} async-done(((bf16[16,256,128]{2,1,0:T(8,128)(2,1)}), bf16[16,256,128]{2,1,0:T(8,128)(2,1)S(1)}, u32[]{:S(2)}, u32[]{:S(2)}) %all-to-all-start) | async-done | bytes 1048608 | tf_op jit(solution)/shard_map/all_to_all | solution.py:148
  64.0 0.0 copy-done
  64.0 1.0 cotangent.1.mine_ref
  65.0 3.9 %collective-permute-start.4 = (f32[256,384]{1,0:T(8,128)S(1)}, f32[256,384]{1,0:T(8,128)S(1)}, u32[]{:S(2)}, u32[]{:S(2)}) collective-permute-start(f32[256,384]{1,0:T(8,128)S(1)} %cotangent.1.mine_ref), channel_id=1, source_target_pairs={{0,1},{1,0},{2,3},{3,2},{4,5},{5,4},{6,7},{7,6},{8,9},{9,8},{10,11... | collective-permute-start | bytes 1179656 | tf_op jit(solution)/shard_map/ppermute | solution.py:152
  68.9 1.3 %collective-permute-done.4.theirs_ref = f32[256,384]{1,0:T(8,128)S(1)} collective-permute-done((f32[256,384]{1,0:T(8,128)S(1)}, f32[256,384]{1,0:T(8,128)S(1)}, u32[]{:S(2)}, u32[]{:S(2)}) %collective-permute-start.4) | collective-permute-done | bytes 393248 | tf_op jit(solution)/shard_map/ppermute | solution.py:152
  70.2 3.6 %backward.1 = (f32[2,128,128]{2,1,0:T(8,128)S(1)}, bf16[4,4,3,128,128]{4,3,2,1,0:T(8,128)(2,1)}, bf16[4,128,256]{2,1,0:T(8,128)(2,1)}, bf16[4,128,256]{2,1,0:T(8...) custom-call(s32[4]{0:T(128)S(1)} %pad_add_fusion.place_ref, bf16[128,128]{1,0:T(8,128)(2,1)S(1)} %copy-done.1, ...), custom_call_target="tpu_custom_call" | custom-call | flops 939524096 | bytes 8388608 | tf_op jit(solution)/shard_map/backward/pallas_call | solution.py:222
  73.9 0.0 copy-start.5
  73.9 0.0 copy-start.4
  73.9 0.0 copy-start.2
  73.9 4.1 %all-to-all-start.1 = ((bf16[4,4,3,128,128]{4,3,2,1,0:T(8,128)(2,1)}), bf16[4,4,3,128,128]{4,3,2,1,0:T(8,128)(2,1)S(1)}, u32[]{:S(2)}, u32[]{:S(2)}) async-start(bf16[4,4,3,128,128]{4,3,2,1,0:T(8,128)(2,1)} %get-tuple-element.55), calls=%async_computation.1 | async-start | bytes 3145728 | tf_op jit(solution)/shard_map/all_to_all | solution.py:148
  78.0 0.0 copy-done.5
  78.0 1.9 %collective-permute-start.6 = (bf16[4,128,256]{2,1,0:T(8,128)(2,1)S(1)}, bf16[4,128,256]{2,1,0:T(8,128)(2,1)S(1)}, u32[]{:S(2)}, u32[]{:S(2)}) collective-permute-start(bf16[4,128,256]{2,1,0:T(8,128)(2,1)S(1)} %copy-done.5), channel_id=1, source_target_pairs={{0,32},{32,0},{64,96},{96,64},{1,33},{33,1},{65,97},{97,65},{2,34}... | collective-permute-start | bytes 786440 | tf_op jit(solution)/shard_map/ppermute | solution.py:152
  80.0 2.6 %collective-permute-start.7 = (f32[128,128]{1,0:T(8,128)S(1)}, f32[128,128]{1,0:T(8,128)S(1)}, u32[]{:S(2)}, u32[]{:S(2)}) collective-permute-start(f32[128,128]{1,0:T(8,128)S(1)} %slice_bitcast_fusion.4), channel_id=1, source_target_pairs={{0,1},{1,0},{2,3},{3,2},{4,5},{5,4},{6,7},{7,6},{8,9},{9,8},{10,11... | collective-permute-start | bytes 196616 | tf_op jit(solution)/shard_map/ppermute | solution.py:152
  82.5 0.0 copy-done.4
  82.5 3.6 %collective-permute-start.5 = (bf16[4,128,256]{2,1,0:T(8,128)(2,1)S(1)}, bf16[4,128,256]{2,1,0:T(8,128)(2,1)S(1)}, u32[]{:S(2)}, u32[]{:S(2)}) collective-permute-start(bf16[4,128,256]{2,1,0:T(8,128)(2,1)S(1)} %copy-done.4), channel_id=1, source_target_pairs={{0,32},{32,0},{64,96},{96,64},{1,33},{33,1},{65,97},{97,65},{2,34}... | collective-permute-start | bytes 786440 | tf_op jit(solution)/shard_map/ppermute | solution.py:152
  86.2 0.0 collective-permute-done.7
  86.2 0.9 collective-permute-done.6
  87.1 0.0 copy-done.2
  87.1 0.1 add_convert_fusion.2
  87.2 0.0 copy-start.3
  87.2 2.1 %collective-permute-start.8 = (bf16[4,128,256]{2,1,0:T(8,128)(2,1)S(1)}, bf16[4,128,256]{2,1,0:T(8,128)(2,1)S(1)}, u32[]{:S(2)}, u32[]{:S(2)}) collective-permute-start(bf16[4,128,256]{2,1,0:T(8,128)(2,1)S(1)} %add_convert_fusion.2), channel_id=1, source_target_pairs={{0,64},{32,96},{64,0},{96,32},{1,65},{33,97},{65,1},{97,33},{2,66}... | collective-permute-start | bytes 786440 | tf_op jit(solution)/shard_map/ppermute | solution.py:152
  89.2 8.9 %all-to-all-done.1 = bf16[4,4,3,128,128]{4,3,2,1,0:T(8,128)(2,1)S(1)} async-done(((bf16[4,4,3,128,128]{4,3,2,1,0:T(8,128)(2,1)}), bf16[4,4,3,128,128]{4,3,2,1,0:T(8,128)(2,1)S(1)}, u32[]{:S(2)}, u32[]{:S(2)}) %all-to-all-start.1) | async-done | bytes 1572896 | tf_op jit(solution)/shard_map/all_to_all | solution.py:148
  98.2 1.0 fusion
  99.1 6.4 %all-to-all-start.2 = ((bf16[4,3,128,128]{3,2,1,0:T(8,128)(2,1)}), bf16[4,3,128,128]{3,2,1,0:T(8,128)(2,1)S(1)}, u32[]{:S(2)}, u32[]{:S(2)}) async-start(bf16[4,3,128,128]{3,2,1,0:T(8,128)(2,1)} %fusion), calls=%async_computation.2 | async-start | bytes 786432 | tf_op jit(solution)/shard_map/all_to_all | solution.py:148
  105.6 0.0 collective-permute-done.5
  105.6 0.0 collective-permute-done.8
  105.6 0.0 copy-done.3
  105.6 0.1 add_convert_fusion.1
  105.7 1.9 %collective-permute-start.9 = (bf16[128,256]{1,0:T(8,128)(2,1)S(1)}, bf16[128,256]{1,0:T(8,128)(2,1)S(1)}, u32[]{:S(2)}, u32[]{:S(2)}) collective-permute-start(bf16[128,256]{1,0:T(8,128)(2,1)S(1)} %get-tuple-element.59), channel_id=1, source_target_pairs={{0,128},{128,0},{256,384},{384,256},{1,129},{129,1},{257,385},{385... | collective-permute-start | bytes 196616 | tf_op jit(solution)/shard_map/ppermute | solution.py:152
  107.7 2.8 %collective-permute-start.11 = (bf16[128,256]{1,0:T(8,128)(2,1)S(1)}, bf16[128,256]{1,0:T(8,128)(2,1)S(1)}, u32[]{:S(2)}, u32[]{:S(2)}) collective-permute-start(bf16[128,256]{1,0:T(8,128)(2,1)S(1)} %get-tuple-element.60), channel_id=1, source_target_pairs={{0,384},{128,256},{256,128},{384,0},{1,385},{129,257},{257,129},{3... | collective-permute-start | bytes 196616 | tf_op jit(solution)/shard_map/ppermute | solution.py:152
  110.4 4.3 %collective-permute-start.10 = (bf16[128,256]{1,0:T(8,128)(2,1)S(1)}, bf16[128,256]{1,0:T(8,128)(2,1)S(1)}, u32[]{:S(2)}, u32[]{:S(2)}) collective-permute-start(bf16[128,256]{1,0:T(8,128)(2,1)S(1)} %get-tuple-element.61), channel_id=1, source_target_pairs={{0,256},{128,384},{256,0},{384,128},{1,257},{129,385},{257,1},{385... | collective-permute-start | bytes 196616 | tf_op jit(solution)/shard_map/ppermute | solution.py:152
  114.7 0.6 fusion.5
  115.4 0.0 collective-permute-done.9
  115.4 0.0 collective-permute-done.11
  115.4 1.6 %collective-permute-done.10 = bf16[128,256]{1,0:T(8,128)(2,1)S(1)} collective-permute-done((bf16[128,256]{1,0:T(8,128)(2,1)S(1)}, bf16[128,256]{1,0:T(8,128)(2,1)S(1)}, u32[]{:S(2)}, u32[]{:S(2)}) %collective-permute-start.10) | collective-permute-done | bytes 65568 | tf_op jit(solution)/shard_map/ppermute | solution.py:152
  116.9 0.7 fusion.3
  117.6 11.1 %all-to-all-done.2.parts_ref = bf16[4,3,128,128]{3,2,1,0:T(8,128)(2,1)S(1)} async-done(((bf16[4,3,128,128]{3,2,1,0:T(8,128)(2,1)}), bf16[4,3,128,128]{3,2,1,0:T(8,128)(2,1)S(1)}, u32[]{:S(2)}, u32[]{:S(2)}) %all-to-all-start.2) | async-done | bytes 393248 | tf_op jit(solution)/shard_map/all_to_all | solution.py:148
  128.7 0.8 finish.1
  (4 shorter events, 0.0 us)
Async XLA Ops:
  2.2 27.9 %collective-permute-start = (bf16[2,128,128]{2,1,0:T(8,128)(2,1)S(1)}, bf16[2,128,128]{2,1,0:T(8,128)(2,1)S(1)}, u32[]{:S(2)}, u32[]{:S(2)}) collective-permute-start(bf16[2,128,128]{2,1,0:T(8,128)(2,1)S(1)} %get-tuple-element.37), channel_id=1, source_target_pairs={{0,1},{1,0},{2,3},{3,2},{4,5},{5,4},{6,7},{7,6},{8,9},{9,8},{10,11... | collective-permute-start | bytes 196616 | tf_op jit(solution)/shard_map/ppermute | solution.py:152
  30.1 23.0 %copy-start.1 = (bf16[128,128]{1,0:T(8,128)(2,1)S(1)}, bf16[128,128]{1,0:T(8,128)(2,1)}, u32[]{:S(2)}) copy-start(bf16[128,128]{1,0:T(8,128)(2,1)} %q_ref.3) | copy-start | bytes 98308
  31.3 32.6 %copy-start = (bf16[128,4096]{1,0:T(8,128)(2,1)S(1)}, bf16[128,4096]{1,0:T(8,128)(2,1)}, u32[]{:S(2)}) copy-start(bf16[128,4096]{1,0:T(8,128)(2,1)} %w_ref.3) | copy-start | bytes 3145732
  31.3 32.6 %all-to-all-start = ((bf16[16,256,128]{2,1,0:T(8,128)(2,1)}), bf16[16,256,128]{2,1,0:T(8,128)(2,1)S(1)}, u32[]{:S(2)}, u32[]{:S(2)}) async-start(bf16[16,256,128]{2,1,0:T(8,128)(2,1)} %broadcast_in_dim.2), calls=%async_computation | async-start | bytes 2097152 | tf_op jit(solution)/shard_map/all_to_all | solution.py:148
  37.2 10.6 %collective-permute-start.3 = (bf16[4,2,128,128]{3,2,1,0:T(8,128)(2,1)S(1)}, bf16[4,2,128,128]{3,2,1,0:T(8,128)(2,1)S(1)}, u32[]{:S(2)}, u32[]{:S(2)}) collective-permute-start(bf16[4,2,128,128]{3,2,1,0:T(8,128)(2,1)S(1)} %bitcast.28), channel_id=1, source_target_pairs={{0,6},{2,4},{4,2},{6,0},{1,7},{3,5},{5,3},{7,1},{8,14},{10,12},{12... | collective-permute-start | bytes 786440 | tf_op jit(solution)/shard_map/ppermute | solution.py:152
  41.6 9.0 %collective-permute-start.2 = (bf16[4,2,128,128]{3,2,1,0:T(8,128)(2,1)S(1)}, bf16[4,2,128,128]{3,2,1,0:T(8,128)(2,1)S(1)}, u32[]{:S(2)}, u32[]{:S(2)}) collective-permute-start(bf16[4,2,128,128]{3,2,1,0:T(8,128)(2,1)S(1)} %bitcast.29), channel_id=1, source_target_pairs={{0,4},{2,6},{4,0},{6,2},{1,5},{3,7},{5,1},{7,3},{8,12},{10,14},{12... | collective-permute-start | bytes 786440 | tf_op jit(solution)/shard_map/ppermute | solution.py:152
  44.1 9.0 %collective-permute-start.1 = (bf16[4,2,128,128]{3,2,1,0:T(8,128)(2,1)S(1)}, bf16[4,2,128,128]{3,2,1,0:T(8,128)(2,1)S(1)}, u32[]{:S(2)}, u32[]{:S(2)}) collective-permute-start(bf16[4,2,128,128]{3,2,1,0:T(8,128)(2,1)S(1)} %bitcast.30), channel_id=1, source_target_pairs={{0,2},{2,0},{4,6},{6,4},{1,3},{3,1},{5,7},{7,5},{8,10},{10,8},{12,... | collective-permute-start | bytes 786440 | tf_op jit(solution)/shard_map/ppermute | solution.py:152
  65.0 5.2 %collective-permute-start.4 = (f32[256,384]{1,0:T(8,128)S(1)}, f32[256,384]{1,0:T(8,128)S(1)}, u32[]{:S(2)}, u32[]{:S(2)}) collective-permute-start(f32[256,384]{1,0:T(8,128)S(1)} %cotangent.1.mine_ref), channel_id=1, source_target_pairs={{0,1},{1,0},{2,3},{3,2},{4,5},{5,4},{6,7},{7,6},{8,9},{9,8},{10,11... | collective-permute-start | bytes 1179656 | tf_op jit(solution)/shard_map/ppermute | solution.py:152
  73.9 4.2 %copy-start.5 = (bf16[4,128,256]{2,1,0:T(8,128)(2,1)S(1)}, bf16[4,128,256]{2,1,0:T(8,128)(2,1)}, u32[]{:S(2)}) copy-start(bf16[4,128,256]{2,1,0:T(8,128)(2,1)} %get-tuple-element.51) | copy-start | bytes 786436
  73.9 8.7 %copy-start.4 = (bf16[4,128,256]{2,1,0:T(8,128)(2,1)S(1)}, bf16[4,128,256]{2,1,0:T(8,128)(2,1)}, u32[]{:S(2)}) copy-start(bf16[4,128,256]{2,1,0:T(8,128)(2,1)} %get-tuple-element.49) | copy-start | bytes 786436
  73.9 13.2 %copy-start.2 = (bf16[4,128,256]{2,1,0:T(8,128)(2,1)S(1)}, bf16[4,128,256]{2,1,0:T(8,128)(2,1)}, u32[]{:S(2)}) copy-start(bf16[4,128,256]{2,1,0:T(8,128)(2,1)} %get-tuple-element.50) | copy-start | bytes 786436
  73.9 24.3 %all-to-all-start.1 = ((bf16[4,4,3,128,128]{4,3,2,1,0:T(8,128)(2,1)}), bf16[4,4,3,128,128]{4,3,2,1,0:T(8,128)(2,1)S(1)}, u32[]{:S(2)}, u32[]{:S(2)}) async-start(bf16[4,4,3,128,128]{4,3,2,1,0:T(8,128)(2,1)} %get-tuple-element.55), calls=%async_computation.1 | async-start | bytes 3145728 | tf_op jit(solution)/shard_map/all_to_all | solution.py:148
  78.0 9.1 %collective-permute-start.6 = (bf16[4,128,256]{2,1,0:T(8,128)(2,1)S(1)}, bf16[4,128,256]{2,1,0:T(8,128)(2,1)S(1)}, u32[]{:S(2)}, u32[]{:S(2)}) collective-permute-start(bf16[4,128,256]{2,1,0:T(8,128)(2,1)S(1)} %copy-done.5), channel_id=1, source_target_pairs={{0,32},{32,0},{64,96},{96,64},{1,33},{33,1},{65,97},{97,65},{2,34}... | collective-permute-start | bytes 786440 | tf_op jit(solution)/shard_map/ppermute | solution.py:152
  80.0 6.2 %collective-permute-start.7 = (f32[128,128]{1,0:T(8,128)S(1)}, f32[128,128]{1,0:T(8,128)S(1)}, u32[]{:S(2)}, u32[]{:S(2)}) collective-permute-start(f32[128,128]{1,0:T(8,128)S(1)} %slice_bitcast_fusion.4), channel_id=1, source_target_pairs={{0,1},{1,0},{2,3},{3,2},{4,5},{5,4},{6,7},{7,6},{8,9},{9,8},{10,11... | collective-permute-start | bytes 196616 | tf_op jit(solution)/shard_map/ppermute | solution.py:152
  82.5 23.0 %collective-permute-start.5 = (bf16[4,128,256]{2,1,0:T(8,128)(2,1)S(1)}, bf16[4,128,256]{2,1,0:T(8,128)(2,1)S(1)}, u32[]{:S(2)}, u32[]{:S(2)}) collective-permute-start(bf16[4,128,256]{2,1,0:T(8,128)(2,1)S(1)} %copy-done.4), channel_id=1, source_target_pairs={{0,32},{32,0},{64,96},{96,64},{1,33},{33,1},{65,97},{97,65},{2,34}... | collective-permute-start | bytes 786440 | tf_op jit(solution)/shard_map/ppermute | solution.py:152
  87.2 18.4 %copy-start.3 = (bf16[4,128,256]{2,1,0:T(8,128)(2,1)S(1)}, bf16[4,128,256]{2,1,0:T(8,128)(2,1)}, u32[]{:S(2)}) copy-start(bf16[4,128,256]{2,1,0:T(8,128)(2,1)} %get-tuple-element.48) | copy-start | bytes 786436
  87.2 18.4 %collective-permute-start.8 = (bf16[4,128,256]{2,1,0:T(8,128)(2,1)S(1)}, bf16[4,128,256]{2,1,0:T(8,128)(2,1)S(1)}, u32[]{:S(2)}, u32[]{:S(2)}) collective-permute-start(bf16[4,128,256]{2,1,0:T(8,128)(2,1)S(1)} %add_convert_fusion.2), channel_id=1, source_target_pairs={{0,64},{32,96},{64,0},{96,32},{1,65},{33,97},{65,1},{97,33},{2,66}... | collective-permute-start | bytes 786440 | tf_op jit(solution)/shard_map/ppermute | solution.py:152
  99.1 29.6 %all-to-all-start.2 = ((bf16[4,3,128,128]{3,2,1,0:T(8,128)(2,1)}), bf16[4,3,128,128]{3,2,1,0:T(8,128)(2,1)S(1)}, u32[]{:S(2)}, u32[]{:S(2)}) async-start(bf16[4,3,128,128]{3,2,1,0:T(8,128)(2,1)} %fusion), calls=%async_computation.2 | async-start | bytes 786432 | tf_op jit(solution)/shard_map/all_to_all | solution.py:148
  105.7 9.6 %collective-permute-start.9 = (bf16[128,256]{1,0:T(8,128)(2,1)S(1)}, bf16[128,256]{1,0:T(8,128)(2,1)S(1)}, u32[]{:S(2)}, u32[]{:S(2)}) collective-permute-start(bf16[128,256]{1,0:T(8,128)(2,1)S(1)} %get-tuple-element.59), channel_id=1, source_target_pairs={{0,128},{128,0},{256,384},{384,256},{1,129},{129,1},{257,385},{385... | collective-permute-start | bytes 196616 | tf_op jit(solution)/shard_map/ppermute | solution.py:152
  107.7 7.7 %collective-permute-start.11 = (bf16[128,256]{1,0:T(8,128)(2,1)S(1)}, bf16[128,256]{1,0:T(8,128)(2,1)S(1)}, u32[]{:S(2)}, u32[]{:S(2)}) collective-permute-start(bf16[128,256]{1,0:T(8,128)(2,1)S(1)} %get-tuple-element.60), channel_id=1, source_target_pairs={{0,384},{128,256},{256,128},{384,0},{1,385},{129,257},{257,129},{3... | collective-permute-start | bytes 196616 | tf_op jit(solution)/shard_map/ppermute | solution.py:152
  110.4 6.5 %collective-permute-start.10 = (bf16[128,256]{1,0:T(8,128)(2,1)S(1)}, bf16[128,256]{1,0:T(8,128)(2,1)S(1)}, u32[]{:S(2)}, u32[]{:S(2)}) collective-permute-start(bf16[128,256]{1,0:T(8,128)(2,1)S(1)} %get-tuple-element.61), channel_id=1, source_target_pairs={{0,256},{128,384},{256,0},{384,128},{1,257},{129,385},{257,1},{385... | collective-permute-start | bytes 196616 | tf_op jit(solution)/shard_map/ppermute | solution.py:152

commit v6 on v5

--- a/solution.py
+++ b/solution.py
@@ -21,45 +21,31 @@
     return lax.dot_general(a, b, (dims, ((), ())), preferred_element_type=F32)
 
 
-def pack_kernel(place_ref, q_hbm, k_hbm, v_hbm, grad_hbm, kv_ref, gift_ref, mine_ref, grad_ref, sems):
+def pack_kernel(k_hbm, v_hbm, grad_hbm, kv_ref, grad_ref, sems):
     copies = [
-        pltpu.make_async_copy(grad_hbm, grad_ref, sems.at[0]),
-        pltpu.make_async_copy(q_hbm, gift_ref.at[0], sems.at[1]),
-        pltpu.make_async_copy(k_hbm, kv_ref.at[pl.ds(0, BLK)], sems.at[2]),
-        pltpu.make_async_copy(v_hbm, kv_ref.at[pl.ds(BLK, BLK)], sems.at[3]),
+        pltpu.make_async_copy(grad_hbm, grad_ref, sems.at[2]),
+        pltpu.make_async_copy(k_hbm, kv_ref.at[pl.ds(0, BLK)], sems.at[0]),
+        pltpu.make_async_copy(v_hbm, kv_ref.at[pl.ds(BLK, BLK)], sems.at[1]),
     ]
     for copy in copies:
         copy.start()
     for copy in copies:
         copy.wait()
-    first = place_ref[0] == 0
-    left, right = grad_ref[:, :BLK], grad_ref[:, BLK:]
-    mine_ref[...] = jnp.where(first, left, right)
-    gift_ref[1] = jnp.where(first, right, left)
-
-
-def copies_kernel(mine_ref, other_ref, cot_hbm, pair_ref, sems):
-    pair_ref[:BLK] = mine_ref[...]
-    pair_ref[BLK:] = other_ref[1]
-    copies = [pltpu.make_async_copy(pair_ref, cot_hbm.at[o], sems.at[o]) for o in range(16)]
-    for copy in copies:
-        copy.start()
-    for copy in copies:
-        copy.wait()
-
-
-def cotangent_kernel(place_ref, w_ref, cot_ref, part_in, part_ref):
-    grad = jnp.zeros((2 * BLK, HDIM), F32)
+
+
+def cotangent_kernel(place_ref, w_ref, cot_ref, gift_ref):
+    core = place_ref[0]
+    grad = jnp.zeros((BLK, HDIM), F32)
     for o in range(16):
-        start = pl.multiple_of(o * 256 + place_ref[0] * BLK, BLK)
-        grad = grad + dot(cot_ref[o], w_ref[:, pl.ds(start, BLK)], ((1,), (1,)))
-    part_ref[:, :HDIM] = grad
-    part_ref[:, HDIM:] = part_in[...]
+        cot = cot_ref[o]
+        grad = grad + dot(cot, w_ref[:, o * 256 : (o + 1) * 256], ((1,), (1,)))
+        gift_ref[1 + o] = jnp.where(core == 0, cot[:, BLK:], cot[:, :BLK])
+    gift_ref[0] = grad.astype(BF16)
 
 
 def forward_kernel(q_ref, other_ref, kv0, kv1, kv2, kv3, part_ref, s_ref):
     pieces = (kv0, kv1, kv2, kv3)
-    q = jnp.concatenate([q_ref[...], other_ref[0]], axis=0)
+    q = jnp.concatenate([q_ref[...], other_ref[...]], axis=0)
     top = jnp.full((2 * BLK, BLK), -jnp.inf, F32)
     for j in range(4):
         k = pieces[j][:, 0].reshape(WIDTH, HDIM)
@@ -81,25 +67,27 @@
     part_ref[:, HDIM:] = jnp.broadcast_to(row_max + jnp.log(totals), (2 * BLK, BLK))
 
 
-def merged(mine_ref, theirs_ref, half):
+def merged(grad, mine_ref, theirs_ref, half):
     rows = slice(half * BLK, (half + 1) * BLK)
     swapped = slice((1 - half) * BLK, (2 - half) * BLK)
-    grad = (mine_ref[rows, :HDIM] + theirs_ref[swapped, :HDIM]).astype(BF16)
-    a, b = mine_ref[rows, 2 * HDIM :], theirs_ref[swapped, 2 * HDIM :]
+    a, b = mine_ref[rows, HDIM:], theirs_ref[swapped, HDIM:]
     top = jnp.maximum(a, b)
     lse = top + jnp.log(jnp.exp(a - top) + jnp.exp(b - top))
-    attn = mine_ref[rows, HDIM : 2 * HDIM] * jnp.exp(a - lse)
-    attn = (attn + theirs_ref[swapped, HDIM : 2 * HDIM] * jnp.exp(b - lse)).astype(BF16)
+    attn = mine_ref[rows, :HDIM] * jnp.exp(a - lse)
+    attn = (attn + theirs_ref[swapped, :HDIM] * jnp.exp(b - lse)).astype(BF16)
     dots = jnp.sum(grad.astype(F32) * attn.astype(F32), axis=1, keepdims=True)
     return grad, attn, lse[:, :1], dots
 
 
 def backward_kernel(
-    place_ref, q_ref, other_ref, kv0, kv1, kv2, kv3, cot_ref, w_ref, mine_ref, theirs_ref, *refs
+    place_ref, q_ref, other_ref, kv0, kv1, kv2, kv3, cot_ref, w_ref, gift_ref, got_ref, mine_ref, theirs_ref, *refs
 ):
     pieces = (kv0, kv1, kv2, kv3)
     dq_ref, pay_hbm, *out_hbm, pay_ref, out_ref, sems = refs
-    halves = [merged(mine_ref, theirs_ref, half) for half in range(2)]
+    halves = [
+        merged(ref[0], mine_ref, theirs_ref, half) for half, ref in enumerate((gift_ref, got_ref))
+    ]
+    mine = pl.ds(pl.multiple_of(place_ref[0] * BLK, BLK), BLK)
     grad, attn, lse, dots = (jnp.concatenate(pair, axis=0) for pair in zip(*halves))
     copies = []
     for r in range(4):
@@ -109,7 +97,7 @@
             out_ref[r, t] = dot(halves[0][1], w_ref[:, cols]).astype(BF16)
         copies.append(pltpu.make_async_copy(out_ref.at[r], out_hbm[r], sems.at[r]))
         copies[r].start()
-    q = jnp.concatenate([q_ref[...], other_ref[0]], axis=0)
+    q = jnp.concatenate([q_ref[...], other_ref[...]], axis=0)
     q_t = q.T
     grad_t = grad.T
     attn_t = attn.T
@@ -128,7 +116,9 @@
         for z in range(4):
             pay_ref[j, z, 0] = dk_t[:, z * BLK : (z + 1) * BLK]
             pay_ref[j, z, 1] = dv_t[:, z * BLK : (z + 1) * BLK]
-            pay_ref[j, z, 2] = dot(attn_t, cot_ref[z * 4 + x]).astype(BF16)
+            o = z * 4 + x
+            cot = jnp.concatenate([cot_ref[o, :, mine], got_ref[1 + o]], axis=0)
+            pay_ref[j, z, 2] = dot(attn_t, cot).astype(BF16)
         copies.append(pltpu.make_async_copy(pay_ref.at[j], pay_hbm.at[x], sems.at[4 + j]))
         copies[4 + j].start()
     dq_ref[0] = dq[:BLK]
@@ -180,22 +170,20 @@
     unit = BLK * BLK * 4096
     tile = shape((BLK, BLK), BF16)
     place = jnp.stack([lax.axis_index(a) for a in ("c", "x", "y", "zl")]).astype(jnp.int32)
-    kv, gift, mine = call(
+    kv, cot = call(
         pack_kernel,
         "pack",
-        (shape((2 * BLK, HDIM), BF16), shape((2, BLK, BLK), BF16), tile),
-        [SMEM] + [HBM] * 4,
+        (shape((2 * BLK, HDIM), BF16), shape((BLK, 2 * BLK), BF16)),
+        [HBM] * 3,
         4,
         0,
-        1 << 19,
-        scratch=[pltpu.VMEM((BLK, 2 * BLK), BF16), pltpu.SemaphoreType.DMA((4,))],
-    )(place, *[in_hbm(block) for block in (queries, keys, values, grad_out)])
-    place, kv, gift, mine = lax.optimization_barrier((place, kv, gift, mine))
+        1 << 18,
+        scratch=[pltpu.SemaphoreType.DMA((3,))],
+    )(in_hbm(keys), in_hbm(values), in_hbm(grad_out))
+    kv = lax.all_gather(kv, "zh", axis=0, tiled=True).reshape(4, 2, BLK, HDIM)
+    kv, gift, cot, place = lax.optimization_barrier((kv, queries, cot, place))
+    cot = exchange(jnp.broadcast_to(cot[None], (16, BLK, 2 * BLK)), ("y", "zl"))
     other = trade(gift, "c", 1)
-    kv = lax.all_gather(kv, "zh", axis=0, tiled=True).reshape(4, 2, BLK, HDIM)
-    kv, other = lax.optimization_barrier((kv, other))
-    cot = jnp.concatenate([mine, other[1]], axis=0)
-    cot = exchange(jnp.broadcast_to(cot[None], (16, 2 * BLK, BLK)), ("y", "zl"))
     pieces = [kv] + [trade(kv, "x", r) for r in (1, 2, 3)]
     part = call(
         forward_kernel,
@@ -208,23 +196,24 @@
         unit // BLK,
         [pltpu.VMEM((2 * BLK, 16 * BLK), F32)],
     )(queries, other, *pieces)
-    cot, part = lax.optimization_barrier((cot, part))
-    part = call(
+    theirs = trade(part, "c", 1)
+    cot, theirs = lax.optimization_barrier((cot, theirs))
+    gift = call(
         cotangent_kernel,
         "cotangent",
-        shape((2 * BLK, 3 * BLK), F32),
-        [SMEM] + [VMEM] * 3,
+        shape((17, BLK, BLK), BF16),
+        [SMEM] + [VMEM] * 2,
         8,
         2 * unit,
         2 << 20,
-    )(place, w_out, cot, part)
-    theirs = trade(part, "c", 1)
+    )(place, w_out, cot)
+    got = trade(gift, "c", 1)
     dq, pay, *outs = call(
         backward_kernel,
         "backward",
         (shape((2, BLK, HDIM), F32), pltpu.HBM((4, 4, 3, BLK, BLK), BF16))
         + (pltpu.HBM((4, BLK, 256), BF16),) * 4,
-        [SMEM] + [VMEM] * 10,
+        [SMEM] + [VMEM] * 12,
         12,
         14 * unit,
         8 << 20,
@@ -235,7 +224,7 @@
             pltpu.SemaphoreType.DMA((8,)),
         ],
         (VMEM,) + (HBM,) * 5,
-    )(place, queries, other, *pieces, cot, w_out, part, theirs)
+    )(place, queries, other, *pieces, cot, w_out, gift, got, part, theirs)
     pay, *outs = lax.optimization_barrier((pay, *outs))
     pay = exchange(pay, "x")
     passing = trade(outs[3], "zl", 1)

time: 130 us -> 127 us (0.977)
  the two profiles are of different devices: /device:TPU:1 before, /device:TPU:32 now
where the time goes in v6:
time: 127 us; the launch traced here: 126 us
  starting transfers between devices  55.8 us (44%)
  waiting for transfers between devices  31.2 us (25%)
  blocking collectives  26 us (20%)
  Pallas kernels  7.43 us (6%)
  other arithmetic  2.51 us (2%)
  local copies, waits for them, and re-layouts  2.48 us (2%)
    ppermute x13, starting transfers between devices, trade(): lax.ppermute(block, axis, [(i, i ^ step) for i in range(2 if axis == 'c'...  37.6 us
    all_gather x1, blocking collectives, body(): kv = lax.all_gather(kv, 'zh', axis=0, tiled=True).reshape(4, 2, BLK, HDIM)  26 us
    all_to_all x3, starting transfers between devices, exchange(): return lax.all_to_all(blocks, axis, 0, 0, tiled=True)  18.3 us
    all_to_all x3, waiting for transfers between devices, exchange(): return lax.all_to_all(blocks, axis, 0, 0, tiled=True)  16.5 us
    ppermute x13, waiting for transfers between devices, trade(): lax.ppermute(block, axis, [(i, i ^ step) for i in range(2 if axis == 'c'...  14.7 us
    pallas_call x1, Pallas kernels, body(): call(backward_kernel, 'backward', (shape((2, BLK, HDIM), F32), pltpu.HBM(...  3.62 us
  transfers between devices with their start and end apart: 16, of which 10 were waited for; matrix products, arithmetic and copies ran while one was open for 2% of the time, Pallas kernels for 1%

profile of v6, /device:TPU:32, one launch (start us, length us, event | category | flops | bytes accessed | tf_op | source)
XLA Modules:
  0.0 126.3 jit_solution(420726889183858705)
XLA Ops:
  0.6 0.9 pack.1
  1.5 26.0 %all_gather.3 = bf16[1024,128]{1,0:T(8,128)(2,1)S(1)} all-gather(bf16[256,128]{1,0:T(8,128)(2,1)S(1)} %get-tuple-element.29), channel_id=1, replica_groups=mesh['y'=4,'zl'=4,'zh'=4,'x'=4,'c'=2] {'zh'}, dimensions={0}, use_global_device_ids=true | all-gather | bytes 327680 | tf_op jit(solution)/shard_map/all_gather | solution.py:183
  27.5 0.1 pad_add_fusion.place_ref
  27.6 0.0 copy-start.3
  27.6 1.1 broadcast_in_dim.2
  28.7 0.0 copy-start
  28.7 7.4 %all-to-all-start = ((bf16[16,128,256]{2,1,0:T(8,128)(2,1)}), bf16[16,128,256]{2,1,0:T(8,128)(2,1)S(1)}, u32[]{:S(2)}, u32[]{:S(2)}) async-start(bf16[16,128,256]{2,1,0:T(8,128)(2,1)} %broadcast_in_dim.2), calls=%async_computation | async-start | bytes 2097152 | tf_op jit(solution)/shard_map/all_to_all | solution.py:138
  36.0 4.7 %collective-permute-start.3 = (bf16[4,2,128,128]{3,2,1,0:T(8,128)(2,1)S(1)}, bf16[4,2,128,128]{3,2,1,0:T(8,128)(2,1)S(1)}, u32[]{:S(2)}, u32[]{:S(2)}) collective-permute-start(bf16[4,2,128,128]{3,2,1,0:T(8,128)(2,1)S(1)} %bitcast.26), channel_id=1, source_target_pairs={{0,6},{2,4},{4,2},{6,0},{1,7},{3,5},{5,3},{7,1},{8,14},{10,12},{12... | collective-permute-start | bytes 786440 | tf_op jit(solution)/shard_map/ppermute | solution.py:142
  40.7 2.7 %collective-permute-start.2 = (bf16[4,2,128,128]{3,2,1,0:T(8,128)(2,1)S(1)}, bf16[4,2,128,128]{3,2,1,0:T(8,128)(2,1)S(1)}, u32[]{:S(2)}, u32[]{:S(2)}) collective-permute-start(bf16[4,2,128,128]{3,2,1,0:T(8,128)(2,1)S(1)} %bitcast.27), channel_id=1, source_target_pairs={{0,4},{2,6},{4,0},{6,2},{1,5},{3,7},{5,1},{7,3},{8,12},{10,14},{12... | collective-permute-start | bytes 786440 | tf_op jit(solution)/shard_map/ppermute | solution.py:142
  43.4 2.4 %collective-permute-start.1 = (bf16[4,2,128,128]{3,2,1,0:T(8,128)(2,1)S(1)}, bf16[4,2,128,128]{3,2,1,0:T(8,128)(2,1)S(1)}, u32[]{:S(2)}, u32[]{:S(2)}) collective-permute-start(bf16[4,2,128,128]{3,2,1,0:T(8,128)(2,1)S(1)} %bitcast.28), channel_id=1, source_target_pairs={{0,2},{2,0},{4,6},{6,4},{1,3},{3,1},{5,7},{7,5},{8,10},{10,8},{12,... | collective-permute-start | bytes 786440 | tf_op jit(solution)/shard_map/ppermute | solution.py:142
  45.9 0.0 copy-done.3
  45.9 1.9 %collective-permute-start = (bf16[128,128]{1,0:T(8,128)(2,1)S(1)}, bf16[128,128]{1,0:T(8,128)(2,1)S(1)}, u32[]{:S(2)}, u32[]{:S(2)}) collective-permute-start(bf16[128,128]{1,0:T(8,128)(2,1)S(1)} %copy-done.3), channel_id=1, source_target_pairs={{0,1},{1,0},{2,3},{3,2},{4,5},{5,4},{6,7},{7,6},{8,9},{9,8},{10,11... | collective-permute-start | bytes 98312 | tf_op jit(solution)/shard_map/ppermute | solution.py:142
  47.8 1.2 collective-permute-done.other_ref
  49.0 0.0 collective-permute-done.3.kv3
  49.0 2.4 %collective-permute-done.2.kv2 = bf16[4,2,128,128]{3,2,1,0:T(8,128)(2,1)S(1)} collective-permute-done((bf16[4,2,128,128]{3,2,1,0:T(8,128)(2,1)S(1)}, bf16[4,2,128,128]{3,2,1,0:T(8,128)(2,1)S(1)}, u32[]{:S(2)}, u32[]{:S(2)}) %collective-permute-start.2) | collective-permute-done | bytes 262176 | tf_op jit(solution)/shard_map/ppermute | solution.py:142
  51.3 0.9 collective-permute-done.1.kv1
  52.3 1.2 forward.1.mine_ref
  53.5 1.9 %collective-permute-start.4 = (f32[256,256]{1,0:T(8,128)S(1)}, f32[256,256]{1,0:T(8,128)S(1)}, u32[]{:S(2)}, u32[]{:S(2)}) collective-permute-start(f32[256,256]{1,0:T(8,128)S(1)} %forward.1.mine_ref), channel_id=1, source_target_pairs={{0,1},{1,0},{2,3},{3,2},{4,5},{5,4},{6,7},{7,6},{8,9},{9,8},{10,11... | collective-permute-start | bytes 786440 | tf_op jit(solution)/shard_map/ppermute | solution.py:142
  55.4 1.5 %collective-permute-done.4.theirs_ref = f32[256,256]{1,0:T(8,128)S(1)} collective-permute-done((f32[256,256]{1,0:T(8,128)S(1)}, f32[256,256]{1,0:T(8,128)S(1)}, u32[]{:S(2)}, u32[]{:S(2)}) %collective-permute-start.4) | collective-permute-done | bytes 262176 | tf_op jit(solution)/shard_map/ppermute | solution.py:142
  56.9 0.0 copy-start.1
  56.9 0.7 copy-done.1
  57.6 0.0 all-to-all-done.cot_ref
  57.6 0.0 copy-done
  57.6 0.0 copy-start.2
  57.6 1.0 cotangent.1.gift_ref
  58.6 2.0 %collective-permute-start.5 = (bf16[17,128,128]{2,1,0:T(8,128)(2,1)S(1)}, bf16[17,128,128]{2,1,0:T(8,128)(2,1)S(1)}, u32[]{:S(2)}, u32[]{:S(2)}) collective-permute-start(bf16[17,128,128]{2,1,0:T(8,128)(2,1)S(1)} %cotangent.1.gift_ref), channel_id=1, source_target_pairs={{0,1},{1,0},{2,3},{3,2},{4,5},{5,4},{6,7},{7,6},{8,9},{9,8},{10,11... | collective-permute-start | bytes 1671176 | tf_op jit(solution)/shard_map/ppermute | solution.py:142
  60.6 1.8 %collective-permute-done.5.got_ref = bf16[17,128,128]{2,1,0:T(8,128)(2,1)S(1)} collective-permute-done((bf16[17,128,128]{2,1,0:T(8,128)(2,1)S(1)}, bf16[17,128,128]{2,1,0:T(8,128)(2,1)S(1)}, u32[]{:S(2)}, u32[]{:S(2)}) %collective-permute-start.5) | collective-permute-done | bytes 557088 | tf_op jit(solution)/shard_map/ppermute | solution.py:142
  62.5 0.0 copy-done.2
  62.5 3.6 %backward.1 = (f32[2,128,128]{2,1,0:T(8,128)S(1)}, bf16[4,4,3,128,128]{4,3,2,1,0:T(8,128)(2,1)}, bf16[4,128,256]{2,1,0:T(8,128)(2,1)}, bf16[4,128,256]{2,1,0:T(8...) custom-call(s32[4]{0:T(128)S(1)} %pad_add_fusion.place_ref, bf16[128,128]{1,0:T(8,128)(2,1)S(1)} %copy-done.3, ...), custom_call_target="tpu_custom_call" | custom-call | flops 939524096 | bytes 8388608 | tf_op jit(solution)/shard_map/backward/pallas_call | solution.py:211
  66.1 0.0 copy-start.4
  66.1 0.6 copy-done.4
  66.7 0.0 copy-start.9
  66.7 0.0 copy-start.5
  66.7 0.0 copy-start.8
  66.7 4.1 %all-to-all-start.1 = ((bf16[4,4,3,128,128]{4,3,2,1,0:T(8,128)(2,1)}), bf16[4,4,3,128,128]{4,3,2,1,0:T(8,128)(2,1)S(1)}, u32[]{:S(2)}, u32[]{:S(2)}) async-start(bf16[4,4,3,128,128]{4,3,2,1,0:T(8,128)(2,1)} %get-tuple-element.49), calls=%async_computation.1 | async-start | bytes 3145728 | tf_op jit(solution)/shard_map/all_to_all | solution.py:138
  70.9 0.0 copy-done.9
  70.9 5.7 %collective-permute-start.7 = (bf16[4,128,256]{2,1,0:T(8,128)(2,1)S(1)}, bf16[4,128,256]{2,1,0:T(8,128)(2,1)S(1)}, u32[]{:S(2)}, u32[]{:S(2)}) collective-permute-start(bf16[4,128,256]{2,1,0:T(8,128)(2,1)S(1)} %copy-done.9), channel_id=1, source_target_pairs={{0,32},{32,0},{64,96},{96,64},{1,33},{33,1},{65,97},{97,65},{2,34}... | collective-permute-start | bytes 786440 | tf_op jit(solution)/shard_map/ppermute | solution.py:142
  76.6 0.0 copy-done.5
  76.6 1.9 %collective-permute-start.8 = (f32[128,128]{1,0:T(8,128)S(1)}, f32[128,128]{1,0:T(8,128)S(1)}, u32[]{:S(2)}, u32[]{:S(2)}) collective-permute-start(f32[128,128]{1,0:T(8,128)S(1)} %slice_bitcast_fusion.4), channel_id=1, source_target_pairs={{0,1},{1,0},{2,3},{3,2},{4,5},{5,4},{6,7},{7,6},{8,9},{9,8},{10,11... | collective-permute-start | bytes 196616 | tf_op jit(solution)/shard_map/ppermute | solution.py:142
  78.6 0.0 copy-done.8
  78.6 1.9 %collective-permute-start.6 = (bf16[4,128,256]{2,1,0:T(8,128)(2,1)S(1)}, bf16[4,128,256]{2,1,0:T(8,128)(2,1)S(1)}, u32[]{:S(2)}, u32[]{:S(2)}) collective-permute-start(bf16[4,128,256]{2,1,0:T(8,128)(2,1)S(1)} %copy-done.8), channel_id=1, source_target_pairs={{0,32},{32,0},{64,96},{96,64},{1,33},{33,1},{65,97},{97,65},{2,34}... | collective-permute-start | bytes 786440 | tf_op jit(solution)/shard_map/ppermute | solution.py:142
  80.5 0.0 collective-permute-done.8
  80.5 2.4 %collective-permute-done.7 = bf16[4,128,256]{2,1,0:T(8,128)(2,1)S(1)} collective-permute-done((bf16[4,128,256]{2,1,0:T(8,128)(2,1)S(1)}, bf16[4,128,256]{2,1,0:T(8,128)(2,1)S(1)}, u32[]{:S(2)}, u32[]{:S(2)}) %collective-permute-start.7) | collective-permute-done | bytes 262176 | tf_op jit(solution)/shard_map/ppermute | solution.py:142
  82.9 0.0 copy-done.6
  82.9 0.1 add_convert_fusion.2
  83.0 0.0 copy-start.7
  83.0 2.4 %collective-permute-start.9 = (bf16[4,128,256]{2,1,0:T(8,128)(2,1)S(1)}, bf16[4,128,256]{2,1,0:T(8,128)(2,1)S(1)}, u32[]{:S(2)}, u32[]{:S(2)}) collective-permute-start(bf16[4,128,256]{2,1,0:T(8,128)(2,1)S(1)} %add_convert_fusion.2), channel_id=1, source_target_pairs={{0,64},{32,96},{64,0},{96,32},{1,65},{33,97},{65,1},{97,33},{2,66}... | collective-permute-start | bytes 786440 | tf_op jit(solution)/shard_map/ppermute | solution.py:142
  85.5 6.4 %all-to-all-done.1 = bf16[4,4,3,128,128]{4,3,2,1,0:T(8,128)(2,1)S(1)} async-done(((bf16[4,4,3,128,128]{4,3,2,1,0:T(8,128)(2,1)}), bf16[4,4,3,128,128]{4,3,2,1,0:T(8,128)(2,1)S(1)}, u32[]{:S(2)}, u32[]{:S(2)}) %all-to-all-start.1) | async-done | bytes 1572896 | tf_op jit(solution)/shard_map/all_to_all | solution.py:138
  91.9 1.0 fusion
  92.9 6.7 %all-to-all-start.2 = ((bf16[4,3,128,128]{3,2,1,0:T(8,128)(2,1)}), bf16[4,3,128,128]{3,2,1,0:T(8,128)(2,1)S(1)}, u32[]{:S(2)}, u32[]{:S(2)}) async-start(bf16[4,3,128,128]{3,2,1,0:T(8,128)(2,1)} %fusion), calls=%async_computation.2 | async-start | bytes 786432 | tf_op jit(solution)/shard_map/all_to_all | solution.py:138
  99.6 0.0 collective-permute-done.6
  99.6 0.0 collective-permute-done.9
  99.6 0.0 copy-done.7
  99.6 0.1 add_convert_fusion.1
  99.8 3.4 %collective-permute-start.10 = (bf16[128,256]{1,0:T(8,128)(2,1)S(1)}, bf16[128,256]{1,0:T(8,128)(2,1)S(1)}, u32[]{:S(2)}, u32[]{:S(2)}) collective-permute-start(bf16[128,256]{1,0:T(8,128)(2,1)S(1)} %get-tuple-element.53), channel_id=1, source_target_pairs={{0,128},{128,0},{256,384},{384,256},{1,129},{129,1},{257,385},{385... | collective-permute-start | bytes 196616 | tf_op jit(solution)/shard_map/ppermute | solution.py:142
  103.2 4.0 %collective-permute-start.12 = (bf16[128,256]{1,0:T(8,128)(2,1)S(1)}, bf16[128,256]{1,0:T(8,128)(2,1)S(1)}, u32[]{:S(2)}, u32[]{:S(2)}) collective-permute-start(bf16[128,256]{1,0:T(8,128)(2,1)S(1)} %get-tuple-element.54), channel_id=1, source_target_pairs={{0,384},{128,256},{256,128},{384,0},{1,385},{129,257},{257,129},{3... | collective-permute-start | bytes 196616 | tf_op jit(solution)/shard_map/ppermute | solution.py:142
  107.1 2.5 %collective-permute-start.11 = (bf16[128,256]{1,0:T(8,128)(2,1)S(1)}, bf16[128,256]{1,0:T(8,128)(2,1)S(1)}, u32[]{:S(2)}, u32[]{:S(2)}) collective-permute-start(bf16[128,256]{1,0:T(8,128)(2,1)S(1)} %get-tuple-element.55), channel_id=1, source_target_pairs={{0,256},{128,384},{256,0},{384,128},{1,257},{129,385},{257,1},{385... | collective-permute-start | bytes 196616 | tf_op jit(solution)/shard_map/ppermute | solution.py:142
  109.7 0.6 fusion.5
  110.3 0.0 collective-permute-done.10
  110.3 0.2 collective-permute-done.12
  110.5 4.3 %collective-permute-done.11 = bf16[128,256]{1,0:T(8,128)(2,1)S(1)} collective-permute-done((bf16[128,256]{1,0:T(8,128)(2,1)S(1)}, bf16[128,256]{1,0:T(8,128)(2,1)S(1)}, u32[]{:S(2)}, u32[]{:S(2)}) %collective-permute-start.11) | collective-permute-done | bytes 65568 | tf_op jit(solution)/shard_map/ppermute | solution.py:142
  114.8 0.7 fusion.3
  115.5 10.1 %all-to-all-done.2.parts_ref = bf16[4,3,128,128]{3,2,1,0:T(8,128)(2,1)S(1)} async-done(((bf16[4,3,128,128]{3,2,1,0:T(8,128)(2,1)}), bf16[4,3,128,128]{3,2,1,0:T(8,128)(2,1)S(1)}, u32[]{:S(2)}, u32[]{:S(2)}) %all-to-all-start.2) | async-done | bytes 393248 | tf_op jit(solution)/shard_map/all_to_all | solution.py:138
  125.5 0.8 finish.1
  (3 shorter events, 0.0 us)
Async XLA Ops:
  27.6 18.3 %copy-start.3 = (bf16[128,128]{1,0:T(8,128)(2,1)S(1)}, bf16[128,128]{1,0:T(8,128)(2,1)}, u32[]{:S(2)}) copy-start(bf16[128,128]{1,0:T(8,128)(2,1)} %q_ref.3) | copy-start | bytes 98308
  28.7 28.9 %copy-start = (bf16[128,4096]{1,0:T(8,128)(2,1)S(1)}, bf16[128,4096]{1,0:T(8,128)(2,1)}, u32[]{:S(2)}) copy-start(bf16[128,4096]{1,0:T(8,128)(2,1)} %w_ref.3) | copy-start | bytes 3145732
  28.7 28.9 %all-to-all-start = ((bf16[16,128,256]{2,1,0:T(8,128)(2,1)}), bf16[16,128,256]{2,1,0:T(8,128)(2,1)S(1)}, u32[]{:S(2)}, u32[]{:S(2)}) async-start(bf16[16,128,256]{2,1,0:T(8,128)(2,1)} %broadcast_in_dim.2), calls=%async_computation | async-start | bytes 2097152 | tf_op jit(solution)/shard_map/all_to_all | solution.py:138
  36.0 12.9 %collective-permute-start.3 = (bf16[4,2,128,128]{3,2,1,0:T(8,128)(2,1)S(1)}, bf16[4,2,128,128]{3,2,1,0:T(8,128)(2,1)S(1)}, u32[]{:S(2)}, u32[]{:S(2)}) collective-permute-start(bf16[4,2,128,128]{3,2,1,0:T(8,128)(2,1)S(1)} %bitcast.26), channel_id=1, source_target_pairs={{0,6},{2,4},{4,2},{6,0},{1,7},{3,5},{5,3},{7,1},{8,14},{10,12},{12... | collective-permute-start | bytes 786440 | tf_op jit(solution)/shard_map/ppermute | solution.py:142
  40.7 10.7 %collective-permute-start.2 = (bf16[4,2,128,128]{3,2,1,0:T(8,128)(2,1)S(1)}, bf16[4,2,128,128]{3,2,1,0:T(8,128)(2,1)S(1)}, u32[]{:S(2)}, u32[]{:S(2)}) collective-permute-start(bf16[4,2,128,128]{3,2,1,0:T(8,128)(2,1)S(1)} %bitcast.27), channel_id=1, source_target_pairs={{0,4},{2,6},{4,0},{6,2},{1,5},{3,7},{5,1},{7,3},{8,12},{10,14},{12... | collective-permute-start | bytes 786440 | tf_op jit(solution)/shard_map/ppermute | solution.py:142
  43.4 8.9 %collective-permute-start.1 = (bf16[4,2,128,128]{3,2,1,0:T(8,128)(2,1)S(1)}, bf16[4,2,128,128]{3,2,1,0:T(8,128)(2,1)S(1)}, u32[]{:S(2)}, u32[]{:S(2)}) collective-permute-start(bf16[4,2,128,128]{3,2,1,0:T(8,128)(2,1)S(1)} %bitcast.28), channel_id=1, source_target_pairs={{0,2},{2,0},{4,6},{6,4},{1,3},{3,1},{5,7},{7,5},{8,10},{10,8},{12,... | collective-permute-start | bytes 786440 | tf_op jit(solution)/shard_map/ppermute | solution.py:142
  45.9 3.1 %collective-permute-start = (bf16[128,128]{1,0:T(8,128)(2,1)S(1)}, bf16[128,128]{1,0:T(8,128)(2,1)S(1)}, u32[]{:S(2)}, u32[]{:S(2)}) collective-permute-start(bf16[128,128]{1,0:T(8,128)(2,1)S(1)} %copy-done.3), channel_id=1, source_target_pairs={{0,1},{1,0},{2,3},{3,2},{4,5},{5,4},{6,7},{7,6},{8,9},{9,8},{10,11... | collective-permute-start | bytes 98312 | tf_op jit(solution)/shard_map/ppermute | solution.py:142
  53.5 3.4 %collective-permute-start.4 = (f32[256,256]{1,0:T(8,128)S(1)}, f32[256,256]{1,0:T(8,128)S(1)}, u32[]{:S(2)}, u32[]{:S(2)}) collective-permute-start(f32[256,256]{1,0:T(8,128)S(1)} %forward.1.mine_ref), channel_id=1, source_target_pairs={{0,1},{1,0},{2,3},{3,2},{4,5},{5,4},{6,7},{7,6},{8,9},{9,8},{10,11... | collective-permute-start | bytes 786440 | tf_op jit(solution)/shard_map/ppermute | solution.py:142
  56.9 0.7 copy-start.1
  57.6 4.9 %copy-start.2 = (f32[256,256]{1,0:T(8,128)S(1)}, f32[256,256]{1,0:T(8,128)}, u32[]{:S(2)}) copy-start(f32[256,256]{1,0:T(8,128)} %copy-done.1) | copy-start | bytes 786436
  58.6 3.9 %collective-permute-start.5 = (bf16[17,128,128]{2,1,0:T(8,128)(2,1)S(1)}, bf16[17,128,128]{2,1,0:T(8,128)(2,1)S(1)}, u32[]{:S(2)}, u32[]{:S(2)}) collective-permute-start(bf16[17,128,128]{2,1,0:T(8,128)(2,1)S(1)} %cotangent.1.gift_ref), channel_id=1, source_target_pairs={{0,1},{1,0},{2,3},{3,2},{4,5},{5,4},{6,7},{7,6},{8,9},{9,8},{10,11... | collective-permute-start | bytes 1671176 | tf_op jit(solution)/shard_map/ppermute | solution.py:142
  66.1 0.6 copy-start.4
  66.7 4.2 %copy-start.9 = (bf16[4,128,256]{2,1,0:T(8,128)(2,1)S(1)}, bf16[4,128,256]{2,1,0:T(8,128)(2,1)}, u32[]{:S(2)}) copy-start(bf16[4,128,256]{2,1,0:T(8,128)(2,1)} %get-tuple-element.45) | copy-start | bytes 786436
  66.7 9.9 %copy-start.5 = (f32[2,128,128]{2,1,0:T(8,128)S(1)}, f32[2,128,128]{2,1,0:T(8,128)}, u32[]{:S(2)}) copy-start(f32[2,128,128]{2,1,0:T(8,128)} %copy-done.4) | copy-start | bytes 393220
  66.7 11.8 %copy-start.8 = (bf16[4,128,256]{2,1,0:T(8,128)(2,1)S(1)}, bf16[4,128,256]{2,1,0:T(8,128)(2,1)}, u32[]{:S(2)}) copy-start(bf16[4,128,256]{2,1,0:T(8,128)(2,1)} %get-tuple-element.43) | copy-start | bytes 786436
  66.7 16.2 %copy-start.6 = (bf16[4,128,256]{2,1,0:T(8,128)(2,1)S(1)}, bf16[4,128,256]{2,1,0:T(8,128)(2,1)}, u32[]{:S(2)}) copy-start(bf16[4,128,256]{2,1,0:T(8,128)(2,1)} %get-tuple-element.44) | copy-start | bytes 786436
  66.7 25.2 %all-to-all-start.1 = ((bf16[4,4,3,128,128]{4,3,2,1,0:T(8,128)(2,1)}), bf16[4,4,3,128,128]{4,3,2,1,0:T(8,128)(2,1)S(1)}, u32[]{:S(2)}, u32[]{:S(2)}) async-start(bf16[4,4,3,128,128]{4,3,2,1,0:T(8,128)(2,1)} %get-tuple-element.49), calls=%async_computation.1 | async-start | bytes 3145728 | tf_op jit(solution)/shard_map/all_to_all | solution.py:138
  70.9 12.0 %collective-permute-start.7 = (bf16[4,128,256]{2,1,0:T(8,128)(2,1)S(1)}, bf16[4,128,256]{2,1,0:T(8,128)(2,1)S(1)}, u32[]{:S(2)}, u32[]{:S(2)}) collective-permute-start(bf16[4,128,256]{2,1,0:T(8,128)(2,1)S(1)} %copy-done.9), channel_id=1, source_target_pairs={{0,32},{32,0},{64,96},{96,64},{1,33},{33,1},{65,97},{97,65},{2,34}... | collective-permute-start | bytes 786440 | tf_op jit(solution)/shard_map/ppermute | solution.py:142
  76.6 3.9 %collective-permute-start.8 = (f32[128,128]{1,0:T(8,128)S(1)}, f32[128,128]{1,0:T(8,128)S(1)}, u32[]{:S(2)}, u32[]{:S(2)}) collective-permute-start(f32[128,128]{1,0:T(8,128)S(1)} %slice_bitcast_fusion.4), channel_id=1, source_target_pairs={{0,1},{1,0},{2,3},{3,2},{4,5},{5,4},{6,7},{7,6},{8,9},{9,8},{10,11... | collective-permute-start | bytes 196616 | tf_op jit(solution)/shard_map/ppermute | solution.py:142
  78.6 21.0 %collective-permute-start.6 = (bf16[4,128,256]{2,1,0:T(8,128)(2,1)S(1)}, bf16[4,128,256]{2,1,0:T(8,128)(2,1)S(1)}, u32[]{:S(2)}, u32[]{:S(2)}) collective-permute-start(bf16[4,128,256]{2,1,0:T(8,128)(2,1)S(1)} %copy-done.8), channel_id=1, source_target_pairs={{0,32},{32,0},{64,96},{96,64},{1,33},{33,1},{65,97},{97,65},{2,34}... | collective-permute-start | bytes 786440 | tf_op jit(solution)/shard_map/ppermute | solution.py:142
  83.0 16.6 %copy-start.7 = (bf16[4,128,256]{2,1,0:T(8,128)(2,1)S(1)}, bf16[4,128,256]{2,1,0:T(8,128)(2,1)}, u32[]{:S(2)}) copy-start(bf16[4,128,256]{2,1,0:T(8,128)(2,1)} %get-tuple-element.42) | copy-start | bytes 786436
  83.0 16.6 %collective-permute-start.9 = (bf16[4,128,256]{2,1,0:T(8,128)(2,1)S(1)}, bf16[4,128,256]{2,1,0:T(8,128)(2,1)S(1)}, u32[]{:S(2)}, u32[]{:S(2)}) collective-permute-start(bf16[4,128,256]{2,1,0:T(8,128)(2,1)S(1)} %add_convert_fusion.2), channel_id=1, source_target_pairs={{0,64},{32,96},{64,0},{96,32},{1,65},{33,97},{65,1},{97,33},{2,66}... | collective-permute-start | bytes 786440 | tf_op jit(solution)/shard_map/ppermute | solution.py:142
  92.9 32.7 %all-to-all-start.2 = ((bf16[4,3,128,128]{3,2,1,0:T(8,128)(2,1)}), bf16[4,3,128,128]{3,2,1,0:T(8,128)(2,1)S(1)}, u32[]{:S(2)}, u32[]{:S(2)}) async-start(bf16[4,3,128,128]{3,2,1,0:T(8,128)(2,1)} %fusion), calls=%async_computation.2 | async-start | bytes 786432 | tf_op jit(solution)/shard_map/all_to_all | solution.py:138
  99.8 10.5 %collective-permute-start.10 = (bf16[128,256]{1,0:T(8,128)(2,1)S(1)}, bf16[128,256]{1,0:T(8,128)(2,1)S(1)}, u32[]{:S(2)}, u32[]{:S(2)}) collective-permute-start(bf16[128,256]{1,0:T(8,128)(2,1)S(1)} %get-tuple-element.53), channel_id=1, source_target_pairs={{0,128},{128,0},{256,384},{384,256},{1,129},{129,1},{257,385},{385... | collective-permute-start | bytes 196616 | tf_op jit(solution)/shard_map/ppermute | solution.py:142
  103.2 7.4 %collective-permute-start.12 = (bf16[128,256]{1,0:T(8,128)(2,1)S(1)}, bf16[128,256]{1,0:T(8,128)(2,1)S(1)}, u32[]{:S(2)}, u32[]{:S(2)}) collective-permute-start(bf16[128,256]{1,0:T(8,128)(2,1)S(1)} %get-tuple-element.54), channel_id=1, source_target_pairs={{0,384},{128,256},{256,128},{384,0},{1,385},{129,257},{257,129},{3... | collective-permute-start | bytes 196616 | tf_op jit(solution)/shard_map/ppermute | solution.py:142
  107.1 7.7 %collective-permute-start.11 = (bf16[128,256]{1,0:T(8,128)(2,1)S(1)}, bf16[128,256]{1,0:T(8,128)(2,1)S(1)}, u32[]{:S(2)}, u32[]{:S(2)}) collective-permute-start(bf16[128,256]{1,0:T(8,128)(2,1)S(1)} %get-tuple-element.55), channel_id=1, source_target_pairs={{0,256},{128,384},{256,0},{384,128},{1,257},{129,385},{257,1},{385... | collective-permute-start | bytes 196616 | tf_op jit(solution)/shard_map/ppermute | solution.py:142

commit v7 on v6

--- a/solution.py
+++ b/solution.py
@@ -33,8 +33,21 @@
         copy.wait()
 
 
-def cotangent_kernel(place_ref, w_ref, cot_ref, gift_ref):
+def cotangent_kernel(place_ref, w_ref, cot_ref, part_ref, gift_ref):
     core = place_ref[0]
+    lane = lax.broadcasted_iota(jnp.int32, (BLK, BLK), 1)
+    for half in range(2):
+        rows = slice(half * BLK, (half + 1) * BLK)
+        values = part_ref[rows, :HDIM]
+        high = values.astype(BF16)
+        gift_ref[17 + 2 * half] = high
+        gift_ref[18 + 2 * half] = (values - high.astype(F32)).astype(BF16)
+        lse = part_ref[rows, HDIM:]
+        first = lse.astype(BF16).astype(F32)
+        second = (lse - first).astype(BF16).astype(F32)
+        third = lse - first - second
+        lse = jnp.where(lane == 0, first, jnp.where(lane == 1, second, third))
+        gift_ref[21 + half] = lse.astype(BF16)
     grad = jnp.zeros((BLK, HDIM), F32)
     for o in range(16):
         cot = cot_ref[o]
@@ -67,25 +80,28 @@
     part_ref[:, HDIM:] = jnp.broadcast_to(row_max + jnp.log(totals), (2 * BLK, BLK))
 
 
-def merged(grad, mine_ref, theirs_ref, half):
+def merged(grad, mine_ref, got_ref, half):
     rows = slice(half * BLK, (half + 1) * BLK)
-    swapped = slice((1 - half) * BLK, (2 - half) * BLK)
-    a, b = mine_ref[rows, HDIM:], theirs_ref[swapped, HDIM:]
+    swapped = 1 - half
+    parts = got_ref[21 + swapped].astype(F32)
+    b = parts[:, :1] + parts[:, 1:2] + parts[:, 2:3]
+    a = mine_ref[rows, HDIM : HDIM + 1]
     top = jnp.maximum(a, b)
     lse = top + jnp.log(jnp.exp(a - top) + jnp.exp(b - top))
+    theirs = got_ref[17 + 2 * swapped].astype(F32) + got_ref[18 + 2 * swapped].astype(F32)
     attn = mine_ref[rows, :HDIM] * jnp.exp(a - lse)
-    attn = (attn + theirs_ref[swapped, :HDIM] * jnp.exp(b - lse)).astype(BF16)
+    attn = (attn + theirs * jnp.exp(b - lse)).astype(BF16)
     dots = jnp.sum(grad.astype(F32) * attn.astype(F32), axis=1, keepdims=True)
-    return grad, attn, lse[:, :1], dots
+    return grad, attn, lse, dots
 
 
 def backward_kernel(
-    place_ref, q_ref, other_ref, kv0, kv1, kv2, kv3, cot_ref, w_ref, gift_ref, got_ref, mine_ref, theirs_ref, *refs
+    place_ref, q_ref, other_ref, kv0, kv1, kv2, kv3, cot_ref, w_ref, gift_ref, got_ref, mine_ref, *refs
 ):
     pieces = (kv0, kv1, kv2, kv3)
     dq_ref, pay_hbm, *out_hbm, pay_ref, out_ref, sems = refs
     halves = [
-        merged(ref[0], mine_ref, theirs_ref, half) for half, ref in enumerate((gift_ref, got_ref))
+        merged(ref[0], mine_ref, got_ref, half) for half, ref in enumerate((gift_ref, got_ref))
     ]
     mine = pl.ds(pl.multiple_of(place_ref[0] * BLK, BLK), BLK)
     grad, attn, lse, dots = (jnp.concatenate(pair, axis=0) for pair in zip(*halves))
@@ -196,24 +212,23 @@
         unit // BLK,
         [pltpu.VMEM((2 * BLK, 16 * BLK), F32)],
     )(queries, other, *pieces)
-    theirs = trade(part, "c", 1)
-    cot, theirs = lax.optimization_barrier((cot, theirs))
+    cot, part = lax.optimization_barrier((cot, part))
     gift = call(
         cotangent_kernel,
         "cotangent",
-        shape((17, BLK, BLK), BF16),
-        [SMEM] + [VMEM] * 2,
+        shape((23, BLK, BLK), BF16),
+        [SMEM] + [VMEM] * 3,
         8,
         2 * unit,
         2 << 20,
-    )(place, w_out, cot)
+    )(place, w_out, cot, part)
     got = trade(gift, "c", 1)
     dq, pay, *outs = call(
         backward_kernel,
         "backward",
         (shape((2, BLK, HDIM), F32), pltpu.HBM((4, 4, 3, BLK, BLK), BF16))
         + (pltpu.HBM((4, BLK, 256), BF16),) * 4,
-        [SMEM] + [VMEM] * 12,
+        [SMEM] + [VMEM] * 11,
         12,
         14 * unit,
         8 << 20,
@@ -224,7 +239,7 @@
             pltpu.SemaphoreType.DMA((8,)),
         ],
         (VMEM,) + (HBM,) * 5,
-    )(place, queries, other, *pieces, cot, w_out, gift, got, part, theirs)
+    )(place, queries, other, *pieces, cot, w_out, gift, got, part)
     pay, *outs = lax.optimization_barrier((pay, *outs))
     pay = exchange(pay, "x")
     passing = trade(outs[3], "zl", 1)

time: 127 us -> 128 us (level)
  the two profiles are of different devices: /device:TPU:32 before, /device:TPU:1 now
where the time goes in v7:
time: 128 us; the launch traced here: 127 us
  starting transfers between devices  55.1 us (43%)
  waiting for transfers between devices  33.8 us (26%)
  blocking collectives  25.3 us (20%)
  Pallas kernels  7.6 us (6%)
  other arithmetic  2.51 us (2%)
  local copies, waits for them, and re-layouts  1.78 us (1%)
    ppermute x12, starting transfers between devices, trade(): lax.ppermute(block, axis, [(i, i ^ step) for i in range(2 if axis == 'c'...  38.7 us
    all_to_all x3, waiting for transfers between devices, exchange(): return lax.all_to_all(blocks, axis, 0, 0, tiled=True)  28.6 us
    all_gather x1, blocking collectives, body(): kv = lax.all_gather(kv, 'zh', axis=0, tiled=True).reshape(4, 2, BLK, HDIM)  25.3 us
    all_to_all x3, starting transfers between devices, exchange(): return lax.all_to_all(blocks, axis, 0, 0, tiled=True)  16.4 us
    ppermute x12, waiting for transfers between devices, trade(): lax.ppermute(block, axis, [(i, i ^ step) for i in range(2 if axis == 'c'...  5.16 us
    pallas_call x1, Pallas kernels, body(): call(backward_kernel, 'backward', (shape((2, BLK, HDIM), F32), pltpu.HBM(...  3.74 us
  transfers between devices with their start and end apart: 15, of which 7 were waited for; matrix products, arithmetic and copies ran while one was open for 2% of the time, Pallas kernels for 1%

profile of v7, /device:TPU:1, one launch (start us, length us, event | category | flops | bytes accessed | tf_op | source)
XLA Modules:
  0.0 127.0 jit_solution(2352590542991087827)
XLA Ops:
  0.6 0.9 pack.1
  1.5 25.3 %all_gather.3 = bf16[1024,128]{1,0:T(8,128)(2,1)S(1)} all-gather(bf16[256,128]{1,0:T(8,128)(2,1)S(1)} %get-tuple-element.29), channel_id=1, replica_groups=mesh['y'=4,'zl'=4,'zh'=4,'x'=4,'c'=2] {'zh'}, dimensions={0}, use_global_device_ids=true | all-gather | bytes 327680 | tf_op jit(solution)/shard_map/all_gather | solution.py:199
  26.8 0.1 pad_add_fusion.place_ref
  26.9 0.0 copy-start.1
  26.9 1.1 broadcast_in_dim.2
  28.0 0.0 copy-start
  28.0 5.8 %all-to-all-start = ((bf16[16,128,256]{2,1,0:T(8,128)(2,1)}), bf16[16,128,256]{2,1,0:T(8,128)(2,1)S(1)}, u32[]{:S(2)}, u32[]{:S(2)}) async-start(bf16[16,128,256]{2,1,0:T(8,128)(2,1)} %broadcast_in_dim.2), calls=%async_computation | async-start | bytes 2097152 | tf_op jit(solution)/shard_map/all_to_all | solution.py:154
  33.8 4.4 %collective-permute-start.3 = (bf16[4,2,128,128]{3,2,1,0:T(8,128)(2,1)S(1)}, bf16[4,2,128,128]{3,2,1,0:T(8,128)(2,1)S(1)}, u32[]{:S(2)}, u32[]{:S(2)}) collective-permute-start(bf16[4,2,128,128]{3,2,1,0:T(8,128)(2,1)S(1)} %bitcast.26), channel_id=1, source_target_pairs={{0,6},{2,4},{4,2},{6,0},{1,7},{3,5},{5,3},{7,1},{8,14},{10,12},{12... | collective-permute-start | bytes 786440 | tf_op jit(solution)/shard_map/ppermute | solution.py:158
  38.2 2.4 %collective-permute-start.2 = (bf16[4,2,128,128]{3,2,1,0:T(8,128)(2,1)S(1)}, bf16[4,2,128,128]{3,2,1,0:T(8,128)(2,1)S(1)}, u32[]{:S(2)}, u32[]{:S(2)}) collective-permute-start(bf16[4,2,128,128]{3,2,1,0:T(8,128)(2,1)S(1)} %bitcast.27), channel_id=1, source_target_pairs={{0,4},{2,6},{4,0},{6,2},{1,5},{3,7},{5,1},{7,3},{8,12},{10,14},{12... | collective-permute-start | bytes 786440 | tf_op jit(solution)/shard_map/ppermute | solution.py:158
  40.6 2.2 %collective-permute-start.1 = (bf16[4,2,128,128]{3,2,1,0:T(8,128)(2,1)S(1)}, bf16[4,2,128,128]{3,2,1,0:T(8,128)(2,1)S(1)}, u32[]{:S(2)}, u32[]{:S(2)}) collective-permute-start(bf16[4,2,128,128]{3,2,1,0:T(8,128)(2,1)S(1)} %bitcast.28), channel_id=1, source_target_pairs={{0,2},{2,0},{4,6},{6,4},{1,3},{3,1},{5,7},{7,5},{8,10},{10,8},{12,... | collective-permute-start | bytes 786440 | tf_op jit(solution)/shard_map/ppermute | solution.py:158
  42.8 0.0 copy-done.1
  42.8 6.5 %collective-permute-start = (bf16[128,128]{1,0:T(8,128)(2,1)S(1)}, bf16[128,128]{1,0:T(8,128)(2,1)S(1)}, u32[]{:S(2)}, u32[]{:S(2)}) collective-permute-start(bf16[128,128]{1,0:T(8,128)(2,1)S(1)} %copy-done.1), channel_id=1, source_target_pairs={{0,1},{1,0},{2,3},{3,2},{4,5},{5,4},{6,7},{7,6},{8,9},{9,8},{10,11... | collective-permute-start | bytes 98312 | tf_op jit(solution)/shard_map/ppermute | solution.py:158
  49.3 0.8 collective-permute-done.other_ref
  50.1 0.0 collective-permute-done.3.kv3
  50.1 0.0 collective-permute-done.2.kv2
  50.2 0.0 collective-permute-done.1.kv1
  50.2 1.2 forward.1.part_ref.mine_ref
  51.4 9.0 %all-to-all-done.cot_ref = bf16[16,128,256]{2,1,0:T(8,128)(2,1)S(1)} async-done(((bf16[16,128,256]{2,1,0:T(8,128)(2,1)}), bf16[16,128,256]{2,1,0:T(8,128)(2,1)S(1)}, u32[]{:S(2)}, u32[]{:S(2)}) %all-to-all-start) | async-done | bytes 1048608 | tf_op jit(solution)/shard_map/all_to_all | solution.py:154
  60.4 0.0 copy-done
  60.4 1.0 cotangent.1.gift_ref
  61.4 4.1 %collective-permute-start.4 = (bf16[23,128,128]{2,1,0:T(8,128)(2,1)S(1)}, bf16[23,128,128]{2,1,0:T(8,128)(2,1)S(1)}, u32[]{:S(2)}, u32[]{:S(2)}) collective-permute-start(bf16[23,128,128]{2,1,0:T(8,128)(2,1)S(1)} %cotangent.1.gift_ref), channel_id=1, source_target_pairs={{0,1},{1,0},{2,3},{3,2},{4,5},{5,4},{6,7},{7,6},{8,9},{9,8},{10,11... | collective-permute-start | bytes 2261000 | tf_op jit(solution)/shard_map/ppermute | solution.py:158
  65.5 1.8 %collective-permute-done.4.got_ref = bf16[23,128,128]{2,1,0:T(8,128)(2,1)S(1)} collective-permute-done((bf16[23,128,128]{2,1,0:T(8,128)(2,1)S(1)}, bf16[23,128,128]{2,1,0:T(8,128)(2,1)S(1)}, u32[]{:S(2)}, u32[]{:S(2)}) %collective-permute-start.4) | collective-permute-done | bytes 753696 | tf_op jit(solution)/shard_map/ppermute | solution.py:158
  67.3 3.7 %backward.1 = (f32[2,128,128]{2,1,0:T(8,128)S(1)}, bf16[4,4,3,128,128]{4,3,2,1,0:T(8,128)(2,1)}, bf16[4,128,256]{2,1,0:T(8,128)(2,1)}, bf16[4,128,256]{2,1,0:T(8...) custom-call(s32[4]{0:T(128)S(1)} %pad_add_fusion.place_ref, bf16[128,128]{1,0:T(8,128)(2,1)S(1)} %copy-done.1, ...), custom_call_target="tpu_custom_call" | custom-call | flops 939524096 | bytes 8388608 | tf_op jit(solution)/shard_map/backward/pallas_call | solution.py:226
  71.1 0.0 copy-start.2
  71.1 0.6 copy-done.2
  71.7 0.0 copy-start.7
  71.7 0.0 copy-start.3
  71.7 0.0 copy-start.6
  71.7 0.0 copy-start.4
  71.7 4.2 %all-to-all-start.1 = ((bf16[4,4,3,128,128]{4,3,2,1,0:T(8,128)(2,1)}), bf16[4,4,3,128,128]{4,3,2,1,0:T(8,128)(2,1)S(1)}, u32[]{:S(2)}, u32[]{:S(2)}) async-start(bf16[4,4,3,128,128]{4,3,2,1,0:T(8,128)(2,1)} %get-tuple-element.49), calls=%async_computation.1 | async-start | bytes 3145728 | tf_op jit(solution)/shard_map/all_to_all | solution.py:154
  75.9 0.0 copy-done.7
  75.9 1.9 %collective-permute-start.6 = (bf16[4,128,256]{2,1,0:T(8,128)(2,1)S(1)}, bf16[4,128,256]{2,1,0:T(8,128)(2,1)S(1)}, u32[]{:S(2)}, u32[]{:S(2)}) collective-permute-start(bf16[4,128,256]{2,1,0:T(8,128)(2,1)S(1)} %copy-done.7), channel_id=1, source_target_pairs={{0,32},{32,0},{64,96},{96,64},{1,33},{33,1},{65,97},{97,65},{2,34}... | collective-permute-start | bytes 786440 | tf_op jit(solution)/shard_map/ppermute | solution.py:158
  77.8 0.0 copy-done.3
  77.8 2.6 %collective-permute-start.7 = (f32[128,128]{1,0:T(8,128)S(1)}, f32[128,128]{1,0:T(8,128)S(1)}, u32[]{:S(2)}, u32[]{:S(2)}) collective-permute-start(f32[128,128]{1,0:T(8,128)S(1)} %slice_bitcast_fusion.4), channel_id=1, source_target_pairs={{0,1},{1,0},{2,3},{3,2},{4,5},{5,4},{6,7},{7,6},{8,9},{9,8},{10,11... | collective-permute-start | bytes 196616 | tf_op jit(solution)/shard_map/ppermute | solution.py:158
  80.4 0.0 copy-done.6
  80.4 3.6 %collective-permute-start.5 = (bf16[4,128,256]{2,1,0:T(8,128)(2,1)S(1)}, bf16[4,128,256]{2,1,0:T(8,128)(2,1)S(1)}, u32[]{:S(2)}, u32[]{:S(2)}) collective-permute-start(bf16[4,128,256]{2,1,0:T(8,128)(2,1)S(1)} %copy-done.6), channel_id=1, source_target_pairs={{0,32},{32,0},{64,96},{96,64},{1,33},{33,1},{65,97},{97,65},{2,34}... | collective-permute-start | bytes 786440 | tf_op jit(solution)/shard_map/ppermute | solution.py:158
  84.1 0.0 collective-permute-done.7
  84.1 0.9 collective-permute-done.6
  85.0 0.0 copy-done.4
  85.0 0.1 add_convert_fusion.2
  85.0 0.0 copy-start.5
  85.1 2.1 %collective-permute-start.8 = (bf16[4,128,256]{2,1,0:T(8,128)(2,1)S(1)}, bf16[4,128,256]{2,1,0:T(8,128)(2,1)S(1)}, u32[]{:S(2)}, u32[]{:S(2)}) collective-permute-start(bf16[4,128,256]{2,1,0:T(8,128)(2,1)S(1)} %add_convert_fusion.2), channel_id=1, source_target_pairs={{0,64},{32,96},{64,0},{96,32},{1,65},{33,97},{65,1},{97,33},{2,66}... | collective-permute-start | bytes 786440 | tf_op jit(solution)/shard_map/ppermute | solution.py:158
  87.1 8.9 %all-to-all-done.1 = bf16[4,4,3,128,128]{4,3,2,1,0:T(8,128)(2,1)S(1)} async-done(((bf16[4,4,3,128,128]{4,3,2,1,0:T(8,128)(2,1)}), bf16[4,4,3,128,128]{4,3,2,1,0:T(8,128)(2,1)S(1)}, u32[]{:S(2)}, u32[]{:S(2)}) %all-to-all-start.1) | async-done | bytes 1572896 | tf_op jit(solution)/shard_map/all_to_all | solution.py:154
  96.0 1.0 fusion
  97.0 6.5 %all-to-all-start.2 = ((bf16[4,3,128,128]{3,2,1,0:T(8,128)(2,1)}), bf16[4,3,128,128]{3,2,1,0:T(8,128)(2,1)S(1)}, u32[]{:S(2)}, u32[]{:S(2)}) async-start(bf16[4,3,128,128]{3,2,1,0:T(8,128)(2,1)} %fusion), calls=%async_computation.2 | async-start | bytes 786432 | tf_op jit(solution)/shard_map/all_to_all | solution.py:154
  103.5 0.0 collective-permute-done.5
  103.5 0.0 collective-permute-done.8
  103.5 0.0 copy-done.5
  103.5 0.1 add_convert_fusion.1
  103.6 1.9 %collective-permute-start.9 = (bf16[128,256]{1,0:T(8,128)(2,1)S(1)}, bf16[128,256]{1,0:T(8,128)(2,1)S(1)}, u32[]{:S(2)}, u32[]{:S(2)}) collective-permute-start(bf16[128,256]{1,0:T(8,128)(2,1)S(1)} %get-tuple-element.53), channel_id=1, source_target_pairs={{0,128},{128,0},{256,384},{384,256},{1,129},{129,1},{257,385},{385... | collective-permute-start | bytes 196616 | tf_op jit(solution)/shard_map/ppermute | solution.py:158
  105.5 2.7 %collective-permute-start.11 = (bf16[128,256]{1,0:T(8,128)(2,1)S(1)}, bf16[128,256]{1,0:T(8,128)(2,1)S(1)}, u32[]{:S(2)}, u32[]{:S(2)}) collective-permute-start(bf16[128,256]{1,0:T(8,128)(2,1)S(1)} %get-tuple-element.54), channel_id=1, source_target_pairs={{0,384},{128,256},{256,128},{384,0},{1,385},{129,257},{257,129},{3... | collective-permute-start | bytes 196616 | tf_op jit(solution)/shard_map/ppermute | solution.py:158
  108.3 4.3 %collective-permute-start.10 = (bf16[128,256]{1,0:T(8,128)(2,1)S(1)}, bf16[128,256]{1,0:T(8,128)(2,1)S(1)}, u32[]{:S(2)}, u32[]{:S(2)}) collective-permute-start(bf16[128,256]{1,0:T(8,128)(2,1)S(1)} %get-tuple-element.55), channel_id=1, source_target_pairs={{0,256},{128,384},{256,0},{384,128},{1,257},{129,385},{257,1},{385... | collective-permute-start | bytes 196616 | tf_op jit(solution)/shard_map/ppermute | solution.py:158
  112.6 0.6 fusion.5
  113.2 0.0 collective-permute-done.9
  113.2 0.0 collective-permute-done.11
  113.2 1.6 %collective-permute-done.10 = bf16[128,256]{1,0:T(8,128)(2,1)S(1)} collective-permute-done((bf16[128,256]{1,0:T(8,128)(2,1)S(1)}, bf16[128,256]{1,0:T(8,128)(2,1)S(1)}, u32[]{:S(2)}, u32[]{:S(2)}) %collective-permute-start.10) | collective-permute-done | bytes 65568 | tf_op jit(solution)/shard_map/ppermute | solution.py:158
  114.8 0.7 fusion.3
  115.5 10.7 %all-to-all-done.2.parts_ref = bf16[4,3,128,128]{3,2,1,0:T(8,128)(2,1)S(1)} async-done(((bf16[4,3,128,128]{3,2,1,0:T(8,128)(2,1)}), bf16[4,3,128,128]{3,2,1,0:T(8,128)(2,1)S(1)}, u32[]{:S(2)}, u32[]{:S(2)}) %all-to-all-start.2) | async-done | bytes 393248 | tf_op jit(solution)/shard_map/all_to_all | solution.py:154
  126.2 0.8 finish.1
  (2 shorter events, 0.0 us)
Async XLA Ops:
  26.9 15.9 %copy-start.1 = (bf16[128,128]{1,0:T(8,128)(2,1)S(1)}, bf16[128,128]{1,0:T(8,128)(2,1)}, u32[]{:S(2)}) copy-start(bf16[128,128]{1,0:T(8,128)(2,1)} %q_ref.3) | copy-start | bytes 98308
  28.0 32.4 %copy-start = (bf16[128,4096]{1,0:T(8,128)(2,1)S(1)}, bf16[128,4096]{1,0:T(8,128)(2,1)}, u32[]{:S(2)}) copy-start(bf16[128,4096]{1,0:T(8,128)(2,1)} %w_ref.3) | copy-start | bytes 3145732
  28.0 32.4 %all-to-all-start = ((bf16[16,128,256]{2,1,0:T(8,128)(2,1)}), bf16[16,128,256]{2,1,0:T(8,128)(2,1)S(1)}, u32[]{:S(2)}, u32[]{:S(2)}) async-start(bf16[16,128,256]{2,1,0:T(8,128)(2,1)} %broadcast_in_dim.2), calls=%async_computation | async-start | bytes 2097152 | tf_op jit(solution)/shard_map/all_to_all | solution.py:154
  33.8 16.4 %collective-permute-start.3 = (bf16[4,2,128,128]{3,2,1,0:T(8,128)(2,1)S(1)}, bf16[4,2,128,128]{3,2,1,0:T(8,128)(2,1)S(1)}, u32[]{:S(2)}, u32[]{:S(2)}) collective-permute-start(bf16[4,2,128,128]{3,2,1,0:T(8,128)(2,1)S(1)} %bitcast.26), channel_id=1, source_target_pairs={{0,6},{2,4},{4,2},{6,0},{1,7},{3,5},{5,3},{7,1},{8,14},{10,12},{12... | collective-permute-start | bytes 786440 | tf_op jit(solution)/shard_map/ppermute | solution.py:158
  38.2 12.0 %collective-permute-start.2 = (bf16[4,2,128,128]{3,2,1,0:T(8,128)(2,1)S(1)}, bf16[4,2,128,128]{3,2,1,0:T(8,128)(2,1)S(1)}, u32[]{:S(2)}, u32[]{:S(2)}) collective-permute-start(bf16[4,2,128,128]{3,2,1,0:T(8,128)(2,1)S(1)} %bitcast.27), channel_id=1, source_target_pairs={{0,4},{2,6},{4,0},{6,2},{1,5},{3,7},{5,1},{7,3},{8,12},{10,14},{12... | collective-permute-start | bytes 786440 | tf_op jit(solution)/shard_map/ppermute | solution.py:158
  40.6 9.5 %collective-permute-start.1 = (bf16[4,2,128,128]{3,2,1,0:T(8,128)(2,1)S(1)}, bf16[4,2,128,128]{3,2,1,0:T(8,128)(2,1)S(1)}, u32[]{:S(2)}, u32[]{:S(2)}) collective-permute-start(bf16[4,2,128,128]{3,2,1,0:T(8,128)(2,1)S(1)} %bitcast.28), channel_id=1, source_target_pairs={{0,2},{2,0},{4,6},{6,4},{1,3},{3,1},{5,7},{7,5},{8,10},{10,8},{12,... | collective-permute-start | bytes 786440 | tf_op jit(solution)/shard_map/ppermute | solution.py:158
  42.8 7.4 %collective-permute-start = (bf16[128,128]{1,0:T(8,128)(2,1)S(1)}, bf16[128,128]{1,0:T(8,128)(2,1)S(1)}, u32[]{:S(2)}, u32[]{:S(2)}) collective-permute-start(bf16[128,128]{1,0:T(8,128)(2,1)S(1)} %copy-done.1), channel_id=1, source_target_pairs={{0,1},{1,0},{2,3},{3,2},{4,5},{5,4},{6,7},{7,6},{8,9},{9,8},{10,11... | collective-permute-start | bytes 98312 | tf_op jit(solution)/shard_map/ppermute | solution.py:158
  61.4 5.9 %collective-permute-start.4 = (bf16[23,128,128]{2,1,0:T(8,128)(2,1)S(1)}, bf16[23,128,128]{2,1,0:T(8,128)(2,1)S(1)}, u32[]{:S(2)}, u32[]{:S(2)}) collective-permute-start(bf16[23,128,128]{2,1,0:T(8,128)(2,1)S(1)} %cotangent.1.gift_ref), channel_id=1, source_target_pairs={{0,1},{1,0},{2,3},{3,2},{4,5},{5,4},{6,7},{7,6},{8,9},{9,8},{10,11... | collective-permute-start | bytes 2261000 | tf_op jit(solution)/shard_map/ppermute | solution.py:158
  71.1 0.6 copy-start.2
  71.7 4.2 %copy-start.7 = (bf16[4,128,256]{2,1,0:T(8,128)(2,1)S(1)}, bf16[4,128,256]{2,1,0:T(8,128)(2,1)}, u32[]{:S(2)}) copy-start(bf16[4,128,256]{2,1,0:T(8,128)(2,1)} %get-tuple-element.45) | copy-start | bytes 786436
  71.7 6.1 %copy-start.3 = (f32[2,128,128]{2,1,0:T(8,128)S(1)}, f32[2,128,128]{2,1,0:T(8,128)}, u32[]{:S(2)}) copy-start(f32[2,128,128]{2,1,0:T(8,128)} %copy-done.2) | copy-start | bytes 393220
  71.7 8.7 %copy-start.6 = (bf16[4,128,256]{2,1,0:T(8,128)(2,1)S(1)}, bf16[4,128,256]{2,1,0:T(8,128)(2,1)}, u32[]{:S(2)}) copy-start(bf16[4,128,256]{2,1,0:T(8,128)(2,1)} %get-tuple-element.43) | copy-start | bytes 786436
  71.7 13.3 %copy-start.4 = (bf16[4,128,256]{2,1,0:T(8,128)(2,1)S(1)}, bf16[4,128,256]{2,1,0:T(8,128)(2,1)}, u32[]{:S(2)}) copy-start(bf16[4,128,256]{2,1,0:T(8,128)(2,1)} %get-tuple-element.44) | copy-start | bytes 786436
  71.7 24.3 %all-to-all-start.1 = ((bf16[4,4,3,128,128]{4,3,2,1,0:T(8,128)(2,1)}), bf16[4,4,3,128,128]{4,3,2,1,0:T(8,128)(2,1)S(1)}, u32[]{:S(2)}, u32[]{:S(2)}) async-start(bf16[4,4,3,128,128]{4,3,2,1,0:T(8,128)(2,1)} %get-tuple-element.49), calls=%async_computation.1 | async-start | bytes 3145728 | tf_op jit(solution)/shard_map/all_to_all | solution.py:154
  75.9 9.1 %collective-permute-start.6 = (bf16[4,128,256]{2,1,0:T(8,128)(2,1)S(1)}, bf16[4,128,256]{2,1,0:T(8,128)(2,1)S(1)}, u32[]{:S(2)}, u32[]{:S(2)}) collective-permute-start(bf16[4,128,256]{2,1,0:T(8,128)(2,1)S(1)} %copy-done.7), channel_id=1, source_target_pairs={{0,32},{32,0},{64,96},{96,64},{1,33},{33,1},{65,97},{97,65},{2,34}... | collective-permute-start | bytes 786440 | tf_op jit(solution)/shard_map/ppermute | solution.py:158
  77.8 6.2 %collective-permute-start.7 = (f32[128,128]{1,0:T(8,128)S(1)}, f32[128,128]{1,0:T(8,128)S(1)}, u32[]{:S(2)}, u32[]{:S(2)}) collective-permute-start(f32[128,128]{1,0:T(8,128)S(1)} %slice_bitcast_fusion.4), channel_id=1, source_target_pairs={{0,1},{1,0},{2,3},{3,2},{4,5},{5,4},{6,7},{7,6},{8,9},{9,8},{10,11... | collective-permute-start | bytes 196616 | tf_op jit(solution)/shard_map/ppermute | solution.py:158
  80.4 23.1 %collective-permute-start.5 = (bf16[4,128,256]{2,1,0:T(8,128)(2,1)S(1)}, bf16[4,128,256]{2,1,0:T(8,128)(2,1)S(1)}, u32[]{:S(2)}, u32[]{:S(2)}) collective-permute-start(bf16[4,128,256]{2,1,0:T(8,128)(2,1)S(1)} %copy-done.6), channel_id=1, source_target_pairs={{0,32},{32,0},{64,96},{96,64},{1,33},{33,1},{65,97},{97,65},{2,34}... | collective-permute-start | bytes 786440 | tf_op jit(solution)/shard_map/ppermute | solution.py:158
  85.0 18.4 %copy-start.5 = (bf16[4,128,256]{2,1,0:T(8,128)(2,1)S(1)}, bf16[4,128,256]{2,1,0:T(8,128)(2,1)}, u32[]{:S(2)}) copy-start(bf16[4,128,256]{2,1,0:T(8,128)(2,1)} %get-tuple-element.42) | copy-start | bytes 786436
  85.1 18.4 %collective-permute-start.8 = (bf16[4,128,256]{2,1,0:T(8,128)(2,1)S(1)}, bf16[4,128,256]{2,1,0:T(8,128)(2,1)S(1)}, u32[]{:S(2)}, u32[]{:S(2)}) collective-permute-start(bf16[4,128,256]{2,1,0:T(8,128)(2,1)S(1)} %add_convert_fusion.2), channel_id=1, source_target_pairs={{0,64},{32,96},{64,0},{96,32},{1,65},{33,97},{65,1},{97,33},{2,66}... | collective-permute-start | bytes 786440 | tf_op jit(solution)/shard_map/ppermute | solution.py:158
  97.0 29.2 %all-to-all-start.2 = ((bf16[4,3,128,128]{3,2,1,0:T(8,128)(2,1)}), bf16[4,3,128,128]{3,2,1,0:T(8,128)(2,1)S(1)}, u32[]{:S(2)}, u32[]{:S(2)}) async-start(bf16[4,3,128,128]{3,2,1,0:T(8,128)(2,1)} %fusion), calls=%async_computation.2 | async-start | bytes 786432 | tf_op jit(solution)/shard_map/all_to_all | solution.py:154
  103.6 9.6 %collective-permute-start.9 = (bf16[128,256]{1,0:T(8,128)(2,1)S(1)}, bf16[128,256]{1,0:T(8,128)(2,1)S(1)}, u32[]{:S(2)}, u32[]{:S(2)}) collective-permute-start(bf16[128,256]{1,0:T(8,128)(2,1)S(1)} %get-tuple-element.53), channel_id=1, source_target_pairs={{0,128},{128,0},{256,384},{384,256},{1,129},{129,1},{257,385},{385... | collective-permute-start | bytes 196616 | tf_op jit(solution)/shard_map/ppermute | solution.py:158
  105.5 7.7 %collective-permute-start.11 = (bf16[128,256]{1,0:T(8,128)(2,1)S(1)}, bf16[128,256]{1,0:T(8,128)(2,1)S(1)}, u32[]{:S(2)}, u32[]{:S(2)}) collective-permute-start(bf16[128,256]{1,0:T(8,128)(2,1)S(1)} %get-tuple-element.54), channel_id=1, source_target_pairs={{0,384},{128,256},{256,128},{384,0},{1,385},{129,257},{257,129},{3... | collective-permute-start | bytes 196616 | tf_op jit(solution)/shard_map/ppermute | solution.py:158
  108.3 6.5 %collective-permute-start.10 = (bf16[128,256]{1,0:T(8,128)(2,1)S(1)}, bf16[128,256]{1,0:T(8,128)(2,1)S(1)}, u32[]{:S(2)}, u32[]{:S(2)}) collective-permute-start(bf16[128,256]{1,0:T(8,128)(2,1)S(1)} %get-tuple-element.55), channel_id=1, source_target_pairs={{0,256},{128,384},{256,0},{384,128},{1,257},{129,385},{257,1},{385... | collective-permute-start | bytes 196616 | tf_op jit(solution)/shard_map/ppermute | solution.py:158

commit v8 on v6

--- a/solution.py
+++ b/solution.py
@@ -229,14 +229,12 @@
     pay = exchange(pay, "x")
     passing = trade(outs[3], "zl", 1)
     near = trade(outs[1], "zl", 1)
-    dq_got = trade(dq[1], "c", 1)
-    passing, dq_got = lax.optimization_barrier((passing, dq_got))
     far = trade(add_all([outs[2], passing]).astype(BF16), "zl", 2)
     pay = add_all([pay[r] for r in range(4)]).astype(BF16)
     pay = exchange(pay, "zh")
     out = add_all([outs[0], near, far]).astype(BF16)
     out = add_all([out[0]] + [trade(out[t], "y", t) for t in (1, 2, 3)]).astype(BF16)
-    dq = ((dq[0] + dq_got) * SCALE).astype(BF16)
+    dq = ((dq[0] + trade(dq[1], "c", 1)) * SCALE).astype(BF16)
     dk, dv, dw = call(
         finish_kernel, "finish", (tile, tile, shape((BLK, BLK), F32)), [VMEM], 4, 0, 1 << 20
     )(pay)

time: 127 us -> 127 us (level)
    all_to_all x3, waiting for transfers between devices: 16.5 us -> 13.6 us  [exchange(): return lax.all_to_all(blocks, axis, 0, 0, tiled=True)]
    ppermute x13, waiting for transfers between devices: 14.7 us -> 17.4 us  [trade(): lax.ppermute(block, axis, [(i, i ^ step) for i in range(2 if axis == 'c'...]
where the time goes in v8:
time: 127 us; the launch traced here: 126 us
  starting transfers between devices  56 us (44%)
  waiting for transfers between devices  31 us (24%)
  blocking collectives  26 us (20%)
  Pallas kernels  7.43 us (6%)
  other arithmetic  2.51 us (2%)
  local copies, waits for them, and re-layouts  2.48 us (2%)
    ppermute x13, starting transfers between devices, trade(): lax.ppermute(block, axis, [(i, i ^ step) for i in range(2 if axis == 'c'...  37.8 us
    all_gather x1, blocking collectives, body(): kv = lax.all_gather(kv, 'zh', axis=0, tiled=True).reshape(4, 2, BLK, HDIM)  26 us
    all_to_all x3, starting transfers between devices, exchange(): return lax.all_to_all(blocks, axis, 0, 0, tiled=True)  18.2 us
    ppermute x13, waiting for transfers between devices, trade(): lax.ppermute(block, axis, [(i, i ^ step) for i in range(2 if axis == 'c'...  17.4 us
    all_to_all x3, waiting for transfers between devices, exchange(): return lax.all_to_all(blocks, axis, 0, 0, tiled=True)  13.6 us
    pallas_call x1, Pallas kernels, body(): call(backward_kernel, 'backward', (shape((2, BLK, HDIM), F32), pltpu.HBM(...  3.62 us
  transfers between devices with their start and end apart: 16, of which 10 were waited for; matrix products, arithmetic and copies ran while one was open for 2% of the time, Pallas kernels for 1%

profile of v8, /device:TPU:32, one launch (start us, length us, event | category | flops | bytes accessed | tf_op | source)
XLA Modules:
  0.0 126.3 jit_solution(4597342129527583762)
XLA Ops:
  0.6 0.9 pack.1
  1.5 26.0 %all_gather.3 = bf16[1024,128]{1,0:T(8,128)(2,1)S(1)} all-gather(bf16[256,128]{1,0:T(8,128)(2,1)S(1)} %get-tuple-element.27), channel_id=1, replica_groups=mesh['y'=4,'zl'=4,'zh'=4,'x'=4,'c'=2] {'zh'}, dimensions={0}, use_global_device_ids=true | all-gather | bytes 327680 | tf_op jit(solution)/shard_map/all_gather | solution.py:183
  27.5 0.1 pad_add_fusion.place_ref
  27.6 0.0 copy-start.3
  27.6 1.1 broadcast_in_dim.2
  28.7 0.0 copy-start
  28.7 7.4 %all-to-all-start = ((bf16[16,128,256]{2,1,0:T(8,128)(2,1)}), bf16[16,128,256]{2,1,0:T(8,128)(2,1)S(1)}, u32[]{:S(2)}, u32[]{:S(2)}) async-start(bf16[16,128,256]{2,1,0:T(8,128)(2,1)} %broadcast_in_dim.2), calls=%async_computation | async-start | bytes 2097152 | tf_op jit(solution)/shard_map/all_to_all | solution.py:138
  36.0 4.7 %collective-permute-start.3 = (bf16[4,2,128,128]{3,2,1,0:T(8,128)(2,1)S(1)}, bf16[4,2,128,128]{3,2,1,0:T(8,128)(2,1)S(1)}, u32[]{:S(2)}, u32[]{:S(2)}) collective-permute-start(bf16[4,2,128,128]{3,2,1,0:T(8,128)(2,1)S(1)} %bitcast.26), channel_id=1, source_target_pairs={{0,6},{2,4},{4,2},{6,0},{1,7},{3,5},{5,3},{7,1},{8,14},{10,12},{12... | collective-permute-start | bytes 786440 | tf_op jit(solution)/shard_map/ppermute | solution.py:142
  40.7 2.7 %collective-permute-start.2 = (bf16[4,2,128,128]{3,2,1,0:T(8,128)(2,1)S(1)}, bf16[4,2,128,128]{3,2,1,0:T(8,128)(2,1)S(1)}, u32[]{:S(2)}, u32[]{:S(2)}) collective-permute-start(bf16[4,2,128,128]{3,2,1,0:T(8,128)(2,1)S(1)} %bitcast.27), channel_id=1, source_target_pairs={{0,4},{2,6},{4,0},{6,2},{1,5},{3,7},{5,1},{7,3},{8,12},{10,14},{12... | collective-permute-start | bytes 786440 | tf_op jit(solution)/shard_map/ppermute | solution.py:142
  43.4 2.4 %collective-permute-start.1 = (bf16[4,2,128,128]{3,2,1,0:T(8,128)(2,1)S(1)}, bf16[4,2,128,128]{3,2,1,0:T(8,128)(2,1)S(1)}, u32[]{:S(2)}, u32[]{:S(2)}) collective-permute-start(bf16[4,2,128,128]{3,2,1,0:T(8,128)(2,1)S(1)} %bitcast.28), channel_id=1, source_target_pairs={{0,2},{2,0},{4,6},{6,4},{1,3},{3,1},{5,7},{7,5},{8,10},{10,8},{12,... | collective-permute-start | bytes 786440 | tf_op jit(solution)/shard_map/ppermute | solution.py:142
  45.9 0.0 copy-done.3
  45.9 1.9 %collective-permute-start = (bf16[128,128]{1,0:T(8,128)(2,1)S(1)}, bf16[128,128]{1,0:T(8,128)(2,1)S(1)}, u32[]{:S(2)}, u32[]{:S(2)}) collective-permute-start(bf16[128,128]{1,0:T(8,128)(2,1)S(1)} %copy-done.3), channel_id=1, source_target_pairs={{0,1},{1,0},{2,3},{3,2},{4,5},{5,4},{6,7},{7,6},{8,9},{9,8},{10,11... | collective-permute-start | bytes 98312 | tf_op jit(solution)/shard_map/ppermute | solution.py:142
  47.8 1.2 collective-permute-done.other_ref
  49.0 0.0 collective-permute-done.3.kv3
  49.0 2.4 %collective-permute-done.2.kv2 = bf16[4,2,128,128]{3,2,1,0:T(8,128)(2,1)S(1)} collective-permute-done((bf16[4,2,128,128]{3,2,1,0:T(8,128)(2,1)S(1)}, bf16[4,2,128,128]{3,2,1,0:T(8,128)(2,1)S(1)}, u32[]{:S(2)}, u32[]{:S(2)}) %collective-permute-start.2) | collective-permute-done | bytes 262176 | tf_op jit(solution)/shard_map/ppermute | solution.py:142
  51.3 0.9 collective-permute-done.1.kv1
  52.3 1.2 forward.1.mine_ref
  53.5 1.9 %collective-permute-start.4 = (f32[256,256]{1,0:T(8,128)S(1)}, f32[256,256]{1,0:T(8,128)S(1)}, u32[]{:S(2)}, u32[]{:S(2)}) collective-permute-start(f32[256,256]{1,0:T(8,128)S(1)} %forward.1.mine_ref), channel_id=1, source_target_pairs={{0,1},{1,0},{2,3},{3,2},{4,5},{5,4},{6,7},{7,6},{8,9},{9,8},{10,11... | collective-permute-start | bytes 786440 | tf_op jit(solution)/shard_map/ppermute | solution.py:142
  55.4 1.5 %collective-permute-done.4.theirs_ref = f32[256,256]{1,0:T(8,128)S(1)} collective-permute-done((f32[256,256]{1,0:T(8,128)S(1)}, f32[256,256]{1,0:T(8,128)S(1)}, u32[]{:S(2)}, u32[]{:S(2)}) %collective-permute-start.4) | collective-permute-done | bytes 262176 | tf_op jit(solution)/shard_map/ppermute | solution.py:142
  56.9 0.0 copy-start.1
  56.9 0.7 copy-done.1
  57.6 0.0 all-to-all-done.cot_ref
  57.6 0.0 copy-done
  57.6 0.0 copy-start.2
  57.6 1.0 cotangent.1.gift_ref
  58.6 2.0 %collective-permute-start.5 = (bf16[17,128,128]{2,1,0:T(8,128)(2,1)S(1)}, bf16[17,128,128]{2,1,0:T(8,128)(2,1)S(1)}, u32[]{:S(2)}, u32[]{:S(2)}) collective-permute-start(bf16[17,128,128]{2,1,0:T(8,128)(2,1)S(1)} %cotangent.1.gift_ref), channel_id=1, source_target_pairs={{0,1},{1,0},{2,3},{3,2},{4,5},{5,4},{6,7},{7,6},{8,9},{9,8},{10,11... | collective-permute-start | bytes 1671176 | tf_op jit(solution)/shard_map/ppermute | solution.py:142
  60.6 1.8 %collective-permute-done.5.got_ref = bf16[17,128,128]{2,1,0:T(8,128)(2,1)S(1)} collective-permute-done((bf16[17,128,128]{2,1,0:T(8,128)(2,1)S(1)}, bf16[17,128,128]{2,1,0:T(8,128)(2,1)S(1)}, u32[]{:S(2)}, u32[]{:S(2)}) %collective-permute-start.5) | collective-permute-done | bytes 557088 | tf_op jit(solution)/shard_map/ppermute | solution.py:142
  62.5 0.0 copy-done.2
  62.5 3.6 %backward.1 = (f32[2,128,128]{2,1,0:T(8,128)S(1)}, bf16[4,4,3,128,128]{4,3,2,1,0:T(8,128)(2,1)}, bf16[4,128,256]{2,1,0:T(8,128)(2,1)}, bf16[4,128,256]{2,1,0:T(8...) custom-call(s32[4]{0:T(128)S(1)} %pad_add_fusion.place_ref, bf16[128,128]{1,0:T(8,128)(2,1)S(1)} %copy-done.3, ...), custom_call_target="tpu_custom_call" | custom-call | flops 939524096 | bytes 8388608 | tf_op jit(solution)/shard_map/backward/pallas_call | solution.py:211
  66.1 0.0 copy-start.4
  66.1 0.6 copy-done.4
  66.7 0.0 copy-start.9
  66.7 0.0 copy-start.8
  66.7 4.1 %all-to-all-start.1 = ((bf16[4,4,3,128,128]{4,3,2,1,0:T(8,128)(2,1)}), bf16[4,4,3,128,128]{4,3,2,1,0:T(8,128)(2,1)S(1)}, u32[]{:S(2)}, u32[]{:S(2)}) async-start(bf16[4,4,3,128,128]{4,3,2,1,0:T(8,128)(2,1)} %get-tuple-element.45), calls=%async_computation.1 | async-start | bytes 3145728 | tf_op jit(solution)/shard_map/all_to_all | solution.py:138
  70.9 0.0 copy-done.9
  70.9 5.7 %collective-permute-start.7 = (bf16[4,128,256]{2,1,0:T(8,128)(2,1)S(1)}, bf16[4,128,256]{2,1,0:T(8,128)(2,1)S(1)}, u32[]{:S(2)}, u32[]{:S(2)}) collective-permute-start(bf16[4,128,256]{2,1,0:T(8,128)(2,1)S(1)} %copy-done.9), channel_id=1, source_target_pairs={{0,32},{32,0},{64,96},{96,64},{1,33},{33,1},{65,97},{97,65},{2,34}... | collective-permute-start | bytes 786440 | tf_op jit(solution)/shard_map/ppermute | solution.py:142
  76.6 0.0 copy-done.8
  76.6 1.9 %collective-permute-start.6 = (bf16[4,128,256]{2,1,0:T(8,128)(2,1)S(1)}, bf16[4,128,256]{2,1,0:T(8,128)(2,1)S(1)}, u32[]{:S(2)}, u32[]{:S(2)}) collective-permute-start(bf16[4,128,256]{2,1,0:T(8,128)(2,1)S(1)} %copy-done.8), channel_id=1, source_target_pairs={{0,32},{32,0},{64,96},{96,64},{1,33},{33,1},{65,97},{97,65},{2,34}... | collective-permute-start | bytes 786440 | tf_op jit(solution)/shard_map/ppermute | solution.py:142
  78.5 5.2 %collective-permute-done.7 = bf16[4,128,256]{2,1,0:T(8,128)(2,1)S(1)} collective-permute-done((bf16[4,128,256]{2,1,0:T(8,128)(2,1)S(1)}, bf16[4,128,256]{2,1,0:T(8,128)(2,1)S(1)}, u32[]{:S(2)}, u32[]{:S(2)}) %collective-permute-start.7) | collective-permute-done | bytes 262176 | tf_op jit(solution)/shard_map/ppermute | solution.py:142
  83.7 0.0 copy-done.6
  83.7 0.1 add_convert_fusion.2
  83.8 0.0 copy-start.5
  83.8 0.0 copy-start.7
  83.8 2.6 %collective-permute-start.8 = (bf16[4,128,256]{2,1,0:T(8,128)(2,1)S(1)}, bf16[4,128,256]{2,1,0:T(8,128)(2,1)S(1)}, u32[]{:S(2)}, u32[]{:S(2)}) collective-permute-start(bf16[4,128,256]{2,1,0:T(8,128)(2,1)S(1)} %add_convert_fusion.2), channel_id=1, source_target_pairs={{0,64},{32,96},{64,0},{96,32},{1,65},{33,97},{65,1},{97,33},{2,66}... | collective-permute-start | bytes 786440 | tf_op jit(solution)/shard_map/ppermute | solution.py:142
  86.4 5.4 %all-to-all-done.1 = bf16[4,4,3,128,128]{4,3,2,1,0:T(8,128)(2,1)S(1)} async-done(((bf16[4,4,3,128,128]{4,3,2,1,0:T(8,128)(2,1)}), bf16[4,4,3,128,128]{4,3,2,1,0:T(8,128)(2,1)S(1)}, u32[]{:S(2)}, u32[]{:S(2)}) %all-to-all-start.1) | async-done | bytes 1572896 | tf_op jit(solution)/shard_map/all_to_all | solution.py:138
  91.9 1.0 fusion
  92.9 6.7 %all-to-all-start.2 = ((bf16[4,3,128,128]{3,2,1,0:T(8,128)(2,1)}), bf16[4,3,128,128]{3,2,1,0:T(8,128)(2,1)S(1)}, u32[]{:S(2)}, u32[]{:S(2)}) async-start(bf16[4,3,128,128]{3,2,1,0:T(8,128)(2,1)} %fusion), calls=%async_computation.2 | async-start | bytes 786432 | tf_op jit(solution)/shard_map/all_to_all | solution.py:138
  99.6 0.0 copy-done.5
  99.6 1.9 %collective-permute-start.12 = (f32[128,128]{1,0:T(8,128)S(1)}, f32[128,128]{1,0:T(8,128)S(1)}, u32[]{:S(2)}, u32[]{:S(2)}) collective-permute-start(f32[128,128]{1,0:T(8,128)S(1)} %slice_bitcast_fusion.4), channel_id=1, source_target_pairs={{0,1},{1,0},{2,3},{3,2},{4,5},{5,4},{6,7},{7,6},{8,9},{9,8},{10,11... | collective-permute-start | bytes 196616 | tf_op jit(solution)/shard_map/ppermute | solution.py:142
  101.5 0.0 collective-permute-done.6
  101.6 0.0 collective-permute-done.8
  101.6 0.0 copy-done.7
  101.6 0.1 add_convert_fusion.1
  101.7 3.4 %collective-permute-start.9 = (bf16[128,256]{1,0:T(8,128)(2,1)S(1)}, bf16[128,256]{1,0:T(8,128)(2,1)S(1)}, u32[]{:S(2)}, u32[]{:S(2)}) collective-permute-start(bf16[128,256]{1,0:T(8,128)(2,1)S(1)} %get-tuple-element.49), channel_id=1, source_target_pairs={{0,128},{128,0},{256,384},{384,256},{1,129},{129,1},{257,385},{385... | collective-permute-start | bytes 196616 | tf_op jit(solution)/shard_map/ppermute | solution.py:142
  105.1 4.0 %collective-permute-start.11 = (bf16[128,256]{1,0:T(8,128)(2,1)S(1)}, bf16[128,256]{1,0:T(8,128)(2,1)S(1)}, u32[]{:S(2)}, u32[]{:S(2)}) collective-permute-start(bf16[128,256]{1,0:T(8,128)(2,1)S(1)} %get-tuple-element.50), channel_id=1, source_target_pairs={{0,384},{128,256},{256,128},{384,0},{1,385},{129,257},{257,129},{3... | collective-permute-start | bytes 196616 | tf_op jit(solution)/shard_map/ppermute | solution.py:142
  109.1 2.5 %collective-permute-start.10 = (bf16[128,256]{1,0:T(8,128)(2,1)S(1)}, bf16[128,256]{1,0:T(8,128)(2,1)S(1)}, u32[]{:S(2)}, u32[]{:S(2)}) collective-permute-start(bf16[128,256]{1,0:T(8,128)(2,1)S(1)} %get-tuple-element.51), channel_id=1, source_target_pairs={{0,256},{128,384},{256,0},{384,128},{1,257},{129,385},{257,1},{385... | collective-permute-start | bytes 196616 | tf_op jit(solution)/shard_map/ppermute | solution.py:142
  111.6 0.0 collective-permute-done.12
  111.6 0.6 fusion.5
  112.2 0.0 collective-permute-done.9
  112.2 0.2 collective-permute-done.11
  112.5 4.3 %collective-permute-done.10 = bf16[128,256]{1,0:T(8,128)(2,1)S(1)} collective-permute-done((bf16[128,256]{1,0:T(8,128)(2,1)S(1)}, bf16[128,256]{1,0:T(8,128)(2,1)S(1)}, u32[]{:S(2)}, u32[]{:S(2)}) %collective-permute-start.10) | collective-permute-done | bytes 65568 | tf_op jit(solution)/shard_map/ppermute | solution.py:142
  116.7 0.7 fusion.3
  117.4 8.1 %all-to-all-done.2.parts_ref = bf16[4,3,128,128]{3,2,1,0:T(8,128)(2,1)S(1)} async-done(((bf16[4,3,128,128]{3,2,1,0:T(8,128)(2,1)}), bf16[4,3,128,128]{3,2,1,0:T(8,128)(2,1)S(1)}, u32[]{:S(2)}, u32[]{:S(2)}) %all-to-all-start.2) | async-done | bytes 393248 | tf_op jit(solution)/shard_map/all_to_all | solution.py:138
  125.5 0.8 finish.1
  (3 shorter events, 0.0 us)
Async XLA Ops:
  27.6 18.3 %copy-start.3 = (bf16[128,128]{1,0:T(8,128)(2,1)S(1)}, bf16[128,128]{1,0:T(8,128)(2,1)}, u32[]{:S(2)}) copy-start(bf16[128,128]{1,0:T(8,128)(2,1)} %q_ref.3) | copy-start | bytes 98308
  28.7 28.9 %copy-start = (bf16[128,4096]{1,0:T(8,128)(2,1)S(1)}, bf16[128,4096]{1,0:T(8,128)(2,1)}, u32[]{:S(2)}) copy-start(bf16[128,4096]{1,0:T(8,128)(2,1)} %w_ref.3) | copy-start | bytes 3145732
  28.7 28.9 %all-to-all-start = ((bf16[16,128,256]{2,1,0:T(8,128)(2,1)}), bf16[16,128,256]{2,1,0:T(8,128)(2,1)S(1)}, u32[]{:S(2)}, u32[]{:S(2)}) async-start(bf16[16,128,256]{2,1,0:T(8,128)(2,1)} %broadcast_in_dim.2), calls=%async_computation | async-start | bytes 2097152 | tf_op jit(solution)/shard_map/all_to_all | solution.py:138
  36.0 12.9 %collective-permute-start.3 = (bf16[4,2,128,128]{3,2,1,0:T(8,128)(2,1)S(1)}, bf16[4,2,128,128]{3,2,1,0:T(8,128)(2,1)S(1)}, u32[]{:S(2)}, u32[]{:S(2)}) collective-permute-start(bf16[4,2,128,128]{3,2,1,0:T(8,128)(2,1)S(1)} %bitcast.26), channel_id=1, source_target_pairs={{0,6},{2,4},{4,2},{6,0},{1,7},{3,5},{5,3},{7,1},{8,14},{10,12},{12... | collective-permute-start | bytes 786440 | tf_op jit(solution)/shard_map/ppermute | solution.py:142
  40.7 10.7 %collective-permute-start.2 = (bf16[4,2,128,128]{3,2,1,0:T(8,128)(2,1)S(1)}, bf16[4,2,128,128]{3,2,1,0:T(8,128)(2,1)S(1)}, u32[]{:S(2)}, u32[]{:S(2)}) collective-permute-start(bf16[4,2,128,128]{3,2,1,0:T(8,128)(2,1)S(1)} %bitcast.27), channel_id=1, source_target_pairs={{0,4},{2,6},{4,0},{6,2},{1,5},{3,7},{5,1},{7,3},{8,12},{10,14},{12... | collective-permute-start | bytes 786440 | tf_op jit(solution)/shard_map/ppermute | solution.py:142
  43.4 8.9 %collective-permute-start.1 = (bf16[4,2,128,128]{3,2,1,0:T(8,128)(2,1)S(1)}, bf16[4,2,128,128]{3,2,1,0:T(8,128)(2,1)S(1)}, u32[]{:S(2)}, u32[]{:S(2)}) collective-permute-start(bf16[4,2,128,128]{3,2,1,0:T(8,128)(2,1)S(1)} %bitcast.28), channel_id=1, source_target_pairs={{0,2},{2,0},{4,6},{6,4},{1,3},{3,1},{5,7},{7,5},{8,10},{10,8},{12,... | collective-permute-start | bytes 786440 | tf_op jit(solution)/shard_map/ppermute | solution.py:142
  45.9 3.1 %collective-permute-start = (bf16[128,128]{1,0:T(8,128)(2,1)S(1)}, bf16[128,128]{1,0:T(8,128)(2,1)S(1)}, u32[]{:S(2)}, u32[]{:S(2)}) collective-permute-start(bf16[128,128]{1,0:T(8,128)(2,1)S(1)} %copy-done.3), channel_id=1, source_target_pairs={{0,1},{1,0},{2,3},{3,2},{4,5},{5,4},{6,7},{7,6},{8,9},{9,8},{10,11... | collective-permute-start | bytes 98312 | tf_op jit(solution)/shard_map/ppermute | solution.py:142
  53.5 3.4 %collective-permute-start.4 = (f32[256,256]{1,0:T(8,128)S(1)}, f32[256,256]{1,0:T(8,128)S(1)}, u32[]{:S(2)}, u32[]{:S(2)}) collective-permute-start(f32[256,256]{1,0:T(8,128)S(1)} %forward.1.mine_ref), channel_id=1, source_target_pairs={{0,1},{1,0},{2,3},{3,2},{4,5},{5,4},{6,7},{7,6},{8,9},{9,8},{10,11... | collective-permute-start | bytes 786440 | tf_op jit(solution)/shard_map/ppermute | solution.py:142
  56.9 0.7 copy-start.1
  57.6 4.9 %copy-start.2 = (f32[256,256]{1,0:T(8,128)S(1)}, f32[256,256]{1,0:T(8,128)}, u32[]{:S(2)}) copy-start(f32[256,256]{1,0:T(8,128)} %copy-done.1) | copy-start | bytes 786436
  58.6 3.9 %collective-permute-start.5 = (bf16[17,128,128]{2,1,0:T(8,128)(2,1)S(1)}, bf16[17,128,128]{2,1,0:T(8,128)(2,1)S(1)}, u32[]{:S(2)}, u32[]{:S(2)}) collective-permute-start(bf16[17,128,128]{2,1,0:T(8,128)(2,1)S(1)} %cotangent.1.gift_ref), channel_id=1, source_target_pairs={{0,1},{1,0},{2,3},{3,2},{4,5},{5,4},{6,7},{7,6},{8,9},{9,8},{10,11... | collective-permute-start | bytes 1671176 | tf_op jit(solution)/shard_map/ppermute | solution.py:142
  66.1 0.6 copy-start.4
  66.7 4.1 %copy-start.9 = (bf16[4,128,256]{2,1,0:T(8,128)(2,1)S(1)}, bf16[4,128,256]{2,1,0:T(8,128)(2,1)}, u32[]{:S(2)}) copy-start(bf16[4,128,256]{2,1,0:T(8,128)(2,1)} %get-tuple-element.43) | copy-start | bytes 786436
  66.7 9.9 %copy-start.8 = (bf16[4,128,256]{2,1,0:T(8,128)(2,1)S(1)}, bf16[4,128,256]{2,1,0:T(8,128)(2,1)}, u32[]{:S(2)}) copy-start(bf16[4,128,256]{2,1,0:T(8,128)(2,1)} %get-tuple-element.41) | copy-start | bytes 786436
  66.7 17.0 %copy-start.6 = (bf16[4,128,256]{2,1,0:T(8,128)(2,1)S(1)}, bf16[4,128,256]{2,1,0:T(8,128)(2,1)}, u32[]{:S(2)}) copy-start(bf16[4,128,256]{2,1,0:T(8,128)(2,1)} %get-tuple-element.42) | copy-start | bytes 786436
  66.7 25.2 %all-to-all-start.1 = ((bf16[4,4,3,128,128]{4,3,2,1,0:T(8,128)(2,1)}), bf16[4,4,3,128,128]{4,3,2,1,0:T(8,128)(2,1)S(1)}, u32[]{:S(2)}, u32[]{:S(2)}) async-start(bf16[4,4,3,128,128]{4,3,2,1,0:T(8,128)(2,1)} %get-tuple-element.45), calls=%async_computation.1 | async-start | bytes 3145728 | tf_op jit(solution)/shard_map/all_to_all | solution.py:138
  70.9 12.8 %collective-permute-start.7 = (bf16[4,128,256]{2,1,0:T(8,128)(2,1)S(1)}, bf16[4,128,256]{2,1,0:T(8,128)(2,1)S(1)}, u32[]{:S(2)}, u32[]{:S(2)}) collective-permute-start(bf16[4,128,256]{2,1,0:T(8,128)(2,1)S(1)} %copy-done.9), channel_id=1, source_target_pairs={{0,32},{32,0},{64,96},{96,64},{1,33},{33,1},{65,97},{97,65},{2,34}... | collective-permute-start | bytes 786440 | tf_op jit(solution)/shard_map/ppermute | solution.py:142
  76.6 24.9 %collective-permute-start.6 = (bf16[4,128,256]{2,1,0:T(8,128)(2,1)S(1)}, bf16[4,128,256]{2,1,0:T(8,128)(2,1)S(1)}, u32[]{:S(2)}, u32[]{:S(2)}) collective-permute-start(bf16[4,128,256]{2,1,0:T(8,128)(2,1)S(1)} %copy-done.8), channel_id=1, source_target_pairs={{0,32},{32,0},{64,96},{96,64},{1,33},{33,1},{65,97},{97,65},{2,34}... | collective-permute-start | bytes 786440 | tf_op jit(solution)/shard_map/ppermute | solution.py:142
  83.8 15.8 %copy-start.5 = (f32[2,128,128]{2,1,0:T(8,128)S(1)}, f32[2,128,128]{2,1,0:T(8,128)}, u32[]{:S(2)}) copy-start(f32[2,128,128]{2,1,0:T(8,128)} %copy-done.4) | copy-start | bytes 393220
  83.8 17.8 %copy-start.7 = (bf16[4,128,256]{2,1,0:T(8,128)(2,1)S(1)}, bf16[4,128,256]{2,1,0:T(8,128)(2,1)}, u32[]{:S(2)}) copy-start(bf16[4,128,256]{2,1,0:T(8,128)(2,1)} %get-tuple-element.40) | copy-start | bytes 786436
  83.8 17.8 %collective-permute-start.8 = (bf16[4,128,256]{2,1,0:T(8,128)(2,1)S(1)}, bf16[4,128,256]{2,1,0:T(8,128)(2,1)S(1)}, u32[]{:S(2)}, u32[]{:S(2)}) collective-permute-start(bf16[4,128,256]{2,1,0:T(8,128)(2,1)S(1)} %add_convert_fusion.2), channel_id=1, source_target_pairs={{0,64},{32,96},{64,0},{96,32},{1,65},{33,97},{65,1},{97,33},{2,66}... | collective-permute-start | bytes 786440 | tf_op jit(solution)/shard_map/ppermute | solution.py:142
  92.9 32.7 %all-to-all-start.2 = ((bf16[4,3,128,128]{3,2,1,0:T(8,128)(2,1)}), bf16[4,3,128,128]{3,2,1,0:T(8,128)(2,1)S(1)}, u32[]{:S(2)}, u32[]{:S(2)}) async-start(bf16[4,3,128,128]{3,2,1,0:T(8,128)(2,1)} %fusion), calls=%async_computation.2 | async-start | bytes 786432 | tf_op jit(solution)/shard_map/all_to_all | solution.py:138
  99.6 12.0 %collective-permute-start.12 = (f32[128,128]{1,0:T(8,128)S(1)}, f32[128,128]{1,0:T(8,128)S(1)}, u32[]{:S(2)}, u32[]{:S(2)}) collective-permute-start(f32[128,128]{1,0:T(8,128)S(1)} %slice_bitcast_fusion.4), channel_id=1, source_target_pairs={{0,1},{1,0},{2,3},{3,2},{4,5},{5,4},{6,7},{7,6},{8,9},{9,8},{10,11... | collective-permute-start | bytes 196616 | tf_op jit(solution)/shard_map/ppermute | solution.py:142
  101.7 10.5 %collective-permute-start.9 = (bf16[128,256]{1,0:T(8,128)(2,1)S(1)}, bf16[128,256]{1,0:T(8,128)(2,1)S(1)}, u32[]{:S(2)}, u32[]{:S(2)}) collective-permute-start(bf16[128,256]{1,0:T(8,128)(2,1)S(1)} %get-tuple-element.49), channel_id=1, source_target_pairs={{0,128},{128,0},{256,384},{384,256},{1,129},{129,1},{257,385},{385... | collective-permute-start | bytes 196616 | tf_op jit(solution)/shard_map/ppermute | solution.py:142
  105.1 7.4 %collective-permute-start.11 = (bf16[128,256]{1,0:T(8,128)(2,1)S(1)}, bf16[128,256]{1,0:T(8,128)(2,1)S(1)}, u32[]{:S(2)}, u32[]{:S(2)}) collective-permute-start(bf16[128,256]{1,0:T(8,128)(2,1)S(1)} %get-tuple-element.50), channel_id=1, source_target_pairs={{0,384},{128,256},{256,128},{384,0},{1,385},{129,257},{257,129},{3... | collective-permute-start | bytes 196616 | tf_op jit(solution)/shard_map/ppermute | solution.py:142
  109.1 7.7 %collective-permute-start.10 = (bf16[128,256]{1,0:T(8,128)(2,1)S(1)}, bf16[128,256]{1,0:T(8,128)(2,1)S(1)}, u32[]{:S(2)}, u32[]{:S(2)}) collective-permute-start(bf16[128,256]{1,0:T(8,128)(2,1)S(1)} %get-tuple-element.51), channel_id=1, source_target_pairs={{0,256},{128,384},{256,0},{384,128},{1,257},{129,385},{257,1},{385... | collective-permute-start | bytes 196616 | tf_op jit(solution)/shard_map/ppermute | solution.py:142

commit v9 on v6

--- a/solution.py
+++ b/solution.py
@@ -230,7 +230,7 @@
     passing = trade(outs[3], "zl", 1)
     near = trade(outs[1], "zl", 1)
     dq_got = trade(dq[1], "c", 1)
-    passing, dq_got = lax.optimization_barrier((passing, dq_got))
+    pay, dq_got = lax.optimization_barrier((pay, dq_got))
     far = trade(add_all([outs[2], passing]).astype(BF16), "zl", 2)
     pay = add_all([pay[r] for r in range(4)]).astype(BF16)
     pay = exchange(pay, "zh")

time: 127 us -> 127 us (level)
  no operation moved by 1% of the time
where the time goes in v9:
time: 127 us; the launch traced here: 126 us
  starting transfers between devices  55.8 us (44%)
  waiting for transfers between devices  31.2 us (25%)
  blocking collectives  26 us (20%)
  Pallas kernels  7.43 us (6%)
  other arithmetic  2.51 us (2%)
  local copies, waits for them, and re-layouts  2.48 us (2%)
    ppermute x13, starting transfers between devices, trade(): lax.ppermute(block, axis, [(i, i ^ step) for i in range(2 if axis == 'c'...  37.6 us
    all_gather x1, blocking collectives, body(): kv = lax.all_gather(kv, 'zh', axis=0, tiled=True).reshape(4, 2, BLK, HDIM)  26 us
    all_to_all x3, starting transfers between devices, exchange(): return lax.all_to_all(blocks, axis, 0, 0, tiled=True)  18.3 us
    all_to_all x3, waiting for transfers between devices, exchange(): return lax.all_to_all(blocks, axis, 0, 0, tiled=True)  15.9 us
    ppermute x13, waiting for transfers between devices, trade(): lax.ppermute(block, axis, [(i, i ^ step) for i in range(2 if axis == 'c'...  15.3 us
    pallas_call x1, Pallas kernels, body(): call(backward_kernel, 'backward', (shape((2, BLK, HDIM), F32), pltpu.HBM(...  3.62 us
  transfers between devices with their start and end apart: 16, of which 10 were waited for; matrix products, arithmetic and copies ran while one was open for 2% of the time, Pallas kernels for 1%

profile of v9, /device:TPU:32, one launch (start us, length us, event | category | flops | bytes accessed | tf_op | source)
XLA Modules:
  0.0 126.3 jit_solution(3258217306186246078)
XLA Ops:
  0.6 0.9 pack.1
  1.5 26.0 %all_gather.3 = bf16[1024,128]{1,0:T(8,128)(2,1)S(1)} all-gather(bf16[256,128]{1,0:T(8,128)(2,1)S(1)} %get-tuple-element.29), channel_id=1, replica_groups=mesh['y'=4,'zl'=4,'zh'=4,'x'=4,'c'=2] {'zh'}, dimensions={0}, use_global_device_ids=true | all-gather | bytes 327680 | tf_op jit(solution)/shard_map/all_gather | solution.py:183
  27.5 0.1 pad_add_fusion.place_ref
  27.6 0.0 copy-start.3
  27.6 1.1 broadcast_in_dim.2
  28.7 0.0 copy-start
  28.7 7.4 %all-to-all-start = ((bf16[16,128,256]{2,1,0:T(8,128)(2,1)}), bf16[16,128,256]{2,1,0:T(8,128)(2,1)S(1)}, u32[]{:S(2)}, u32[]{:S(2)}) async-start(bf16[16,128,256]{2,1,0:T(8,128)(2,1)} %broadcast_in_dim.2), calls=%async_computation | async-start | bytes 2097152 | tf_op jit(solution)/shard_map/all_to_all | solution.py:138
  36.0 4.7 %collective-permute-start.3 = (bf16[4,2,128,128]{3,2,1,0:T(8,128)(2,1)S(1)}, bf16[4,2,128,128]{3,2,1,0:T(8,128)(2,1)S(1)}, u32[]{:S(2)}, u32[]{:S(2)}) collective-permute-start(bf16[4,2,128,128]{3,2,1,0:T(8,128)(2,1)S(1)} %bitcast.26), channel_id=1, source_target_pairs={{0,6},{2,4},{4,2},{6,0},{1,7},{3,5},{5,3},{7,1},{8,14},{10,12},{12... | collective-permute-start | bytes 786440 | tf_op jit(solution)/shard_map/ppermute | solution.py:142
  40.7 2.7 %collective-permute-start.2 = (bf16[4,2,128,128]{3,2,1,0:T(8,128)(2,1)S(1)}, bf16[4,2,128,128]{3,2,1,0:T(8,128)(2,1)S(1)}, u32[]{:S(2)}, u32[]{:S(2)}) collective-permute-start(bf16[4,2,128,128]{3,2,1,0:T(8,128)(2,1)S(1)} %bitcast.27), channel_id=1, source_target_pairs={{0,4},{2,6},{4,0},{6,2},{1,5},{3,7},{5,1},{7,3},{8,12},{10,14},{12... | collective-permute-start | bytes 786440 | tf_op jit(solution)/shard_map/ppermute | solution.py:142
  43.4 2.4 %collective-permute-start.1 = (bf16[4,2,128,128]{3,2,1,0:T(8,128)(2,1)S(1)}, bf16[4,2,128,128]{3,2,1,0:T(8,128)(2,1)S(1)}, u32[]{:S(2)}, u32[]{:S(2)}) collective-permute-start(bf16[4,2,128,128]{3,2,1,0:T(8,128)(2,1)S(1)} %bitcast.28), channel_id=1, source_target_pairs={{0,2},{2,0},{4,6},{6,4},{1,3},{3,1},{5,7},{7,5},{8,10},{10,8},{12,... | collective-permute-start | bytes 786440 | tf_op jit(solution)/shard_map/ppermute | solution.py:142
  45.9 0.0 copy-done.3
  45.9 1.9 %collective-permute-start = (bf16[128,128]{1,0:T(8,128)(2,1)S(1)}, bf16[128,128]{1,0:T(8,128)(2,1)S(1)}, u32[]{:S(2)}, u32[]{:S(2)}) collective-permute-start(bf16[128,128]{1,0:T(8,128)(2,1)S(1)} %copy-done.3), channel_id=1, source_target_pairs={{0,1},{1,0},{2,3},{3,2},{4,5},{5,4},{6,7},{7,6},{8,9},{9,8},{10,11... | collective-permute-start | bytes 98312 | tf_op jit(solution)/shard_map/ppermute | solution.py:142
  47.8 1.2 collective-permute-done.other_ref
  49.0 0.0 collective-permute-done.3.kv3
  49.0 2.4 %collective-permute-done.2.kv2 = bf16[4,2,128,128]{3,2,1,0:T(8,128)(2,1)S(1)} collective-permute-done((bf16[4,2,128,128]{3,2,1,0:T(8,128)(2,1)S(1)}, bf16[4,2,128,128]{3,2,1,0:T(8,128)(2,1)S(1)}, u32[]{:S(2)}, u32[]{:S(2)}) %collective-permute-start.2) | collective-permute-done | bytes 262176 | tf_op jit(solution)/shard_map/ppermute | solution.py:142
  51.3 0.9 collective-permute-done.1.kv1
  52.3 1.2 forward.1.mine_ref
  53.5 1.9 %collective-permute-start.4 = (f32[256,256]{1,0:T(8,128)S(1)}, f32[256,256]{1,0:T(8,128)S(1)}, u32[]{:S(2)}, u32[]{:S(2)}) collective-permute-start(f32[256,256]{1,0:T(8,128)S(1)} %forward.1.mine_ref), channel_id=1, source_target_pairs={{0,1},{1,0},{2,3},{3,2},{4,5},{5,4},{6,7},{7,6},{8,9},{9,8},{10,11... | collective-permute-start | bytes 786440 | tf_op jit(solution)/shard_map/ppermute | solution.py:142
  55.4 1.5 %collective-permute-done.4.theirs_ref = f32[256,256]{1,0:T(8,128)S(1)} collective-permute-done((f32[256,256]{1,0:T(8,128)S(1)}, f32[256,256]{1,0:T(8,128)S(1)}, u32[]{:S(2)}, u32[]{:S(2)}) %collective-permute-start.4) | collective-permute-done | bytes 262176 | tf_op jit(solution)/shard_map/ppermute | solution.py:142
  56.9 0.0 copy-start.1
  56.9 0.7 copy-done.1
  57.6 0.0 all-to-all-done.cot_ref
  57.6 0.0 copy-done
  57.6 0.0 copy-start.2
  57.6 1.0 cotangent.1.gift_ref
  58.6 2.0 %collective-permute-start.5 = (bf16[17,128,128]{2,1,0:T(8,128)(2,1)S(1)}, bf16[17,128,128]{2,1,0:T(8,128)(2,1)S(1)}, u32[]{:S(2)}, u32[]{:S(2)}) collective-permute-start(bf16[17,128,128]{2,1,0:T(8,128)(2,1)S(1)} %cotangent.1.gift_ref), channel_id=1, source_target_pairs={{0,1},{1,0},{2,3},{3,2},{4,5},{5,4},{6,7},{7,6},{8,9},{9,8},{10,11... | collective-permute-start | bytes 1671176 | tf_op jit(solution)/shard_map/ppermute | solution.py:142
  60.6 1.8 %collective-permute-done.5.got_ref = bf16[17,128,128]{2,1,0:T(8,128)(2,1)S(1)} collective-permute-done((bf16[17,128,128]{2,1,0:T(8,128)(2,1)S(1)}, bf16[17,128,128]{2,1,0:T(8,128)(2,1)S(1)}, u32[]{:S(2)}, u32[]{:S(2)}) %collective-permute-start.5) | collective-permute-done | bytes 557088 | tf_op jit(solution)/shard_map/ppermute | solution.py:142
  62.5 0.0 copy-done.2
  62.5 3.6 %backward.1 = (f32[2,128,128]{2,1,0:T(8,128)S(1)}, bf16[4,4,3,128,128]{4,3,2,1,0:T(8,128)(2,1)}, bf16[4,128,256]{2,1,0:T(8,128)(2,1)}, bf16[4,128,256]{2,1,0:T(8...) custom-call(s32[4]{0:T(128)S(1)} %pad_add_fusion.place_ref, bf16[128,128]{1,0:T(8,128)(2,1)S(1)} %copy-done.3, ...), custom_call_target="tpu_custom_call" | custom-call | flops 939524096 | bytes 8388608 | tf_op jit(solution)/shard_map/backward/pallas_call | solution.py:211
  66.1 0.0 copy-start.4
  66.1 0.6 copy-done.4
  66.7 0.0 copy-start.9
  66.7 0.0 copy-start.5
  66.7 0.0 copy-start.8
  66.7 4.1 %all-to-all-start.1 = ((bf16[4,4,3,128,128]{4,3,2,1,0:T(8,128)(2,1)}), bf16[4,4,3,128,128]{4,3,2,1,0:T(8,128)(2,1)S(1)}, u32[]{:S(2)}, u32[]{:S(2)}) async-start(bf16[4,4,3,128,128]{4,3,2,1,0:T(8,128)(2,1)} %get-tuple-element.47), calls=%async_computation.1 | async-start | bytes 3145728 | tf_op jit(solution)/shard_map/all_to_all | solution.py:138
  70.9 0.0 copy-done.9
  70.9 5.7 %collective-permute-start.7 = (bf16[4,128,256]{2,1,0:T(8,128)(2,1)S(1)}, bf16[4,128,256]{2,1,0:T(8,128)(2,1)S(1)}, u32[]{:S(2)}, u32[]{:S(2)}) collective-permute-start(bf16[4,128,256]{2,1,0:T(8,128)(2,1)S(1)} %copy-done.9), channel_id=1, source_target_pairs={{0,32},{32,0},{64,96},{96,64},{1,33},{33,1},{65,97},{97,65},{2,34}... | collective-permute-start | bytes 786440 | tf_op jit(solution)/shard_map/ppermute | solution.py:142
  76.6 0.0 copy-done.5
  76.6 1.9 %collective-permute-start.12 = (f32[128,128]{1,0:T(8,128)S(1)}, f32[128,128]{1,0:T(8,128)S(1)}, u32[]{:S(2)}, u32[]{:S(2)}) collective-permute-start(f32[128,128]{1,0:T(8,128)S(1)} %slice_bitcast_fusion.4), channel_id=1, source_target_pairs={{0,1},{1,0},{2,3},{3,2},{4,5},{5,4},{6,7},{7,6},{8,9},{9,8},{10,11... | collective-permute-start | bytes 196616 | tf_op jit(solution)/shard_map/ppermute | solution.py:142
  78.6 0.0 copy-done.8
  78.6 1.9 %collective-permute-start.6 = (bf16[4,128,256]{2,1,0:T(8,128)(2,1)S(1)}, bf16[4,128,256]{2,1,0:T(8,128)(2,1)S(1)}, u32[]{:S(2)}, u32[]{:S(2)}) collective-permute-start(bf16[4,128,256]{2,1,0:T(8,128)(2,1)S(1)} %copy-done.8), channel_id=1, source_target_pairs={{0,32},{32,0},{64,96},{96,64},{1,33},{33,1},{65,97},{97,65},{2,34}... | collective-permute-start | bytes 786440 | tf_op jit(solution)/shard_map/ppermute | solution.py:142
  80.5 2.4 %collective-permute-done.7 = bf16[4,128,256]{2,1,0:T(8,128)(2,1)S(1)} collective-permute-done((bf16[4,128,256]{2,1,0:T(8,128)(2,1)S(1)}, bf16[4,128,256]{2,1,0:T(8,128)(2,1)S(1)}, u32[]{:S(2)}, u32[]{:S(2)}) %collective-permute-start.7) | collective-permute-done | bytes 262176 | tf_op jit(solution)/shard_map/ppermute | solution.py:142
  82.9 0.0 copy-done.6
  82.9 0.1 add_convert_fusion.2
  83.0 0.0 copy-start.7
  83.0 2.4 %collective-permute-start.8 = (bf16[4,128,256]{2,1,0:T(8,128)(2,1)S(1)}, bf16[4,128,256]{2,1,0:T(8,128)(2,1)S(1)}, u32[]{:S(2)}, u32[]{:S(2)}) collective-permute-start(bf16[4,128,256]{2,1,0:T(8,128)(2,1)S(1)} %add_convert_fusion.2), channel_id=1, source_target_pairs={{0,64},{32,96},{64,0},{96,32},{1,65},{33,97},{65,1},{97,33},{2,66}... | collective-permute-start | bytes 786440 | tf_op jit(solution)/shard_map/ppermute | solution.py:142
  85.5 0.0 collective-permute-done.12
  85.5 6.4 %all-to-all-done.1 = bf16[4,4,3,128,128]{4,3,2,1,0:T(8,128)(2,1)S(1)} async-done(((bf16[4,4,3,128,128]{4,3,2,1,0:T(8,128)(2,1)}), bf16[4,4,3,128,128]{4,3,2,1,0:T(8,128)(2,1)S(1)}, u32[]{:S(2)}, u32[]{:S(2)}) %all-to-all-start.1) | async-done | bytes 1572896 | tf_op jit(solution)/shard_map/all_to_all | solution.py:138
  91.9 1.0 fusion
  92.9 6.7 %all-to-all-start.2 = ((bf16[4,3,128,128]{3,2,1,0:T(8,128)(2,1)}), bf16[4,3,128,128]{3,2,1,0:T(8,128)(2,1)S(1)}, u32[]{:S(2)}, u32[]{:S(2)}) async-start(bf16[4,3,128,128]{3,2,1,0:T(8,128)(2,1)} %fusion), calls=%async_computation.2 | async-start | bytes 786432 | tf_op jit(solution)/shard_map/all_to_all | solution.py:138
  99.6 0.0 collective-permute-done.6
  99.6 0.0 collective-permute-done.8
  99.6 0.0 copy-done.7
  99.6 0.1 add_convert_fusion.1
  99.8 3.4 %collective-permute-start.9 = (bf16[128,256]{1,0:T(8,128)(2,1)S(1)}, bf16[128,256]{1,0:T(8,128)(2,1)S(1)}, u32[]{:S(2)}, u32[]{:S(2)}) collective-permute-start(bf16[128,256]{1,0:T(8,128)(2,1)S(1)} %get-tuple-element.53), channel_id=1, source_target_pairs={{0,128},{128,0},{256,384},{384,256},{1,129},{129,1},{257,385},{385... | collective-permute-start | bytes 196616 | tf_op jit(solution)/shard_map/ppermute | solution.py:142
  103.2 4.0 %collective-permute-start.11 = (bf16[128,256]{1,0:T(8,128)(2,1)S(1)}, bf16[128,256]{1,0:T(8,128)(2,1)S(1)}, u32[]{:S(2)}, u32[]{:S(2)}) collective-permute-start(bf16[128,256]{1,0:T(8,128)(2,1)S(1)} %get-tuple-element.54), channel_id=1, source_target_pairs={{0,384},{128,256},{256,128},{384,0},{1,385},{129,257},{257,129},{3... | collective-permute-start | bytes 196616 | tf_op jit(solution)/shard_map/ppermute | solution.py:142
  107.1 2.5 %collective-permute-start.10 = (bf16[128,256]{1,0:T(8,128)(2,1)S(1)}, bf16[128,256]{1,0:T(8,128)(2,1)S(1)}, u32[]{:S(2)}, u32[]{:S(2)}) collective-permute-start(bf16[128,256]{1,0:T(8,128)(2,1)S(1)} %get-tuple-element.55), channel_id=1, source_target_pairs={{0,256},{128,384},{256,0},{384,128},{1,257},{129,385},{257,1},{385... | collective-permute-start | bytes 196616 | tf_op jit(solution)/shard_map/ppermute | solution.py:142
  109.7 0.0 collective-permute-done.9
  109.7 0.8 collective-permute-done.11
  110.5 4.3 %collective-permute-done.10 = bf16[128,256]{1,0:T(8,128)(2,1)S(1)} collective-permute-done((bf16[128,256]{1,0:T(8,128)(2,1)S(1)}, bf16[128,256]{1,0:T(8,128)(2,1)S(1)}, u32[]{:S(2)}, u32[]{:S(2)}) %collective-permute-start.10) | collective-permute-done | bytes 65568 | tf_op jit(solution)/shard_map/ppermute | solution.py:142
  114.8 0.7 fusion.3
  115.5 0.6 fusion.5
  116.1 9.5 %all-to-all-done.2.parts_ref = bf16[4,3,128,128]{3,2,1,0:T(8,128)(2,1)S(1)} async-done(((bf16[4,3,128,128]{3,2,1,0:T(8,128)(2,1)}), bf16[4,3,128,128]{3,2,1,0:T(8,128)(2,1)S(1)}, u32[]{:S(2)}, u32[]{:S(2)}) %all-to-all-start.2) | async-done | bytes 393248 | tf_op jit(solution)/shard_map/all_to_all | solution.py:138
  125.5 0.8 finish.1
  (3 shorter events, 0.0 us)
Async XLA Ops:
  27.6 18.3 %copy-start.3 = (bf16[128,128]{1,0:T(8,128)(2,1)S(1)}, bf16[128,128]{1,0:T(8,128)(2,1)}, u32[]{:S(2)}) copy-start(bf16[128,128]{1,0:T(8,128)(2,1)} %q_ref.3) | copy-start | bytes 98308
  28.7 28.9 %copy-start = (bf16[128,4096]{1,0:T(8,128)(2,1)S(1)}, bf16[128,4096]{1,0:T(8,128)(2,1)}, u32[]{:S(2)}) copy-start(bf16[128,4096]{1,0:T(8,128)(2,1)} %w_ref.3) | copy-start | bytes 3145732
  28.7 28.9 %all-to-all-start = ((bf16[16,128,256]{2,1,0:T(8,128)(2,1)}), bf16[16,128,256]{2,1,0:T(8,128)(2,1)S(1)}, u32[]{:S(2)}, u32[]{:S(2)}) async-start(bf16[16,128,256]{2,1,0:T(8,128)(2,1)} %broadcast_in_dim.2), calls=%async_computation | async-start | bytes 2097152 | tf_op jit(solution)/shard_map/all_to_all | solution.py:138
  36.0 12.9 %collective-permute-start.3 = (bf16[4,2,128,128]{3,2,1,0:T(8,128)(2,1)S(1)}, bf16[4,2,128,128]{3,2,1,0:T(8,128)(2,1)S(1)}, u32[]{:S(2)}, u32[]{:S(2)}) collective-permute-start(bf16[4,2,128,128]{3,2,1,0:T(8,128)(2,1)S(1)} %bitcast.26), channel_id=1, source_target_pairs={{0,6},{2,4},{4,2},{6,0},{1,7},{3,5},{5,3},{7,1},{8,14},{10,12},{12... | collective-permute-start | bytes 786440 | tf_op jit(solution)/shard_map/ppermute | solution.py:142
  40.7 10.7 %collective-permute-start.2 = (bf16[4,2,128,128]{3,2,1,0:T(8,128)(2,1)S(1)}, bf16[4,2,128,128]{3,2,1,0:T(8,128)(2,1)S(1)}, u32[]{:S(2)}, u32[]{:S(2)}) collective-permute-start(bf16[4,2,128,128]{3,2,1,0:T(8,128)(2,1)S(1)} %bitcast.27), channel_id=1, source_target_pairs={{0,4},{2,6},{4,0},{6,2},{1,5},{3,7},{5,1},{7,3},{8,12},{10,14},{12... | collective-permute-start | bytes 786440 | tf_op jit(solution)/shard_map/ppermute | solution.py:142
  43.4 8.9 %collective-permute-start.1 = (bf16[4,2,128,128]{3,2,1,0:T(8,128)(2,1)S(1)}, bf16[4,2,128,128]{3,2,1,0:T(8,128)(2,1)S(1)}, u32[]{:S(2)}, u32[]{:S(2)}) collective-permute-start(bf16[4,2,128,128]{3,2,1,0:T(8,128)(2,1)S(1)} %bitcast.28), channel_id=1, source_target_pairs={{0,2},{2,0},{4,6},{6,4},{1,3},{3,1},{5,7},{7,5},{8,10},{10,8},{12,... | collective-permute-start | bytes 786440 | tf_op jit(solution)/shard_map/ppermute | solution.py:142
  45.9 3.1 %collective-permute-start = (bf16[128,128]{1,0:T(8,128)(2,1)S(1)}, bf16[128,128]{1,0:T(8,128)(2,1)S(1)}, u32[]{:S(2)}, u32[]{:S(2)}) collective-permute-start(bf16[128,128]{1,0:T(8,128)(2,1)S(1)} %copy-done.3), channel_id=1, source_target_pairs={{0,1},{1,0},{2,3},{3,2},{4,5},{5,4},{6,7},{7,6},{8,9},{9,8},{10,11... | collective-permute-start | bytes 98312 | tf_op jit(solution)/shard_map/ppermute | solution.py:142
  53.5 3.4 %collective-permute-start.4 = (f32[256,256]{1,0:T(8,128)S(1)}, f32[256,256]{1,0:T(8,128)S(1)}, u32[]{:S(2)}, u32[]{:S(2)}) collective-permute-start(f32[256,256]{1,0:T(8,128)S(1)} %forward.1.mine_ref), channel_id=1, source_target_pairs={{0,1},{1,0},{2,3},{3,2},{4,5},{5,4},{6,7},{7,6},{8,9},{9,8},{10,11... | collective-permute-start | bytes 786440 | tf_op jit(solution)/shard_map/ppermute | solution.py:142
  56.9 0.7 copy-start.1
  57.6 4.9 %copy-start.2 = (f32[256,256]{1,0:T(8,128)S(1)}, f32[256,256]{1,0:T(8,128)}, u32[]{:S(2)}) copy-start(f32[256,256]{1,0:T(8,128)} %copy-done.1) | copy-start | bytes 786436
  58.6 3.9 %collective-permute-start.5 = (bf16[17,128,128]{2,1,0:T(8,128)(2,1)S(1)}, bf16[17,128,128]{2,1,0:T(8,128)(2,1)S(1)}, u32[]{:S(2)}, u32[]{:S(2)}) collective-permute-start(bf16[17,128,128]{2,1,0:T(8,128)(2,1)S(1)} %cotangent.1.gift_ref), channel_id=1, source_target_pairs={{0,1},{1,0},{2,3},{3,2},{4,5},{5,4},{6,7},{7,6},{8,9},{9,8},{10,11... | collective-permute-start | bytes 1671176 | tf_op jit(solution)/shard_map/ppermute | solution.py:142
  66.1 0.6 copy-start.4
  66.7 4.2 %copy-start.9 = (bf16[4,128,256]{2,1,0:T(8,128)(2,1)S(1)}, bf16[4,128,256]{2,1,0:T(8,128)(2,1)}, u32[]{:S(2)}) copy-start(bf16[4,128,256]{2,1,0:T(8,128)(2,1)} %get-tuple-element.45) | copy-start | bytes 786436
  66.7 9.9 %copy-start.5 = (f32[2,128,128]{2,1,0:T(8,128)S(1)}, f32[2,128,128]{2,1,0:T(8,128)}, u32[]{:S(2)}) copy-start(f32[2,128,128]{2,1,0:T(8,128)} %copy-done.4) | copy-start | bytes 393220
  66.7 11.8 %copy-start.8 = (bf16[4,128,256]{2,1,0:T(8,128)(2,1)S(1)}, bf16[4,128,256]{2,1,0:T(8,128)(2,1)}, u32[]{:S(2)}) copy-start(bf16[4,128,256]{2,1,0:T(8,128)(2,1)} %get-tuple-element.43) | copy-start | bytes 786436
  66.7 16.2 %copy-start.6 = (bf16[4,128,256]{2,1,0:T(8,128)(2,1)S(1)}, bf16[4,128,256]{2,1,0:T(8,128)(2,1)}, u32[]{:S(2)}) copy-start(bf16[4,128,256]{2,1,0:T(8,128)(2,1)} %get-tuple-element.44) | copy-start | bytes 786436
  66.7 25.2 %all-to-all-start.1 = ((bf16[4,4,3,128,128]{4,3,2,1,0:T(8,128)(2,1)}), bf16[4,4,3,128,128]{4,3,2,1,0:T(8,128)(2,1)S(1)}, u32[]{:S(2)}, u32[]{:S(2)}) async-start(bf16[4,4,3,128,128]{4,3,2,1,0:T(8,128)(2,1)} %get-tuple-element.47), calls=%async_computation.1 | async-start | bytes 3145728 | tf_op jit(solution)/shard_map/all_to_all | solution.py:138
  70.9 12.0 %collective-permute-start.7 = (bf16[4,128,256]{2,1,0:T(8,128)(2,1)S(1)}, bf16[4,128,256]{2,1,0:T(8,128)(2,1)S(1)}, u32[]{:S(2)}, u32[]{:S(2)}) collective-permute-start(bf16[4,128,256]{2,1,0:T(8,128)(2,1)S(1)} %copy-done.9), channel_id=1, source_target_pairs={{0,32},{32,0},{64,96},{96,64},{1,33},{33,1},{65,97},{97,65},{2,34}... | collective-permute-start | bytes 786440 | tf_op jit(solution)/shard_map/ppermute | solution.py:142
  76.6 8.8 %collective-permute-start.12 = (f32[128,128]{1,0:T(8,128)S(1)}, f32[128,128]{1,0:T(8,128)S(1)}, u32[]{:S(2)}, u32[]{:S(2)}) collective-permute-start(f32[128,128]{1,0:T(8,128)S(1)} %slice_bitcast_fusion.4), channel_id=1, source_target_pairs={{0,1},{1,0},{2,3},{3,2},{4,5},{5,4},{6,7},{7,6},{8,9},{9,8},{10,11... | collective-permute-start | bytes 196616 | tf_op jit(solution)/shard_map/ppermute | solution.py:142
  78.6 21.0 %collective-permute-start.6 = (bf16[4,128,256]{2,1,0:T(8,128)(2,1)S(1)}, bf16[4,128,256]{2,1,0:T(8,128)(2,1)S(1)}, u32[]{:S(2)}, u32[]{:S(2)}) collective-permute-start(bf16[4,128,256]{2,1,0:T(8,128)(2,1)S(1)} %copy-done.8), channel_id=1, source_target_pairs={{0,32},{32,0},{64,96},{96,64},{1,33},{33,1},{65,97},{97,65},{2,34}... | collective-permute-start | bytes 786440 | tf_op jit(solution)/shard_map/ppermute | solution.py:142
  83.0 16.6 %copy-start.7 = (bf16[4,128,256]{2,1,0:T(8,128)(2,1)S(1)}, bf16[4,128,256]{2,1,0:T(8,128)(2,1)}, u32[]{:S(2)}) copy-start(bf16[4,128,256]{2,1,0:T(8,128)(2,1)} %get-tuple-element.42) | copy-start | bytes 786436
  83.0 16.6 %collective-permute-start.8 = (bf16[4,128,256]{2,1,0:T(8,128)(2,1)S(1)}, bf16[4,128,256]{2,1,0:T(8,128)(2,1)S(1)}, u32[]{:S(2)}, u32[]{:S(2)}) collective-permute-start(bf16[4,128,256]{2,1,0:T(8,128)(2,1)S(1)} %add_convert_fusion.2), channel_id=1, source_target_pairs={{0,64},{32,96},{64,0},{96,32},{1,65},{33,97},{65,1},{97,33},{2,66}... | collective-permute-start | bytes 786440 | tf_op jit(solution)/shard_map/ppermute | solution.py:142
  92.9 32.7 %all-to-all-start.2 = ((bf16[4,3,128,128]{3,2,1,0:T(8,128)(2,1)}), bf16[4,3,128,128]{3,2,1,0:T(8,128)(2,1)S(1)}, u32[]{:S(2)}, u32[]{:S(2)}) async-start(bf16[4,3,128,128]{3,2,1,0:T(8,128)(2,1)} %fusion), calls=%async_computation.2 | async-start | bytes 786432 | tf_op jit(solution)/shard_map/all_to_all | solution.py:138
  99.8 9.9 %collective-permute-start.9 = (bf16[128,256]{1,0:T(8,128)(2,1)S(1)}, bf16[128,256]{1,0:T(8,128)(2,1)S(1)}, u32[]{:S(2)}, u32[]{:S(2)}) collective-permute-start(bf16[128,256]{1,0:T(8,128)(2,1)S(1)} %get-tuple-element.53), channel_id=1, source_target_pairs={{0,128},{128,0},{256,384},{384,256},{1,129},{129,1},{257,385},{385... | collective-permute-start | bytes 196616 | tf_op jit(solution)/shard_map/ppermute | solution.py:142
  103.2 7.4 %collective-permute-start.11 = (bf16[128,256]{1,0:T(8,128)(2,1)S(1)}, bf16[128,256]{1,0:T(8,128)(2,1)S(1)}, u32[]{:S(2)}, u32[]{:S(2)}) collective-permute-start(bf16[128,256]{1,0:T(8,128)(2,1)S(1)} %get-tuple-element.54), channel_id=1, source_target_pairs={{0,384},{128,256},{256,128},{384,0},{1,385},{129,257},{257,129},{3... | collective-permute-start | bytes 196616 | tf_op jit(solution)/shard_map/ppermute | solution.py:142
  107.1 7.7 %collective-permute-start.10 = (bf16[128,256]{1,0:T(8,128)(2,1)S(1)}, bf16[128,256]{1,0:T(8,128)(2,1)S(1)}, u32[]{:S(2)}, u32[]{:S(2)}) collective-permute-start(bf16[128,256]{1,0:T(8,128)(2,1)S(1)} %get-tuple-element.55), channel_id=1, source_target_pairs={{0,256},{128,384},{256,0},{384,128},{1,257},{129,385},{257,1},{385... | collective-permute-start | bytes 196616 | tf_op jit(solution)/shard_map/ppermute | solution.py:142
